TPU v7x, 512 devices: a whole 4x8x8 slice. The times are simulated.
512 devices in a mesh: prow: 16 (over z, core), pcol: 32 (over x, y).
Axes of the slice: x: 4, y: 8, z: 8, core: 2. Of those that a mesh axis runs over, the one named last changes fastest.
Arguments:
- window: float32 [8192, 32768], P('prow', 'pcol'), may hold values from -6 to 6
- panel: float32 [8192, 256], P(('prow', 'pcol')), may hold values from -0.375 to 0.375
- linv: float32 [256, 256], replicated, as said below
- pivots: int32 [256], replicated, may hold values from 0 to 8191, as said below
Outputs:
- updated: float32 [8192, 32768], P('prow', 'pcol')
Inputs may be any that keep to these rules, and one draw needn't show every extreme that they name: `pivots`: each entry k is either k itself or a row at or past 256; entries of the second kind are all distinct. `linv`: zero above the diagonal, ones on it.
All inputs are finite; a program needn't handle non-finite values.
Results may differ from a plain program's by a relative error of at most 0.000055.
Values sent between devices are 32-bit elements; how exact they have to be, the bound alone decides.
No kernel may reach another device: no remote copies, remote signals or barrier semaphores. Data moves between devices by JAX's collectives and lax.ppermute only.
A program may use at most 64 MiB of HBM per device.

v0:
```python
import jax
import jax.numpy as jnp
from jax import lax
from jax.sharding import PartitionSpec as P


def spread(value, axis, source):
    kept = jnp.where(lax.axis_index(axis) == source, value, 0).astype(value.dtype)
    return lax.psum(kept, axis)


def on_device(window, panel, linv, pivots):
    nrows = window.shape[0]
    ncols = window.shape[1]
    nbw = pivots.shape[0]
    first = lax.axis_index("prow") * nrows
    ident = jnp.arange(nbw, dtype=jnp.int32)
    local = pivots - first
    inside = (local >= 0) & (local < nrows)
    picked = jnp.take(window, jnp.clip(local, 0, nrows - 1), axis=0)
    picked = jnp.where(inside[:, None], picked, 0.0)
    top = lax.psum(picked, "prow")
    former = spread(window[:nbw], "prow", 0)
    moved = inside & (pivots != ident)
    target = jnp.where(moved, local, nrows)
    slot = jnp.zeros((nrows,), jnp.int32).at[target].set(ident + 1, mode="drop")
    incoming = jnp.take(former, jnp.clip(slot - 1, 0, nbw - 1), axis=0)
    swapped = jnp.where((slot > 0)[:, None], incoming, window)
    solved = jnp.dot(linv, top, precision=lax.Precision.HIGHEST, preferred_element_type=jnp.float32)
    result = swapped - jnp.dot(
        lax.all_gather(panel, "pcol", axis=0, tiled=True),
        solved,
        precision=lax.Precision.HIGHEST,
        preferred_element_type=jnp.float32,
    )
    global_row = first + jnp.arange(nrows, dtype=jnp.int32)
    filler = jnp.concatenate([solved, jnp.zeros((nrows - nbw, ncols), jnp.float32)], axis=0)
    return jnp.where((global_row < nbw)[:, None], filler, result)


def solution(mesh):
    return jax.shard_map(
        on_device,
        mesh=mesh,
        in_specs=(P("prow", "pcol"), P(("prow", "pcol"), None), P(), P()),
        out_specs=P("prow", "pcol"),
        check_vma=False,
    )
```

profile of v0, /device:TPU:1, one launch (start us, length us, event | category | flops | bytes accessed | tf_op | source)
XLA Modules:
  0.0 162.7 jit_solution(13974479313580061462)
XLA Ops:
  6.5 0.0 copy-start
  6.5 0.0 all-reduce.4.cloned.1.call-start
  6.5 0.7 compare_and_fusion.1
  7.3 0.0 copy-start.1
  7.3 3.3 %gather_fusion = f32[256,1024]{1,0:T(8,128)S(1)} fusion(f32[512,1024]{1,0:T(8,128)} %param.4, s32[1024]{0:T(1024)S(1)} %pad_clamp_fusion.1), kind=kCustom, calls=%fused_computation | custom fusion | bytes 2098176 | tf_op jit(solution)/shard_map/jit(_take)/gather | solution.py:20
  10.6 0.0 copy-done.1
  10.6 1.5 slice_select_fusion
  12.1 0.0 all-reduce.4.cloned.1.call-update
  12.2 0.0 copy-start.4
  12.2 0.0 copy-start.3
  12.2 1.8 %copy.6 = f32[512,1024]{0,1:T(8,128)} copy(f32[512,1024]{1,0:T(8,128)S(1)} %copy-done.1) | data formatting | bytes 4194304 | tf_op args[0]
  14.0 0.0 copy-done.4
  14.0 1.4 scatter_custom_fusion
  15.4 0.0 copy-done.3
  15.4 40.6 %all_gather.3 = f32[512,256]{1,0:T(8,128)S(1)} all-gather(f32[16,256]{1,0:T(8,128)S(1)} %copy-done.3), channel_id=1, replica_groups=mesh['prow'=16,'pcol'=32] {'pcol'}, dimensions={0}, use_global_device_ids=true | all-gather | bytes 540672 | tf_op jit(solution)/shard_map/all_gather | solution.py:31
  56.1 83.4 %all-reduce.4.cloned.1.call-done = (f32[256,1024]{1,0:T(8,128)}, f32[256,1024]{1,0:T(8,128)}) async-done(((f32[256,1024]{1,0:T(8,128)}, f32[256,1024]{1,0:T(8,128)}), (f32[256,1024]{1,0:T(8,128)}, f32[256,1024]{1,0:T(8,128)})) %all-reduce.4.cloned.1.call-update) | async-done | bytes 2097168 | tf_op jit(solution)/shard_map/psum | solution.py:9
  139.5 4.9 %gather_fusion.1 = f32[512,1024]{1,0:T(8,128)} fusion(f32[256,1024]{1,0:T(8,128)} %get-tuple-element.5, s32[1024]{0:T(1024)S(1)} %pad_clamp_fusion), kind=kCustom, calls=%fused_computation.1 | custom fusion | bytes 4196352 | tf_op jit(solution)/shard_map/jit(_take)/gather | solution.py:27
  144.3 1.9 %copy.5 = f32[512,1024]{0,1:T(8,128)S(1)} copy(f32[512,1024]{1,0:T(8,128)} %gather_fusion.1) | data formatting | bytes 4194304 | tf_op jit(solution)/shard_map/jit(_take)/gather | solution.py:27
  146.3 0.0 copy-start.2
  146.3 0.0 copy-done
  146.3 3.2 %fusion.3 = f32[1024,256]{1,0:T(8,128)S(1)} fusion(f32[256,1024]{1,0:T(8,128)} %get-tuple-element.6, f32[256,256]{1,0:T(8,128)S(1)} %copy-done), kind=kOutput, calls=%fused_computation.22 | convolution fusion | flops 805306368 | bytes 2359296 | tf_op jit(solution)/shard_map/dot_general | solution.py:29
  149.5 0.0 copy-done.2
  149.5 3.5 %fusion = f32[512,1024]{0,1:T(8,128)} fusion(f32[512,1024]{0,1:T(8,128)S(1)} %copy-done.2, f32[512,1024]{0,1:T(8,128)S(1)} %copy.5, f32[256,1024]{0,1:T(8,128)S(1)} %bitcast.10, f32[1024,256]{1,0:T(8,128)S(1)} %fusion.3, f32[512,256]{1,0:T(8,128)S(1)} %all_gather.3, pred[512]{0:T(512)(128)(4,1)S(1)} %get-tuple-element.10, ...), kind=kOutput, calls=%fused_computation.4 | convolution fusion | flops 1612709888 | bytes 8914432 | tf_op jit(solution)/shard_map/dot_general | solution.py:30
  153.0 2.9 %copy.7 = f32[512,1024]{1,0:T(8,128)} copy(f32[512,1024]{0,1:T(8,128)} %fusion) | data formatting | bytes 4194304 | tf_op jit(solution)/shard_map/jit(_where)/select_n | solution.py:38
  (6 shorter events, 0.0 us)
Async XLA Ops:
  6.5 139.7 %copy-start = (f32[256,256]{1,0:T(8,128)S(1)}, f32[256,256]{1,0:T(8,128)}, u32[]{:S(2)}) copy-start(f32[256,256]{1,0:T(8,128)} %param.6) | copy-start | bytes 786436
  6.5 132.9 %all-reduce.4.cloned.1.call-start = ((), (), s32[]{:S(2)}) async-start(), calls=%async_computation | async-start | bytes 4194304 | tf_op jit(solution)/shard_map/psum | solution.py:9
  7.3 3.3 %copy-start.1 = (f32[512,1024]{1,0:T(8,128)S(1)}, f32[512,1024]{1,0:T(8,128)}, u32[]{:S(2)}) copy-start(f32[512,1024]{1,0:T(8,128)} %param.4) | copy-start | bytes 6291460
  12.2 1.8 %copy-start.4 = (s32[256]{0:T(256)S(1)}, s32[256]{0:T(256)}, u32[]{:S(2)}) copy-start(s32[256]{0:T(256)} %param.7) | copy-start | bytes 3076
  12.2 3.3 %copy-start.3 = (f32[16,256]{1,0:T(8,128)S(1)}, f32[16,256]{1,0:T(8,128)}, u32[]{:S(2)}) copy-start(f32[16,256]{1,0:T(8,128)} %param.5) | copy-start | bytes 49156
  146.3 3.2 %copy-start.2 = (f32[512,1024]{0,1:T(8,128)S(1)}, f32[512,1024]{0,1:T(8,128)}, u32[]{:S(2)}) copy-start(f32[512,1024]{0,1:T(8,128)} %copy.6) | copy-start | bytes 6291460
Sparse Core Ops, SparseCore 0:
  12.3 127.1 all-reduce.3
where the time goes:
time: 163 us
  waiting for transfers between devices  83.4 us (51%)
  blocking collectives  40.6 us (25%)
  local copies, waits for them, and re-layouts  16.2 us (10%)
  between operations  13.5 us (8%)
  matrix products  6.71 us (4%)
  other arithmetic  2.28 us (1%)
    psum x1, waiting for transfers between devices, spread(): return lax.psum(kept, axis)  83.4 us
    all_gather x1, blocking collectives, on_device(): lax.all_gather(panel, 'pcol', axis=0, tiled=True)  40.6 us
    gather x2, local copies, waits for them, and re-layouts, on_device(): incoming = jnp.take(former, jnp.clip(slot - 1, 0, nbw - 1), axis=0)  6.8 us
    dot_general x1, matrix products, on_device(): jnp.dot(lax.all_gather(panel, 'pcol', axis=0, tiled=True), solved, precis...  3.53 us
    gather x1, local copies, waits for them, and re-layouts, on_device(): picked = jnp.take(window, jnp.clip(local, 0, nrows - 1), axis=0)  3.31 us
  transfers between devices with their start and end apart: 1, of which 1 were waited for; matrix products, arithmetic and copies ran while one was open for 2% of the time, Pallas kernels for 0%

commit v1 on v0

v1 whole, which is shorter than its diff:
```python
import functools

import jax
import jax.numpy as jnp
from jax import lax
from jax.experimental import pallas as pl
from jax.experimental.pallas import tpu as pltpu
from jax.sharding import PartitionSpec as P

CORES = 2
LANES = 128
STEP = 256
PARAMS = pltpu.CompilerParams(vmem_limit_bytes=32 * 1024 * 1024)


def vmem(count):
    return [pl.BlockSpec(memory_space=pltpu.VMEM)] * count


def smem(count):
    return [pl.BlockSpec(memory_space=pltpu.SMEM)] * count


def cost(flops, nbytes):
    return pl.CostEstimate(flops=flops, bytes_accessed=nbytes, transcendentals=0)


def tiles(ncols):
    return [slice(c, c + LANES) for c in range(0, ncols, LANES)]


def sides(me, half):
    core = lax.rem(me, CORES)
    return core, me + 1 - 2 * core, core * half, half - core * half


def scan_kernel(nrows, piv, me, lists, counts):
    half = piv.shape[0] // CORES
    _, _, base, other = sides(me[0], half)
    first = me[0] * nrows

    def step(i, totals):
        new = []
        for side, start in enumerate((base, other)):
            local = piv[start + i] - first
            inside = (local >= 0) & (local < nrows)
            lists[side, totals[side]] = start + i
            new.append(totals[side] + inside.astype(jnp.int32))
        return tuple(new)

    counts[0], counts[1] = lax.fori_loop(0, half, step, (jnp.int32(0), jnp.int32(0)), unroll=8)


def scan(nrows, pivots, me):
    half = pivots.shape[0] // CORES
    return pl.pallas_call(
        functools.partial(scan_kernel, nrows),
        out_shape=(
            jax.ShapeDtypeStruct((CORES, half), jnp.int32),
            jax.ShapeDtypeStruct((CORES,), jnp.int32),
        ),
        in_specs=smem(2),
        out_specs=tuple(smem(2)),
        compiler_params=PARAMS,
        cost_estimate=cost(0, 2**20),
        name="scan",
    )(pivots, me)


def pick_kernel(piv, me, lists, counts, win, own, give):
    nrows = win.shape[0]
    half = own.shape[0]
    _, _, base, other = sides(me[0], half)
    first = me[0] * nrows
    for side, start, out in ((1, other, give), (0, base, own)):
        out[...] = win[pl.ds(pl.multiple_of(start, half), half), :]

        def put(i, carry, side=side, start=start, out=out):
            k = lists[side, i]
            out[pl.ds(k - start, 1), :] = win[pl.ds(piv[k] - first, 1), :]
            return carry

        lax.fori_loop(0, counts[side], put, 0)


def pick(pivots, me, lists, counts, window):
    half = pivots.shape[0] // CORES
    ncols = window.shape[1]
    block = jax.ShapeDtypeStruct((half, ncols), window.dtype)
    return pl.pallas_call(
        pick_kernel,
        out_shape=(block, block),
        in_specs=smem(4) + vmem(1),
        out_specs=tuple(vmem(2)),
        compiler_params=PARAMS,
        cost_estimate=cost(0, 16 * half * ncols),
        name="pick",
    )(pivots, me, lists, counts, window)


def half_of(owner, base, half):
    return owner[pl.ds(pl.multiple_of(base, half), half), :]


def deal_kernel(me, owner, own, got, out):
    half, ncols = own.shape
    _, partner, base, _ = sides(me[0], half)
    who = half_of(owner, base, half)
    theirs = (who == partner) | ((who != me[0]) & (who != jnp.where(me[0] == 0, who, -1)))
    for cols in tiles(ncols):
        out[:, cols] = jnp.where(theirs, got[:, cols], own[:, cols])


def pair_kernel(me, owner, own, got, left, out):
    half, ncols = own.shape
    _, partner, base, _ = sides(me[0], half)
    who = half_of(owner, base, half)
    mine = (who == me[0]) | (who == jnp.where(me[0] == 0, partner, me[0]))
    for cols in tiles(ncols):
        out[:, cols] = jnp.where(mine, own[:, cols], got[:, cols])


def home_kernel(nz, me, owner, got, out):
    half, ncols = got.shape
    part = half // nz
    _, _, base, _ = sides(me[0], half)
    at = pl.multiple_of(base + me[0] // CORES * part, part)
    chip = owner[pl.ds(at, part), :] // CORES
    for cols in tiles(ncols):
        former = got[0:part, cols]
        top = former
        for z in range(1, nz):
            top = jnp.where(chip == z, got[z * part : (z + 1) * part, cols], top)
        for z in range(nz):
            out[z * part : (z + 1) * part, cols] = jnp.where(chip == z, former, top)


def choose(kernel, name, me, owner, *blocks):
    shape = blocks[0].shape
    return pl.pallas_call(
        kernel,
        out_shape=jax.ShapeDtypeStruct(shape, blocks[0].dtype),
        in_specs=smem(1) + vmem(1 + len(blocks)),
        out_specs=pl.BlockSpec(memory_space=pltpu.VMEM),
        compiler_params=PARAMS,
        cost_estimate=cost(0, 12 * shape[0] * shape[1]),
        name=name,
    )(me, owner, *blocks)


def parts(value):
    high = value.astype(jnp.bfloat16)
    return high, (value - high.astype(jnp.float32)).astype(jnp.bfloat16)


def split_kernel(linv, panel, left, right):
    for source, out in ((linv, left), (panel, right)):
        nb = source.shape[1]
        high, low = parts(source[...])
        out[:, 0:nb] = high
        out[:, nb : 2 * nb] = low
        out[:, 2 * nb : 3 * nb] = high


def split(linv, panel):
    shapes = [jax.ShapeDtypeStruct((a.shape[0], 3 * a.shape[1]), jnp.bfloat16) for a in (linv, panel)]
    return pl.pallas_call(
        split_kernel,
        out_shape=tuple(shapes),
        in_specs=vmem(2),
        out_specs=tuple(vmem(2)),
        compiler_params=PARAMS,
        cost_estimate=cost(0, 10 * (linv.size + panel.size)),
        name="split",
    )(linv, panel)


def ready_kernel(piv, me, lists, counts, owner, own, got, far, win, top, swapped):
    half, ncols = own.shape
    nrows = win.shape[0]
    _, partner, base, _ = sides(me[0], half)
    first = me[0] * nrows
    who = half_of(owner, base, half)
    for cols in tiles(ncols):
        theirs = jnp.where(who == partner, got[:, cols], far[:, cols])
        top[:, cols] = jnp.where(who == me[0], own[:, cols], theirs)
    swapped[...] = win[...]

    def put(source, side, start):
        def one(i, carry):
            k = lists[side, i]
            swapped[pl.ds(piv[k] - first, 1), :] = source[pl.ds(k - start, 1), :]
            return carry

        lax.fori_loop(0, counts[side], one, 0)

    @pl.when(me[0] == 0)
    def _():
        put(win, 0, 0)
        put(win, 1, 0)

    @pl.when(me[0] == 1)
    def _():
        put(got, 0, base)

    @pl.when(me[0] > 1)
    def _():
        put(far, 0, base)


def ready(pivots, me, lists, counts, owner, own, got, far, window):
    return pl.pallas_call(
        ready_kernel,
        out_shape=(
            jax.ShapeDtypeStruct(own.shape, own.dtype),
            jax.ShapeDtypeStruct(window.shape, window.dtype),
        ),
        in_specs=smem(4) + vmem(5),
        out_specs=tuple(vmem(2)),
        compiler_params=PARAMS,
        cost_estimate=cost(0, 8 * window.size + 16 * own.size),
        name="ready",
    )(pivots, me, lists, counts, owner, own, got, far, window)


def final_kernel(piv, me, lists, counts, owner, left, right, swapped, top, give, got, out, full, rhs):
    half = top.shape[0]
    nb = 2 * half
    nrows, step = out.shape
    first = me[0] * nrows
    _, _, base, other = sides(me[0], half)
    base = pl.multiple_of(base, half)
    other = pl.multiple_of(other, half)
    at = pl.multiple_of(pl.program_id(0) * step, step)
    who = half_of(owner, other, half)
    full[pl.ds(base, half), :] = top[:, pl.ds(at, step)]
    for c in range(0, step, LANES):
        cols = pl.ds(pl.multiple_of(at + c, LANES), LANES)
        full[pl.ds(other, half), c : c + LANES] = jnp.where(who == me[0], give[:, cols], got[:, cols])

    def product(rows, value):
        high, low = parts(value)
        rhs[0:nb, :] = high
        rhs[nb : 2 * nb, :] = high
        rhs[2 * nb : 3 * nb, :] = low
        return jnp.dot(rows[...], rhs[...], preferred_element_type=jnp.float32)

    out[...] = swapped[:, pl.ds(at, step)]

    def put(i, carry):
        k = lists[1, i]
        out[pl.ds(piv[k] - first, 1), :] = got[pl.ds(k - other, 1), pl.ds(at, step)]
        return carry

    lax.fori_loop(0, jnp.where(me[0] == 0, 0, counts[1]), put, 0)
    solved = product(left, full[...])
    out[...] = out[...] - product(right, solved)

    @pl.when(me[0] == 0)
    def _():
        out[0:nb, :] = solved


def final(pivots, me, lists, counts, owner, left, right, swapped, top, give, got):
    nrows, ncols = swapped.shape
    nb = 2 * top.shape[0]
    step = min(STEP, ncols)
    return pl.pallas_call(
        final_kernel,
        grid=(ncols // step,),
        out_shape=jax.ShapeDtypeStruct(swapped.shape, swapped.dtype),
        in_specs=smem(4) + vmem(7),
        out_specs=pl.BlockSpec((nrows, step), lambda c: (0, c)),
        scratch_shapes=[pltpu.VMEM((nb, step), jnp.float32), pltpu.VMEM((3 * nb, step), jnp.bfloat16)],
        compiler_params=PARAMS,
        cost_estimate=cost(6 * (nb + nrows) * nb * ncols, 8 * nrows * ncols),
        name="final",
    )(pivots, me, lists, counts, owner, left, right, swapped, top, give, got)


def on_device(nprow, npcol, window, panel, linv, pivots):
    nrows, ncols = window.shape
    nbw = pivots.shape[0]
    nz = nprow // CORES
    columns = [[z * CORES + core for z in range(nz)] for core in range(CORES)]

    def swap(value):
        return lax.ppermute(value, "prow", [(p, p ^ 1) for p in range(nprow)])

    def exchange(value):
        return lax.all_to_all(value, "prow", 0, 0, axis_index_groups=columns, tiled=True)

    me = lax.axis_index("prow").astype(jnp.int32)[None]
    owner = jnp.broadcast_to((pivots // nrows)[:, None], (nbw, LANES))
    lists, counts = scan(nrows, pivots, me)
    own, give = pick(pivots, me, lists, counts, window)
    got = swap(give)
    dealt = exchange(choose(deal_kernel, "deal", me, owner, own, got))
    copies = jnp.broadcast_to(panel[None], (npcol,) + panel.shape)
    whole = lax.all_to_all(copies, "pcol", 0, 0).reshape(nrows, nbw)
    far = exchange(choose(functools.partial(home_kernel, nz), "home", me, owner, dealt))
    left, right = split(linv, whole)
    last = swap(choose(pair_kernel, "pair", me, owner, own, far, left))
    top, swapped = ready(pivots, me, lists, counts, owner, own, got, far, window)
    return final(pivots, me, lists, counts, owner, left, right, swapped, top, give, last)


def solution(mesh):
    return jax.shard_map(
        functools.partial(on_device, mesh.shape["prow"], mesh.shape["pcol"]),
        mesh=mesh,
        in_specs=(P("prow", "pcol"), P(("prow", "pcol"), None), P(), P()),
        out_specs=P("prow", "pcol"),
        check_vma=False,
    )
```

time: 163 us -> 95.9 us (0.59); the launches traced: 163 us -> 94 us
  waiting for transfers between devices: 83.4 us -> 23.3 us
  starting transfers between devices: 0.01 us -> 31.1 us
  blocking collectives: 40.6 us -> 21 us
  between operations: 13.5 us -> 0.22 us
  Pallas kernels: 0 us -> 9.11 us
  local copies, waits for them, and re-layouts: 16.2 us -> 9.26 us
  matrix products: 6.71 us -> 0 us
  other arithmetic: 2.28 us -> 0.01 us
    psum x1 -> x0, waiting for transfers between devices: 83.4 us -> none  [spread(): return lax.psum(kept, axis)]
    all_gather x1 -> x0, blocking collectives: 40.6 us -> none  [on_device(): lax.all_gather(panel, 'pcol', axis=0, tiled=True)]
    all_to_all x0 -> x2, waiting for transfers between devices: none -> 21.2 us  [the longest x1 12.1 us: on_device(): whole = lax.all_to_all(copies, 'pcol', 0, 0).reshape(nrows, nbw)]
    all_to_all x0 -> x1, blocking collectives: none -> 21 us  [exchange(): lax.all_to_all(value, 'prow', 0, 0, axis_index_groups=columns, tiled=True)]
    ppermute x0 -> x2, starting transfers between devices: none -> 17.9 us  [swap(): return lax.ppermute(value, 'prow', [(p, p ^ 1) for p in range(nprow)])]
    all_to_all x0 -> x2, starting transfers between devices: none -> 13.2 us  [the longest x1 9.67 us: on_device(): whole = lax.all_to_all(copies, 'pcol', 0, 0).reshape(nrows, nbw)]
    gather x3 -> x0, local copies, waits for them, and re-layouts: 10.1 us -> none  [the longest x2 6.8 us: on_device(): incoming = jnp.take(former, jnp.clip(slot - 1, 0, nbw - 1), axis=0)]
    pallas_call x0 -> x8, Pallas kernels: none -> 9.11 us  [the longest x1 5.05 us: final(): pl.pallas_call(final_kernel, grid=(ncols // step,), out_shape=jax.ShapeDt...]
  transfers between devices with their start and end apart: 1 -> 4, of which waited for: 1 -> 4; matrix products, arithmetic and copies ran while one was open for 2% -> 0% of each run, Pallas kernels for 0% -> 1%
where the time goes in v1:
time: 95.9 us; the launch traced here: 94 us
  starting transfers between devices  31.1 us (32%)
  waiting for transfers between devices  23.3 us (24%)
  blocking collectives  21 us (22%)
  local copies, waits for them, and re-layouts  9.26 us (10%)
  Pallas kernels  9.11 us (9%)
    all_to_all x1, blocking collectives, exchange(): lax.all_to_all(value, 'prow', 0, 0, axis_index_groups=columns, tiled=True)  21 us
    ppermute x2, starting transfers between devices, swap(): return lax.ppermute(value, 'prow', [(p, p ^ 1) for p in range(nprow)])  17.9 us
    all_to_all x1, waiting for transfers between devices, on_device(): whole = lax.all_to_all(copies, 'pcol', 0, 0).reshape(nrows, nbw)  12.1 us
    all_to_all x1, starting transfers between devices, on_device(): whole = lax.all_to_all(copies, 'pcol', 0, 0).reshape(nrows, nbw)  9.67 us
    all_to_all x1, waiting for transfers between devices, exchange(): lax.all_to_all(value, 'prow', 0, 0, axis_index_groups=columns, tiled=True)  9.04 us
    unnamed x38, local copies, waits for them, and re-layouts  8.32 us
    pallas_call x1, Pallas kernels, final(): pl.pallas_call(final_kernel, grid=(ncols // step,), out_shape=jax.ShapeDt...  5.05 us
    all_to_all x1, starting transfers between devices, exchange(): lax.all_to_all(value, 'prow', 0, 0, axis_index_groups=columns, tiled=True)  3.49 us
  transfers between devices with their start and end apart: 4, of which 4 were waited for; matrix products, arithmetic and copies ran while one was open for 0% of the time, Pallas kernels for 1%

profile of v1, /device:TPU:1, one launch (start us, length us, event | category | flops | bytes accessed | tf_op | source)
XLA Modules:
  0.0 94.0 jit_solution(13358483906549005378)
XLA Ops:
  0.0 0.7 copy-done.15
  0.7 2.2 %scan.1 = (s32[2,128]{1,0:T(2,128)S(1)}, s32[2]{0:T(128)S(1)}) custom-call(s32[256]{0:T(256)S(1)} %copy-done.15, s32[1]{0:T(128)} %bitcast.me), custom_call_target="tpu_custom_call" | custom-call | bytes 1048576 | tf_op jit(solution)/shard_map/scan/pallas_call | solution.py:56
  2.9 0.0 copy-start
  2.9 1.6 %copy-done = f32[512,1024]{1,0:T(8,128)S(1)} copy-done((f32[512,1024]{1,0:T(8,128)S(1)}, f32[512,1024]{1,0:T(8,128)}, u32[]{:S(2)}) %copy-start) | copy-done | bytes 2097176
  4.4 0.7 copy-done.16
  5.1 0.7 pick.1
  5.8 0.0 copy-start.12
  5.8 9.3 %collective-permute-start = (f32[128,1024]{1,0:T(8,128)S(1)}, f32[128,1024]{1,0:T(8,128)S(1)}, u32[]{:S(2)}, u32[]{:S(2)}) collective-permute-start(f32[128,1024]{1,0:T(8,128)S(1)} %get-tuple-element.18.give), channel_id=1, source_target_pairs={{0,32},{32,0},{64,96},{96,64},{128,160},{160,128},{192,224},{224,1... | collective-permute-start | bytes 1572872 | tf_op jit(solution)/shard_map/ppermute | solution.py:288
  15.1 1.5 %collective-permute-done.got = f32[128,1024]{1,0:T(8,128)S(1)} collective-permute-done((f32[128,1024]{1,0:T(8,128)S(1)}, f32[128,1024]{1,0:T(8,128)S(1)}, u32[]{:S(2)}, u32[]{:S(2)}) %collective-permute-start) | collective-permute-done | bytes 524320 | tf_op jit(solution)/shard_map/ppermute | solution.py:288
  16.6 0.1 broadcast_in_dim.7.owner
  16.7 0.1 deal.1
  16.8 21.0 %all_to_all.27 = f32[8,16,1024]{2,1,0:T(8,128)S(1)} all-to-all(f32[8,16,1024]{2,1,0:T(8,128)S(1)} %bitcast.11), channel_id=1, replica_groups={{0,64,128,192,256,320,384,448},{32,96,160,224,288,352,416,480},{1,65,12..., dimensions={0} | all-to-all | bytes 1048576 | tf_op jit(solution)/shard_map/all_to_all | solution.py:291
  37.9 0.0 copy-done.12
  37.9 0.0 copy-done.5
  37.9 0.0 copy-done.18
  37.9 0.0 copy-start.14
  37.9 0.9 broadcast_in_dim.8
  38.7 9.7 %all-to-all-start = ((f32[32,16,256]{2,1,0:T(8,128)}), f32[32,16,256]{2,1,0:T(8,128)S(1)}, u32[]{:S(2)}, u32[]{:S(2)}) async-start(f32[32,16,256]{2,1,0:T(8,128)} %broadcast_in_dim.8), calls=%async_computation | async-start | bytes 1048576 | tf_op jit(solution)/shard_map/all_to_all | solution.py:300
  48.4 0.0 copy-start.17
  48.4 0.1 home.1
  48.5 0.0 copy-start.4
  48.5 0.8 copy-done.4
  49.3 12.1 %all-to-all-done = f32[32,16,256]{2,1,0:T(8,128)S(1)} async-done(((f32[32,16,256]{2,1,0:T(8,128)}), f32[32,16,256]{2,1,0:T(8,128)S(1)}, u32[]{:S(2)}, u32[]{:S(2)}) %all-to-all-start) | async-done | bytes 524320 | tf_op jit(solution)/shard_map/all_to_all | solution.py:300
  61.5 0.8 copy-done.2
  62.2 3.5 %all-to-all-start.2 = ((f32[8,16,1024]{2,1,0:T(8,128)}), f32[8,16,1024]{2,1,0:T(8,128)S(1)}, u32[]{:S(2)}, u32[]{:S(2)}) async-start(f32[8,16,1024]{2,1,0:T(8,128)} %bitcast.9), calls=%async_computation.2 | async-start | bytes 1048576 | tf_op jit(solution)/shard_map/all_to_all | solution.py:291
  65.7 0.0 copy-done.14
  65.8 0.0 copy-start.3
  65.8 1.0 %copy-done.3 = f32[32,16,256]{2,1,0:T(8,128)S(1)} copy-done((f32[32,16,256]{2,1,0:T(8,128)S(1)}, f32[32,16,256]{2,1,0:T(8,128)}, u32[]{:S(2)}) %copy-start.3) | copy-done | bytes 524312
  66.8 0.2 split.1
  67.0 0.0 copy-start.7
  67.0 0.8 copy-done.7
  67.8 0.9 copy-done.10
  68.6 9.0 %all-to-all-done.2 = f32[8,16,1024]{2,1,0:T(8,128)S(1)} async-done(((f32[8,16,1024]{2,1,0:T(8,128)}), f32[8,16,1024]{2,1,0:T(8,128)S(1)}, u32[]{:S(2)}, u32[]{:S(2)}) %all-to-all-start.2) | async-done | bytes 524320 | tf_op jit(solution)/shard_map/all_to_all | solution.py:291
  77.7 1.1 %copy-done.8 = bf16[256,768]{1,0:T(8,128)(2,1)S(1)} copy-done((bf16[256,768]{1,0:T(8,128)(2,1)S(1)}, bf16[256,768]{1,0:T(8,128)(2,1)}, u32[]{:S(2)}) %copy-start.8) | copy-done | bytes 393240
  78.7 0.1 pair.1
  78.8 0.0 copy-start.9
  78.8 0.0 copy-start.11
  78.8 0.0 copy-start.13
  78.8 8.6 %collective-permute-start.1 = (f32[128,1024]{1,0:T(8,128)S(1)}, f32[128,1024]{1,0:T(8,128)S(1)}, u32[]{:S(2)}, u32[]{:S(2)}) collective-permute-start(f32[128,1024]{1,0:T(8,128)S(1)} %pair.1), channel_id=1, source_target_pairs={{0,32},{32,0},{64,96},{96,64},{128,160},{160,128},{192,224},{224,1... | collective-permute-start | bytes 1572872 | tf_op jit(solution)/shard_map/ppermute | solution.py:288
  87.4 0.0 copy-done.17
  87.4 0.0 copy-done.1
  87.4 0.0 copy-done.6
  87.5 0.9 ready.1
  88.3 0.6 collective-permute-done.1.got
  88.9 0.0 copy-done.9
  88.9 0.0 copy-done.11
  88.9 0.0 copy-done.13
  88.9 5.1 %final.1 = f32[512,1024]{1,0:T(8,128)} custom-call(s32[256]{0:T(256)S(1)} %copy-done.17, s32[1]{0:T(128)} %bitcast.me, s32[2,128]{1,0:T(2,128)S(1)} %get-tuple-element.13.lists, s32[2]{0:T(128)S(1)} %get-tuple-element.14.counts, s32[256,128]{1,0:T(8,128)S(1)} %broadcast_in_dim.7.owner, bf16[256,768]{1,0:T(8,128)(2,1)S(1)} %copy-done.9, ...), custom_call_target="tpu_custom_call" | custom-call | flops 1207959552 | bytes 4194304 | tf_op jit(solution)/shard_map/final/pallas_call | solution.py:268
  (10 shorter events, 0.0 us)
Async XLA Ops:
  0.0 0.7 copy-start.15
  2.9 1.6 %copy-start = (f32[512,1024]{1,0:T(8,128)S(1)}, f32[512,1024]{1,0:T(8,128)}, u32[]{:S(2)}) copy-start(f32[512,1024]{1,0:T(8,128)} %win.3) | copy-start | bytes 6291460
  4.4 0.7 copy-start.16
  5.1 32.7 %copy-start.18 = (f32[16,256]{1,0:T(8,128)S(1)}, f32[16,256]{1,0:T(8,128)}, u32[]{:S(2)}) copy-start(f32[16,256]{1,0:T(8,128)} %param.5) | copy-start | bytes 49156
  5.8 32.1 %copy-start.12 = (f32[128,1024]{1,0:T(8,128)}, f32[128,1024]{1,0:T(8,128)S(1)}, u32[]{:S(2)}) copy-start(f32[128,1024]{1,0:T(8,128)S(1)} %get-tuple-element.18.give) | copy-start | bytes 1572868
  5.8 10.8 %collective-permute-start = (f32[128,1024]{1,0:T(8,128)S(1)}, f32[128,1024]{1,0:T(8,128)S(1)}, u32[]{:S(2)}, u32[]{:S(2)}) collective-permute-start(f32[128,1024]{1,0:T(8,128)S(1)} %get-tuple-element.18.give), channel_id=1, source_target_pairs={{0,32},{32,0},{64,96},{96,64},{128,160},{160,128},{192,224},{224,1... | collective-permute-start | bytes 1572872 | tf_op jit(solution)/shard_map/ppermute | solution.py:288
  16.6 21.2 %copy-start.5 = (f32[128,1024]{1,0:T(8,128)}, f32[128,1024]{1,0:T(8,128)S(1)}, u32[]{:S(2)}) copy-start(f32[128,1024]{1,0:T(8,128)S(1)} %collective-permute-done.got) | copy-start | bytes 1572868
  37.9 27.9 %copy-start.14 = (f32[256,256]{1,0:T(8,128)S(1)}, f32[256,256]{1,0:T(8,128)}, u32[]{:S(2)}) copy-start(f32[256,256]{1,0:T(8,128)} %linv.1) | copy-start | bytes 786436
  38.7 22.7 %all-to-all-start = ((f32[32,16,256]{2,1,0:T(8,128)}), f32[32,16,256]{2,1,0:T(8,128)S(1)}, u32[]{:S(2)}, u32[]{:S(2)}) async-start(f32[32,16,256]{2,1,0:T(8,128)} %broadcast_in_dim.8), calls=%async_computation | async-start | bytes 1048576 | tf_op jit(solution)/shard_map/all_to_all | solution.py:300
  48.4 39.0 %copy-start.17 = (s32[256]{0:T(256)S(1)}, s32[256]{0:T(256)}, u32[]{:S(2)}) copy-start(s32[256]{0:T(256)} %piv.7) | copy-start | bytes 3076
  48.5 0.8 copy-start.4
  49.3 38.1 %copy-start.1 = (f32[512,1024]{1,0:T(8,128)S(1)}, f32[512,1024]{1,0:T(8,128)}, u32[]{:S(2)}) copy-start(f32[512,1024]{1,0:T(8,128)} %win.3) | copy-start | bytes 6291460
  61.4 0.8 copy-start.2
  62.2 15.4 %all-to-all-start.2 = ((f32[8,16,1024]{2,1,0:T(8,128)}), f32[8,16,1024]{2,1,0:T(8,128)S(1)}, u32[]{:S(2)}, u32[]{:S(2)}) async-start(f32[8,16,1024]{2,1,0:T(8,128)} %bitcast.9), calls=%async_computation.2 | async-start | bytes 1048576 | tf_op jit(solution)/shard_map/all_to_all | solution.py:291
  65.8 1.0 %copy-start.3 = (f32[32,16,256]{2,1,0:T(8,128)S(1)}, f32[32,16,256]{2,1,0:T(8,128)}, u32[]{:S(2)}) copy-start(f32[32,16,256]{2,1,0:T(8,128)} %copy-done.2) | copy-start | bytes 1572868
  67.0 0.8 copy-start.7
  67.7 0.9 copy-start.10
  77.7 9.8 %copy-start.6 = (f32[128,1024]{1,0:T(8,128)S(1)}, f32[128,1024]{1,0:T(8,128)}, u32[]{:S(2)}) copy-start(f32[128,1024]{1,0:T(8,128)} %copy-done.5) | copy-start | bytes 1572868
  77.7 1.1 %copy-start.8 = (bf16[256,768]{1,0:T(8,128)(2,1)S(1)}, bf16[256,768]{1,0:T(8,128)(2,1)}, u32[]{:S(2)}) copy-start(bf16[256,768]{1,0:T(8,128)(2,1)} %copy-done.7) | copy-start | bytes 1179652
  78.8 10.1 %copy-start.9 = (bf16[256,768]{1,0:T(8,128)(2,1)S(1)}, bf16[256,768]{1,0:T(8,128)(2,1)}, u32[]{:S(2)}) copy-start(bf16[256,768]{1,0:T(8,128)(2,1)} %copy-done.7) | copy-start | bytes 1179652
  78.8 10.1 %copy-start.11 = (bf16[512,768]{1,0:T(8,128)(2,1)S(1)}, bf16[512,768]{1,0:T(8,128)(2,1)}, u32[]{:S(2)}) copy-start(bf16[512,768]{1,0:T(8,128)(2,1)} %copy-done.10) | copy-start | bytes 2359300
  78.8 10.1 %copy-start.13 = (f32[128,1024]{1,0:T(8,128)S(1)}, f32[128,1024]{1,0:T(8,128)}, u32[]{:S(2)}) copy-start(f32[128,1024]{1,0:T(8,128)} %copy-done.12) | copy-start | bytes 1572868
  78.8 10.1 %collective-permute-start.1 = (f32[128,1024]{1,0:T(8,128)S(1)}, f32[128,1024]{1,0:T(8,128)S(1)}, u32[]{:S(2)}, u32[]{:S(2)}) collective-permute-start(f32[128,1024]{1,0:T(8,128)S(1)} %pair.1), channel_id=1, source_target_pairs={{0,32},{32,0},{64,96},{96,64},{128,160},{160,128},{192,224},{224,1... | collective-permute-start | bytes 1572872 | tf_op jit(solution)/shard_map/ppermute | solution.py:288

commit v2 on v1

v2 whole, which is shorter than its diff:
```python
import functools

import jax
import jax.numpy as jnp
from jax import lax
from jax.experimental import pallas as pl
from jax.experimental.pallas import tpu as pltpu
from jax.sharding import PartitionSpec as P

CORES = 2
YS = 8
LANES = 128
STEP = 256
PARAMS = pltpu.CompilerParams(vmem_limit_bytes=32 * 1024 * 1024)
ROOMY = pltpu.CompilerParams(vmem_limit_bytes=58 * 1024 * 1024)


def vmem(count):
    return [pl.BlockSpec(memory_space=pltpu.VMEM)] * count


def smem(count):
    return [pl.BlockSpec(memory_space=pltpu.SMEM)] * count


def cost(flops, nbytes):
    return pl.CostEstimate(flops=flops, bytes_accessed=nbytes, transcendentals=0)


def tiles(ncols):
    return [slice(c, c + LANES) for c in range(0, ncols, LANES)]


def sides(me, half):
    core = lax.rem(me, CORES)
    return core, me + 1 - 2 * core, core * half, half - core * half


def each(count, body):
    def four(j, carry):
        for u in range(4):
            body(jnp.minimum(4 * j + u, count - 1))
        return carry

    lax.fori_loop(0, (count + 3) // 4, four, 0)


def pick_kernel(piv, me, win, own, give, slots, rows, counts, held, sem):
    nrows = win.shape[0]
    half = own.shape[0]
    _, _, base, other = sides(me[0], half)
    first = me[0] * nrows
    load = pltpu.make_async_copy(win, held, sem)
    load.start()

    def step(i, totals):
        new = []
        for side, start in enumerate((base, other)):
            local = piv[start + i] - first
            inside = (local >= 0) & (local < nrows)
            slots[side, totals[side]] = i
            rows[side, totals[side]] = local
            new.append(totals[side] + inside.astype(jnp.int32))
        return tuple(new)

    totals = lax.fori_loop(0, half, step, (jnp.int32(0), jnp.int32(0)), unroll=8)
    load.wait()
    for side, start, out in ((1, other, give), (0, base, own)):
        counts[side] = totals[side]
        out[...] = held[pl.ds(pl.multiple_of(start, half), half), :]

        def put(i, side=side, out=out):
            out[pl.ds(slots[side, i], 1), :] = held[pl.ds(rows[side, i], 1), :]

        each(totals[side], put)


def pick(pivots, me, window):
    half = pivots.shape[0] // CORES
    ncols = window.shape[1]
    block = jax.ShapeDtypeStruct((half, ncols), window.dtype)
    table = jax.ShapeDtypeStruct((CORES, half), jnp.int32)
    out = pl.pallas_call(
        pick_kernel,
        out_shape=(block, block, table, table, jax.ShapeDtypeStruct((CORES,), jnp.int32)),
        in_specs=smem(2) + [pl.BlockSpec(memory_space=pltpu.HBM)],
        out_specs=tuple(vmem(2) + smem(3)),
        scratch_shapes=[pltpu.VMEM(window.shape, window.dtype), pltpu.SemaphoreType.DMA],
        compiler_params=ROOMY,
        cost_estimate=cost(0, 16 * half * ncols),
        name="pick",
    )(pivots, me, window)
    return out[0], out[1], out[2:]


def half_of(owner, base, half):
    return owner[pl.ds(pl.multiple_of(base, half), half), :]


def deal_kernel(me, owner, own, got, panel, out, same):
    half, ncols = own.shape
    _, partner, base, _ = sides(me[0], half)
    who = half_of(owner, base, half)
    theirs = (who == partner) | ((who != me[0]) & (who != jnp.where(me[0] == 0, who, -1)))
    for cols in tiles(ncols):
        out[:, cols] = jnp.where(theirs, got[:, cols], own[:, cols])
    same[...] = panel[...]


def line_kernel(me, *refs):
    pieces, out = refs[:-1], refs[-1]
    rows = pieces[0].shape[0]
    at = me[2] // 2
    for d, piece in enumerate(pieces):
        source = lax.rem(at - d + len(pieces), len(pieces))
        out[pl.ds(pl.multiple_of(source * rows, rows), rows), :] = piece[...]


def home_kernel(nz, part_rows, me, owner, got, mine, theirs, out, strip):
    half, ncols = got.shape
    part = half // nz
    _, _, base, _ = sides(me[0], half)
    at = pl.multiple_of(base + me[0] // CORES * part, part)
    chip = owner[pl.ds(at, part), :] // CORES
    for cols in tiles(ncols):
        former = got[0:part, cols]
        top = former
        for z in range(1, nz):
            top = jnp.where(chip == z, got[z * part : (z + 1) * part, cols], top)
        for z in range(nz):
            out[z * part : (z + 1) * part, cols] = jnp.where(chip == z, former, top)
    odd = lax.rem(me[2], 2)
    for q in range(mine.shape[0] // part_rows):
        source = slice(q * part_rows, (q + 1) * part_rows)
        for block, side in ((mine, odd), (theirs, 1 - odd)):
            strip[pl.ds(pl.multiple_of((2 * q + side) * part_rows, part_rows), part_rows), :] = block[source, :]


def pair_kernel(me, owner, own, got, token, out):
    half, ncols = own.shape
    _, partner, base, _ = sides(me[0], half)
    who = half_of(owner, base, half)
    mine = (who == me[0]) | (who == jnp.where(me[0] == 0, partner, me[0]))
    for cols in tiles(ncols):
        out[:, cols] = jnp.where(mine, own[:, cols], got[:, cols])


def local(kernel, name, shapes, me, *blocks):
    outs = tuple(jax.ShapeDtypeStruct(shape, jnp.float32) for shape in shapes)
    return pl.pallas_call(
        kernel,
        out_shape=outs,
        in_specs=smem(1) + vmem(len(blocks)),
        out_specs=tuple(vmem(len(outs))),
        compiler_params=PARAMS,
        cost_estimate=cost(0, 4 * sum(block.size for block in blocks)),
        name=name,
    )(me, *blocks)


def parts(value):
    high = value.astype(jnp.bfloat16)
    return high, (value - high.astype(jnp.float32)).astype(jnp.bfloat16)


def split_kernel(me, linv, *refs):
    strips, (left, right, token) = refs[:-3], refs[-3:]
    nb = linv.shape[1]

    def put(value, out, rows):
        high, low = parts(value)
        out[rows, 0:nb] = high
        out[rows, nb : 2 * nb] = low
        out[rows, 2 * nb : 3 * nb] = high

    put(linv[...], left, slice(None))
    count = strips[0].shape[0]
    for d, strip in enumerate(strips):
        source = lax.rem(me[1] - d + len(strips), len(strips))
        put(strip[...], right, pl.ds(pl.multiple_of(source * count, count), count))
    token[...] = jnp.zeros_like(token)


def split(me, linv, strips):
    nb = linv.shape[1]
    nrows = sum(strip.shape[0] for strip in strips)
    return pl.pallas_call(
        split_kernel,
        out_shape=(
            jax.ShapeDtypeStruct((nb, 3 * nb), jnp.bfloat16),
            jax.ShapeDtypeStruct((nrows, 3 * nb), jnp.bfloat16),
            jax.ShapeDtypeStruct((8, LANES), jnp.float32),
        ),
        in_specs=smem(1) + vmem(1 + len(strips)),
        out_specs=tuple(vmem(3)),
        compiler_params=PARAMS,
        cost_estimate=cost(0, 10 * nb * (nb + nrows)),
        name="split",
    )(me, linv, *strips)


def ready_kernel(me, slots, rows, counts, owner, own, got, far, win, top, swapped):
    half, ncols = own.shape
    _, partner, base, other = sides(me[0], half)
    who = half_of(owner, base, half)
    for cols in tiles(ncols):
        theirs = jnp.where(who == partner, got[:, cols], far[:, cols])
        top[:, cols] = jnp.where(who == me[0], own[:, cols], theirs)
    swapped[...] = win[...]

    def put(source, side, start):
        def one(i):
            swapped[pl.ds(rows[side, i], 1), :] = source[pl.ds(start + slots[side, i], 1), :]

        each(counts[side], one)

    @pl.when(me[0] == 0)
    def _():
        put(win, 0, base)
        put(win, 1, other)

    @pl.when(me[0] == 1)
    def _():
        put(got, 0, 0)

    @pl.when(me[0] > 1)
    def _():
        put(far, 0, 0)


def ready(me, table, owner, own, got, far, window):
    return pl.pallas_call(
        ready_kernel,
        out_shape=(
            jax.ShapeDtypeStruct(own.shape, own.dtype),
            jax.ShapeDtypeStruct(window.shape, window.dtype),
        ),
        in_specs=smem(4) + vmem(5),
        out_specs=tuple(vmem(2)),
        compiler_params=PARAMS,
        cost_estimate=cost(0, 8 * window.size + 16 * own.size),
        name="ready",
    )(me, *table, owner, own, got, far, window)


def final_kernel(me, slots, rows, counts, owner, left, right, swapped, top, give, got, out, full, rhs):
    half = top.shape[0]
    nb = 2 * half
    nrows, step = out.shape
    _, _, base, other = sides(me[0], half)
    base = pl.multiple_of(base, half)
    other = pl.multiple_of(other, half)
    at = pl.multiple_of(pl.program_id(0) * step, step)
    who = half_of(owner, other, half)
    full[pl.ds(base, half), :] = top[:, pl.ds(at, step)]
    for c in range(0, step, LANES):
        cols = pl.ds(pl.multiple_of(at + c, LANES), LANES)
        full[pl.ds(other, half), c : c + LANES] = jnp.where(who == me[0], give[:, cols], got[:, cols])

    def product(factor, value):
        high, low = parts(value)
        rhs[0:nb, :] = high
        rhs[nb : 2 * nb, :] = high
        rhs[2 * nb : 3 * nb, :] = low
        return jnp.dot(factor[...], rhs[...], preferred_element_type=jnp.float32)

    out[...] = swapped[:, pl.ds(at, step)]

    def put(i):
        out[pl.ds(rows[1, i], 1), :] = got[pl.ds(slots[1, i], 1), pl.ds(at, step)]

    each(jnp.where(me[0] == 0, 0, counts[1]), put)
    solved = product(left, full[...])
    out[...] = out[...] - product(right, solved)

    @pl.when(me[0] == 0)
    def _():
        out[0:nb, :] = solved


def final(me, table, owner, left, right, swapped, top, give, got):
    nrows, ncols = swapped.shape
    nb = 2 * top.shape[0]
    step = min(STEP, ncols)
    return pl.pallas_call(
        final_kernel,
        grid=(ncols // step,),
        out_shape=jax.ShapeDtypeStruct(swapped.shape, swapped.dtype),
        in_specs=smem(4) + vmem(7),
        out_specs=pl.BlockSpec((nrows, step), lambda c: (0, c)),
        scratch_shapes=[pltpu.VMEM((nb, step), jnp.float32), pltpu.VMEM((3 * nb, step), jnp.bfloat16)],
        compiler_params=PARAMS,
        cost_estimate=cost(6 * (nb + nrows) * nb * ncols, 8 * nrows * ncols),
        name="final",
    )(me, *table, owner, left, right, swapped, top, give, got)


def on_device(nprow, npcol, window, panel, linv, pivots):
    nrows, ncols = window.shape
    nbw = pivots.shape[0]
    nz = nprow // CORES
    columns = [[z * CORES + core for z in range(nz)] for core in range(CORES)]

    def swap(value):
        return lax.ppermute(value, "prow", [(p, p ^ 1) for p in range(nprow)])

    def exchange(value):
        return lax.all_to_all(value, "prow", 0, 0, axis_index_groups=columns, tiled=True)

    def ring(value, size, stride):
        span = size * stride
        pairs = lambda d: [(c, c // span * span + (c + d * stride) % span) for c in range(npcol)]
        return [value] + [lax.ppermute(value, "pcol", pairs(d)) for d in range(1, size)]

    pcol = lax.axis_index("pcol")
    me = jnp.stack([lax.axis_index("prow"), pcol // YS, pcol % YS]).astype(jnp.int32)
    owner = jnp.broadcast_to((pivots // nrows)[:, None], (nbw, LANES))
    half, strip = nbw // CORES, (YS * panel.shape[0], nbw)

    own, give, table = pick(pivots, me, window)
    got = swap(give)
    chip, rows = local(deal_kernel, "deal", [own.shape, panel.shape], me, owner, own, got, panel)
    dealt = exchange(chip)
    (mine,) = local(line_kernel, "line", [(strip[0] // 2, nbw)], me, *ring(rows, YS // 2, 2))
    theirs = lax.ppermute(mine, "pcol", [(c, c ^ 1) for c in range(npcol)])
    kernel = functools.partial(home_kernel, nz, panel.shape[0])
    chosen, whole = local(kernel, "home", [own.shape, strip], me, owner, dealt, mine, theirs)
    far = exchange(chosen)
    left, right, token = split(me, linv, ring(whole, npcol // YS, YS))
    (paired,) = local(pair_kernel, "pair", [own.shape], me, owner, own, far, token)
    last = swap(paired)
    top, swapped = ready(me, table, owner, own, got, far, window)
    return final(me, table, owner, left, right, swapped, top, give, last)


def solution(mesh):
    return jax.shard_map(
        functools.partial(on_device, mesh.shape["prow"], mesh.shape["pcol"]),
        mesh=mesh,
        in_specs=(P("prow", "pcol"), P(("prow", "pcol"), None), P(), P()),
        out_specs=P("prow", "pcol"),
        check_vma=False,
    )
```

time: 95.9 us -> 89.4 us (0.932); the launches traced: 94 us -> 88.6 us
  starting transfers between devices: 31.1 us -> 53.4 us
  blocking collectives: 21 us -> 0 us
  waiting for transfers between devices: 23.3 us -> 10.2 us
  Pallas kernels: 9.11 us -> 14.2 us
    ppermute x0 -> x7, starting transfers between devices: none -> 26.2 us  [the longest x6 22.9 us: ring(): lax.ppermute(value, 'pcol', pairs(d))]
    all_to_all x1 -> x0, blocking collectives: 21 us -> none  [exchange(): lax.all_to_all(value, 'prow', 0, 0, axis_index_groups=columns, tiled=True)]
    all_to_all x1 -> x0, waiting for transfers between devices: 12.1 us -> none  [on_device(): whole = lax.all_to_all(copies, 'pcol', 0, 0).reshape(nrows, nbw)]
    all_to_all x1 -> x0, starting transfers between devices: 9.67 us -> none  [on_device(): whole = lax.all_to_all(copies, 'pcol', 0, 0).reshape(nrows, nbw)]
    all_to_all x1 -> x2, waiting for transfers between devices: 9.04 us -> 0.01 us  [exchange(): lax.all_to_all(value, 'prow', 0, 0, axis_index_groups=columns, tiled=True)]
    ppermute x0 -> x7, waiting for transfers between devices: none -> 8.49 us  [the longest x6 7.38 us: ring(): lax.ppermute(value, 'pcol', pairs(d))]
    all_to_all x1 -> x2, starting transfers between devices: 3.49 us -> 11.1 us  [exchange(): lax.all_to_all(value, 'prow', 0, 0, axis_index_groups=columns, tiled=True)]
    pallas_call x6, Pallas kernels: 3.2 us -> 7.53 us  [the longest x1 3.68 us: pick(): pl.pallas_call(pick_kernel, out_shape=(block, block, table, table, jax.Sh...]
  transfers between devices with their start and end apart: 4 -> 11, of which waited for: 4 -> 6; matrix products, arithmetic and copies ran while one was open for 0% -> 0% of each run, Pallas kernels for 1% -> 3%
where the time goes in v2:
time: 89.4 us; the launch traced here: 88.6 us
  starting transfers between devices  53.4 us (60%)
  Pallas kernels  14.2 us (16%)
  waiting for transfers between devices  10.2 us (11%)
  local copies, waits for them, and re-layouts  9.78 us (11%)
    ppermute x6, starting transfers between devices, ring(): lax.ppermute(value, 'pcol', pairs(d))  22.9 us
    ppermute x2, starting transfers between devices, swap(): return lax.ppermute(value, 'prow', [(p, p ^ 1) for p in range(nprow)])  16.1 us
    all_to_all x2, starting transfers between devices, exchange(): lax.all_to_all(value, 'prow', 0, 0, axis_index_groups=columns, tiled=True)  11.1 us
    unnamed x48, local copies, waits for them, and re-layouts  9.69 us
    ppermute x6, waiting for transfers between devices, ring(): lax.ppermute(value, 'pcol', pairs(d))  7.38 us
    pallas_call x1, Pallas kernels, final(): pl.pallas_call(final_kernel, grid=(ncols // step,), out_shape=jax.ShapeDt...  5.7 us
    pallas_call x1, Pallas kernels, pick(): pl.pallas_call(pick_kernel, out_shape=(block, block, table, table, jax.Sh...  3.68 us
    ppermute x1, starting transfers between devices, on_device(): theirs = lax.ppermute(mine, 'pcol', [(c, c ^ 1) for c in range(npcol)])  3.27 us
  transfers between devices with their start and end apart: 11, of which 6 were waited for; matrix products, arithmetic and copies ran while one was open for 0% of the time, Pallas kernels for 3%

profile of v2, /device:TPU:1, one launch (start us, length us, event | category | flops | bytes accessed | tf_op | source)
XLA Modules:
  0.0 88.6 jit_solution(11560031838166157992)
XLA Ops:
  0.0 0.6 pad_add_fusion.me
  0.6 3.7 %pick.1 = (f32[128,1024]{1,0:T(8,128)}, f32[128,1024]{1,0:T(8,128)}, s32[2,128]{1,0:T(2,128)}, s32[2,128]{1,0:T(2,128)}, s32[2]{0:T(128)}) custom-call(s32[256]{0:T(256)} %piv.1, s32[3]{0:T(128)} %pad_add_fusion.me, f32[512,1024]{1,0:T(8,128)} %win.3), custom_call_target="tpu_custom_call" | custom-call | bytes 2097152 | tf_op jit(solution)/shard_map/pick/pallas_call | solution.py:83
  4.3 8.8 %collective-permute-start = (f32[128,1024]{1,0:T(8,128)}, f32[128,1024]{1,0:T(8,128)S(1)}, u32[]{:S(2)}, u32[]{:S(2)}) collective-permute-start(f32[128,1024]{1,0:T(8,128)} %get-tuple-element.23.give), channel_id=1, source_target_pairs={{0,32},{32,0},{64,96},{96,64},{128,160},{160,128},{192,224},{224,1... | collective-permute-start | bytes 1572872 | tf_op jit(solution)/shard_map/ppermute | solution.py:305
  13.2 1.7 %collective-permute-done.got = f32[128,1024]{1,0:T(8,128)S(1)} collective-permute-done((f32[128,1024]{1,0:T(8,128)}, f32[128,1024]{1,0:T(8,128)S(1)}, u32[]{:S(2)}, u32[]{:S(2)}) %collective-permute-start) | collective-permute-done | bytes 524320 | tf_op jit(solution)/shard_map/ppermute | solution.py:305
  14.9 0.1 broadcast_in_dim.2.owner
  15.0 1.1 %copy-done.1 = f32[128,1024]{1,0:T(8,128)S(1)} copy-done((f32[128,1024]{1,0:T(8,128)S(1)}, f32[128,1024]{1,0:T(8,128)}, u32[]{:S(2)}) %copy-start.1) | copy-done | bytes 524312
  16.2 1.4 %deal.1 = (f32[128,1024]{1,0:T(8,128)}, f32[16,256]{1,0:T(8,128)S(1)}) custom-call(s32[3]{0:T(128)S(1)} %copy-done.18, s32[256,128]{1,0:T(8,128)S(1)} %broadcast_in_dim.2.owner, f32[128,1024]{1,0:T(8,128)S(1)} %copy-done.1, f32[128,1024]{1,0:T(8,128)S(1)} %collective-permute-done.got, f32[16,256]{1,0:T(8,128)S(1)} %copy-done.19), custom_call_target="tpu_custom_call" | custom-call | bytes 1196032 | tf_op jit(solution)/shard_map/deal/pallas_call | solution.py:150
  17.6 4.5 %all-to-all-start = ((f32[8,16,1024]{2,1,0:T(8,128)}), f32[8,16,1024]{2,1,0:T(8,128)S(1)}, u32[]{:S(2)}, u32[]{:S(2)}) async-start(f32[8,16,1024]{2,1,0:T(8,128)} %bitcast.3), calls=%async_computation | async-start | bytes 1048576 | tf_op jit(solution)/shard_map/all_to_all | solution.py:308
  22.0 5.9 %collective-permute-start.3 = (f32[16,256]{1,0:T(8,128)S(1)}, f32[16,256]{1,0:T(8,128)S(1)}, u32[]{:S(2)}, u32[]{:S(2)}) collective-permute-start(f32[16,256]{1,0:T(8,128)S(1)} %get-tuple-element.25.refs_0_), channel_id=1, source_target_pairs={{0,6},{1,7},{2,0},{3,1},{4,2},{5,3},{6,4},{7,5},{8,14},{9,15},{10,... | collective-permute-start | bytes 49160 | tf_op jit(solution)/shard_map/ppermute | solution.py:313
  27.9 3.5 %collective-permute-start.2 = (f32[16,256]{1,0:T(8,128)S(1)}, f32[16,256]{1,0:T(8,128)S(1)}, u32[]{:S(2)}, u32[]{:S(2)}) collective-permute-start(f32[16,256]{1,0:T(8,128)S(1)} %get-tuple-element.25.refs_0_), channel_id=1, source_target_pairs={{0,4},{1,5},{2,6},{3,7},{4,0},{5,1},{6,2},{7,3},{8,12},{9,13},{10,... | collective-permute-start | bytes 49160 | tf_op jit(solution)/shard_map/ppermute | solution.py:313
  31.5 4.2 %collective-permute-start.1 = (f32[16,256]{1,0:T(8,128)S(1)}, f32[16,256]{1,0:T(8,128)S(1)}, u32[]{:S(2)}, u32[]{:S(2)}) collective-permute-start(f32[16,256]{1,0:T(8,128)S(1)} %get-tuple-element.25.refs_0_), channel_id=1, source_target_pairs={{0,2},{1,3},{2,4},{3,5},{4,6},{5,7},{6,0},{7,1},{8,10},{9,11},{10,... | collective-permute-start | bytes 49160 | tf_op jit(solution)/shard_map/ppermute | solution.py:313
  35.7 0.0 collective-permute-done.3.refs_3_
  35.7 0.6 collective-permute-done.2.refs_2_
  36.3 2.0 %collective-permute-done.1.refs_1_ = f32[16,256]{1,0:T(8,128)S(1)} collective-permute-done((f32[16,256]{1,0:T(8,128)S(1)}, f32[16,256]{1,0:T(8,128)S(1)}, u32[]{:S(2)}, u32[]{:S(2)}) %collective-permute-start.1) | collective-permute-done | bytes 16416 | tf_op jit(solution)/shard_map/ppermute | solution.py:313
  38.4 0.6 line.1.mine
  38.9 3.3 %collective-permute-start.4 = (f32[64,256]{1,0:T(8,128)S(1)}, f32[64,256]{1,0:T(8,128)S(1)}, u32[]{:S(2)}, u32[]{:S(2)}) collective-permute-start(f32[64,256]{1,0:T(8,128)S(1)} %line.1.mine), channel_id=1, source_target_pairs={{0,1},{1,0},{2,3},{3,2},{4,5},{5,4},{6,7},{7,6},{8,9},{9,8},{10,11... | collective-permute-start | bytes 196616 | tf_op jit(solution)/shard_map/ppermute | solution.py:325
  42.2 0.6 copy-done.12
  42.8 1.1 %collective-permute-done.4.theirs = f32[64,256]{1,0:T(8,128)S(1)} collective-permute-done((f32[64,256]{1,0:T(8,128)S(1)}, f32[64,256]{1,0:T(8,128)S(1)}, u32[]{:S(2)}, u32[]{:S(2)}) %collective-permute-start.4) | collective-permute-done | bytes 65568 | tf_op jit(solution)/shard_map/ppermute | solution.py:325
  43.9 0.6 copy-done.16
  44.6 0.0 all-to-all-done
  44.6 0.8 copy-done.13
  45.4 0.8 copy-done.17
  46.3 0.6 home.1
  46.9 0.8 copy-done.7
  47.7 0.7 copy-done.14
  48.3 6.7 %all-to-all-start.1 = ((f32[8,16,1024]{2,1,0:T(8,128)}), f32[8,16,1024]{2,1,0:T(8,128)S(1)}, u32[]{:S(2)}, u32[]{:S(2)}) async-start(f32[8,16,1024]{2,1,0:T(8,128)} %bitcast.10), calls=%async_computation.1 | async-start | bytes 1048576 | tf_op jit(solution)/shard_map/all_to_all | solution.py:308
  55.0 4.4 %collective-permute-start.7 = (f32[128,256]{1,0:T(8,128)}, f32[128,256]{1,0:T(8,128)S(1)}, u32[]{:S(2)}, u32[]{:S(2)}) collective-permute-start(f32[128,256]{1,0:T(8,128)} %copy-done.14), channel_id=1, source_target_pairs={{0,24},{1,25},{2,26},{3,27},{4,28},{5,29},{6,30},{7,31},{8,0},{9,1... | collective-permute-start | bytes 393224 | tf_op jit(solution)/shard_map/ppermute | solution.py:313
  59.4 2.4 %collective-permute-start.6 = (f32[128,256]{1,0:T(8,128)}, f32[128,256]{1,0:T(8,128)S(1)}, u32[]{:S(2)}, u32[]{:S(2)}) collective-permute-start(f32[128,256]{1,0:T(8,128)} %copy-done.14), channel_id=1, source_target_pairs={{0,16},{1,17},{2,18},{3,19},{4,20},{5,21},{6,22},{7,23},{8,24},{9,... | collective-permute-start | bytes 393224 | tf_op jit(solution)/shard_map/ppermute | solution.py:313
  61.8 2.5 %collective-permute-start.5 = (f32[128,256]{1,0:T(8,128)}, f32[128,256]{1,0:T(8,128)S(1)}, u32[]{:S(2)}, u32[]{:S(2)}) collective-permute-start(f32[128,256]{1,0:T(8,128)} %copy-done.14), channel_id=1, source_target_pairs={{0,8},{1,9},{2,10},{3,11},{4,12},{5,13},{6,14},{7,15},{8,16},{9,17... | collective-permute-start | bytes 393224 | tf_op jit(solution)/shard_map/ppermute | solution.py:313
  64.3 0.0 collective-permute-done.7.refs_3_
  64.4 2.5 %collective-permute-done.6.refs_2_ = f32[128,256]{1,0:T(8,128)S(1)} collective-permute-done((f32[128,256]{1,0:T(8,128)}, f32[128,256]{1,0:T(8,128)S(1)}, u32[]{:S(2)}, u32[]{:S(2)}) %collective-permute-start.6) | collective-permute-done | bytes 131104 | tf_op jit(solution)/shard_map/ppermute | solution.py:313
  66.8 2.3 %collective-permute-done.5.refs_1_ = f32[128,256]{1,0:T(8,128)S(1)} collective-permute-done((f32[128,256]{1,0:T(8,128)}, f32[128,256]{1,0:T(8,128)S(1)}, u32[]{:S(2)}, u32[]{:S(2)}) %collective-permute-start.5) | collective-permute-done | bytes 131104 | tf_op jit(solution)/shard_map/ppermute | solution.py:313
  69.1 0.9 %copy-done.15 = f32[128,256]{1,0:T(8,128)S(1)} copy-done((f32[128,256]{1,0:T(8,128)S(1)}, f32[128,256]{1,0:T(8,128)}, u32[]{:S(2)}) %copy-start.15) | copy-done | bytes 131096
  70.0 0.7 split.1
  70.7 0.0 copy-start.5
  70.7 0.9 copy-done.5
  71.5 0.8 copy-done.9
  72.3 0.0 all-to-all-done.1
  72.3 0.6 pair.1
  72.9 7.3 %collective-permute-start.8 = (f32[128,1024]{1,0:T(8,128)S(1)}, f32[128,1024]{1,0:T(8,128)S(1)}, u32[]{:S(2)}, u32[]{:S(2)}) collective-permute-start(f32[128,1024]{1,0:T(8,128)S(1)} %pair.1), channel_id=1, source_target_pairs={{0,32},{32,0},{64,96},{96,64},{128,160},{160,128},{192,224},{224,1... | collective-permute-start | bytes 1572872 | tf_op jit(solution)/shard_map/ppermute | solution.py:305
  80.2 1.0 %copy-done.4 = f32[128,1024]{1,0:T(8,128)S(1)} copy-done((f32[128,1024]{1,0:T(8,128)S(1)}, f32[128,1024]{1,0:T(8,128)}, u32[]{:S(2)}) %copy-start.4) | copy-done | bytes 524312
  81.3 0.6 copy-done.22
  81.9 1.0 %ready.1 = (f32[128,1024]{1,0:T(8,128)S(1)}, f32[512,1024]{1,0:T(8,128)S(1)}) custom-call(s32[3]{0:T(128)S(1)} %copy-done.18, s32[2,128]{1,0:T(2,128)S(1)} %copy-done.20, s32[2,128]{1,0:T(2,128)S(1)} %copy-done.21, s32[2]{0:T(128)S(1)} %copy-done.22, s32[256,128]{1,0:T(8,128)S(1)} %broadcast_in_dim.2.owner, f32[128,1024]{1,0:T(8,128)S(1)} %copy-done.2, ...), custom_call_target="tpu_custom_call" | custom-call | bytes 6291456 | tf_op jit(solution)/shard_map/ready/pallas_call | solution.py:232
  82.9 0.0 collective-permute-done.8.got
  82.9 0.0 copy-done.6
  82.9 0.0 copy-done.8
  82.9 0.0 copy-done.10
  82.9 5.7 %final.1 = f32[512,1024]{1,0:T(8,128)} custom-call(s32[3]{0:T(128)S(1)} %copy-done.18, s32[2,128]{1,0:T(2,128)S(1)} %copy-done.20, s32[2,128]{1,0:T(2,128)S(1)} %copy-done.21, s32[2]{0:T(128)S(1)} %copy-done.22, s32[256,128]{1,0:T(8,128)S(1)} %broadcast_in_dim.2.owner, bf16[256,768]{1,0:T(8,128)(2,1)S(1)} %copy-done.10, bf16[512,768]{1,0:T(8,128)(2,1)S(1)} %copy-done.6, ...), custom_call_target="tpu_custom_call" | custom-call | flops 1207959552 | bytes 4194304 | tf_op jit(solution)/shard_map/final/pallas_call | solution.py:285
  (33 shorter events, 0.1 us)
Async XLA Ops:
  0.0 13.2 %copy-start.23 = (s32[256]{0:T(256)S(1)}, s32[256]{0:T(256)}, u32[]{:S(2)}) copy-start(s32[256]{0:T(256)} %piv.1) | copy-start | bytes 3076
  0.0 15.0 %copy-start.19 = (f32[16,256]{1,0:T(8,128)S(1)}, f32[16,256]{1,0:T(8,128)}, u32[]{:S(2)}) copy-start(f32[16,256]{1,0:T(8,128)} %panel.1) | copy-start | bytes 49156
  0.6 14.4 %copy-start.18 = (s32[3]{0:T(128)S(1)}, s32[3]{0:T(128)}, u32[]{:S(2)}) copy-start(s32[3]{0:T(128)} %pad_add_fusion.me) | copy-start | bytes 40
  4.3 10.6 %collective-permute-start = (f32[128,1024]{1,0:T(8,128)}, f32[128,1024]{1,0:T(8,128)S(1)}, u32[]{:S(2)}, u32[]{:S(2)}) collective-permute-start(f32[128,1024]{1,0:T(8,128)} %get-tuple-element.23.give), channel_id=1, source_target_pairs={{0,32},{32,0},{64,96},{96,64},{128,160},{160,128},{192,224},{224,1... | collective-permute-start | bytes 1572872 | tf_op jit(solution)/shard_map/ppermute | solution.py:305
  14.9 2.6 %copy-start.3 = (f32[128,1024]{1,0:T(8,128)}, f32[128,1024]{1,0:T(8,128)S(1)}, u32[]{:S(2)}) copy-start(f32[128,1024]{1,0:T(8,128)S(1)} %collective-permute-done.got) | copy-start | bytes 1572868
  15.0 1.1 %copy-start.1 = (f32[128,1024]{1,0:T(8,128)S(1)}, f32[128,1024]{1,0:T(8,128)}, u32[]{:S(2)}) copy-start(f32[128,1024]{1,0:T(8,128)} %get-tuple-element.22.own) | copy-start | bytes 1572868
  16.2 52.9 %copy-start.11 = (f32[256,256]{1,0:T(8,128)S(1)}, f32[256,256]{1,0:T(8,128)}, u32[]{:S(2)}) copy-start(f32[256,256]{1,0:T(8,128)} %linv.1) | copy-start | bytes 786436
  17.6 54.8 %copy-start.2 = (f32[128,1024]{1,0:T(8,128)S(1)}, f32[128,1024]{1,0:T(8,128)}, u32[]{:S(2)}) copy-start(f32[128,1024]{1,0:T(8,128)} %get-tuple-element.22.own) | copy-start | bytes 1572868
  17.6 27.0 %all-to-all-start = ((f32[8,16,1024]{2,1,0:T(8,128)}), f32[8,16,1024]{2,1,0:T(8,128)S(1)}, u32[]{:S(2)}, u32[]{:S(2)}) async-start(f32[8,16,1024]{2,1,0:T(8,128)} %bitcast.3), calls=%async_computation | async-start | bytes 1048576 | tf_op jit(solution)/shard_map/all_to_all | solution.py:308
  22.0 13.6 %collective-permute-start.3 = (f32[16,256]{1,0:T(8,128)S(1)}, f32[16,256]{1,0:T(8,128)S(1)}, u32[]{:S(2)}, u32[]{:S(2)}) collective-permute-start(f32[16,256]{1,0:T(8,128)S(1)} %get-tuple-element.25.refs_0_), channel_id=1, source_target_pairs={{0,6},{1,7},{2,0},{3,1},{4,2},{5,3},{6,4},{7,5},{8,14},{9,15},{10,... | collective-permute-start | bytes 49160 | tf_op jit(solution)/shard_map/ppermute | solution.py:313
  27.9 8.4 %collective-permute-start.2 = (f32[16,256]{1,0:T(8,128)S(1)}, f32[16,256]{1,0:T(8,128)S(1)}, u32[]{:S(2)}, u32[]{:S(2)}) collective-permute-start(f32[16,256]{1,0:T(8,128)S(1)} %get-tuple-element.25.refs_0_), channel_id=1, source_target_pairs={{0,4},{1,5},{2,6},{3,7},{4,0},{5,1},{6,2},{7,3},{8,12},{9,13},{10,... | collective-permute-start | bytes 49160 | tf_op jit(solution)/shard_map/ppermute | solution.py:313
  31.5 6.9 %collective-permute-start.1 = (f32[16,256]{1,0:T(8,128)S(1)}, f32[16,256]{1,0:T(8,128)S(1)}, u32[]{:S(2)}, u32[]{:S(2)}) collective-permute-start(f32[16,256]{1,0:T(8,128)S(1)} %get-tuple-element.25.refs_0_), channel_id=1, source_target_pairs={{0,2},{1,3},{2,4},{3,5},{4,6},{5,7},{6,0},{7,1},{8,10},{9,11},{10,... | collective-permute-start | bytes 49160 | tf_op jit(solution)/shard_map/ppermute | solution.py:313
  38.4 41.9 %copy-start.21 = (s32[2,128]{1,0:T(2,128)S(1)}, s32[2,128]{1,0:T(2,128)}, u32[]{:S(2)}) copy-start(s32[2,128]{1,0:T(2,128)} %get-tuple-element.20.rows) | copy-start | bytes 3076
  38.9 5.0 %collective-permute-start.4 = (f32[64,256]{1,0:T(8,128)S(1)}, f32[64,256]{1,0:T(8,128)S(1)}, u32[]{:S(2)}, u32[]{:S(2)}) collective-permute-start(f32[64,256]{1,0:T(8,128)S(1)} %line.1.mine), channel_id=1, source_target_pairs={{0,1},{1,0},{2,3},{3,2},{4,5},{5,4},{6,7},{7,6},{8,9},{9,8},{10,11... | collective-permute-start | bytes 196616 | tf_op jit(solution)/shard_map/ppermute | solution.py:325
  42.2 0.6 copy-start.12
  43.9 0.6 copy-start.16
  44.6 35.7 %copy-start.20 = (s32[2,128]{1,0:T(2,128)S(1)}, s32[2,128]{1,0:T(2,128)}, u32[]{:S(2)}) copy-start(s32[2,128]{1,0:T(2,128)} %get-tuple-element.19.slots) | copy-start | bytes 3076
  44.6 0.8 copy-start.13
  45.4 0.8 copy-start.17
  46.2 34.0 %copy-start = (f32[512,1024]{1,0:T(8,128)S(1)}, f32[512,1024]{1,0:T(8,128)}, u32[]{:S(2)}) copy-start(f32[512,1024]{1,0:T(8,128)} %win.3) | copy-start | bytes 6291460
  46.9 0.8 copy-start.7
  47.7 0.7 copy-start.14
  48.3 24.0 %all-to-all-start.1 = ((f32[8,16,1024]{2,1,0:T(8,128)}), f32[8,16,1024]{2,1,0:T(8,128)S(1)}, u32[]{:S(2)}, u32[]{:S(2)}) async-start(f32[8,16,1024]{2,1,0:T(8,128)} %bitcast.10), calls=%async_computation.1 | async-start | bytes 1048576 | tf_op jit(solution)/shard_map/all_to_all | solution.py:308
  55.0 9.3 %collective-permute-start.7 = (f32[128,256]{1,0:T(8,128)}, f32[128,256]{1,0:T(8,128)S(1)}, u32[]{:S(2)}, u32[]{:S(2)}) collective-permute-start(f32[128,256]{1,0:T(8,128)} %copy-done.14), channel_id=1, source_target_pairs={{0,24},{1,25},{2,26},{3,27},{4,28},{5,29},{6,30},{7,31},{8,0},{9,1... | collective-permute-start | bytes 393224 | tf_op jit(solution)/shard_map/ppermute | solution.py:313
  59.4 7.4 %collective-permute-start.6 = (f32[128,256]{1,0:T(8,128)}, f32[128,256]{1,0:T(8,128)S(1)}, u32[]{:S(2)}, u32[]{:S(2)}) collective-permute-start(f32[128,256]{1,0:T(8,128)} %copy-done.14), channel_id=1, source_target_pairs={{0,16},{1,17},{2,18},{3,19},{4,20},{5,21},{6,22},{7,23},{8,24},{9,... | collective-permute-start | bytes 393224 | tf_op jit(solution)/shard_map/ppermute | solution.py:313
  61.8 7.3 %collective-permute-start.5 = (f32[128,256]{1,0:T(8,128)}, f32[128,256]{1,0:T(8,128)S(1)}, u32[]{:S(2)}, u32[]{:S(2)}) collective-permute-start(f32[128,256]{1,0:T(8,128)} %copy-done.14), channel_id=1, source_target_pairs={{0,8},{1,9},{2,10},{3,11},{4,12},{5,13},{6,14},{7,15},{8,16},{9,17... | collective-permute-start | bytes 393224 | tf_op jit(solution)/shard_map/ppermute | solution.py:313
  69.1 0.9 %copy-start.15 = (f32[128,256]{1,0:T(8,128)S(1)}, f32[128,256]{1,0:T(8,128)}, u32[]{:S(2)}) copy-start(f32[128,256]{1,0:T(8,128)} %copy-done.14) | copy-start | bytes 393220
  70.7 0.9 copy-start.5
  71.5 0.8 copy-start.9
  72.3 10.6 %copy-start.6 = (bf16[512,768]{1,0:T(8,128)(2,1)S(1)}, bf16[512,768]{1,0:T(8,128)(2,1)}, u32[]{:S(2)}) copy-start(bf16[512,768]{1,0:T(8,128)(2,1)} %copy-done.5) | copy-start | bytes 2359300
  72.3 10.6 %copy-start.8 = (f32[128,1024]{1,0:T(8,128)S(1)}, f32[128,1024]{1,0:T(8,128)}, u32[]{:S(2)}) copy-start(f32[128,1024]{1,0:T(8,128)} %get-tuple-element.23.give) | copy-start | bytes 1572868
  72.3 10.6 %copy-start.10 = (bf16[256,768]{1,0:T(8,128)(2,1)S(1)}, bf16[256,768]{1,0:T(8,128)(2,1)}, u32[]{:S(2)}) copy-start(bf16[256,768]{1,0:T(8,128)(2,1)} %copy-done.9) | copy-start | bytes 1179652
  72.9 9.9 %collective-permute-start.8 = (f32[128,1024]{1,0:T(8,128)S(1)}, f32[128,1024]{1,0:T(8,128)S(1)}, u32[]{:S(2)}, u32[]{:S(2)}) collective-permute-start(f32[128,1024]{1,0:T(8,128)S(1)} %pair.1), channel_id=1, source_target_pairs={{0,32},{32,0},{64,96},{96,64},{128,160},{160,128},{192,224},{224,1... | collective-permute-start | bytes 1572872 | tf_op jit(solution)/shard_map/ppermute | solution.py:305
  80.2 1.0 %copy-start.4 = (f32[128,1024]{1,0:T(8,128)S(1)}, f32[128,1024]{1,0:T(8,128)}, u32[]{:S(2)}) copy-start(f32[128,1024]{1,0:T(8,128)} %copy-done.3) | copy-start | bytes 1572868
  81.3 0.6 copy-start.22

commit v3 on v2

v3 whole, which is shorter than its diff:
```python
import functools

import jax
import jax.numpy as jnp
from jax import lax
from jax.experimental import pallas as pl
from jax.experimental.pallas import tpu as pltpu
from jax.sharding import PartitionSpec as P

CORES = 2
YS = 8
LANES = 128
STEP = 256
PARAMS = pltpu.CompilerParams(vmem_limit_bytes=32 * 1024 * 1024)
ROOMY = pltpu.CompilerParams(vmem_limit_bytes=58 * 1024 * 1024)


def vmem(count):
    return [pl.BlockSpec(memory_space=pltpu.VMEM)] * count


def smem(count):
    return [pl.BlockSpec(memory_space=pltpu.SMEM)] * count


def cost(flops, nbytes):
    return pl.CostEstimate(flops=flops, bytes_accessed=nbytes, transcendentals=0)


def tiles(ncols):
    return [slice(c, c + LANES) for c in range(0, ncols, LANES)]


def sides(half):
    me = lax.axis_index("prow")
    core = lax.rem(me, CORES)
    return me, me + 1 - 2 * core, core * half, half - core * half


def each(count, body):
    def four(j, carry):
        for u in range(4):
            body(jnp.minimum(4 * j + u, count - 1))
        return carry

    lax.fori_loop(0, (count + 3) // 4, four, 0)


def pick_kernel(piv, win, own, give, slots, rows, counts, held, sem):
    nrows = win.shape[0]
    half = own.shape[0]
    me, _, base, other = sides(half)
    first = me * nrows
    load = pltpu.make_async_copy(win, held, sem)
    load.start()

    def step(i, totals):
        new = []
        for side, start in enumerate((base, other)):
            local = piv[start + i] - first
            inside = (local >= 0) & (local < nrows)
            slots[side, totals[side]] = i
            rows[side, totals[side]] = local
            new.append(totals[side] + inside.astype(jnp.int32))
        return tuple(new)

    totals = lax.fori_loop(0, half, step, (jnp.int32(0), jnp.int32(0)), unroll=8)
    load.wait()
    for side, start, out in ((1, other, give), (0, base, own)):
        counts[side] = totals[side]
        out[...] = held[pl.ds(pl.multiple_of(start, half), half), :]

        def put(i, side=side, out=out):
            out[pl.ds(slots[side, i], 1), :] = held[pl.ds(rows[side, i], 1), :]

        each(totals[side], put)


def pick(pivots, window):
    half = pivots.shape[0] // CORES
    ncols = window.shape[1]
    block = jax.ShapeDtypeStruct((half, ncols), window.dtype)
    table = jax.ShapeDtypeStruct((CORES, half), jnp.int32)
    out = pl.pallas_call(
        pick_kernel,
        out_shape=(block, block, table, table, jax.ShapeDtypeStruct((CORES,), jnp.int32)),
        in_specs=smem(1) + [pl.BlockSpec(memory_space=pl.ANY)],
        out_specs=tuple(vmem(2) + smem(3)),
        scratch_shapes=[pltpu.VMEM(window.shape, window.dtype), pltpu.SemaphoreType.DMA],
        compiler_params=ROOMY,
        cost_estimate=cost(0, 16 * half * ncols),
        name="pick",
    )(pivots, window)
    return out[0], out[1], out[2:]


def half_of(owner, base, half):
    return owner[pl.ds(pl.multiple_of(base, half), half), :]


def deal_kernel(owner, own, got, panel, beside, out, rows):
    half, ncols = own.shape
    me, partner, base, _ = sides(half)
    who = half_of(owner, base, half)
    theirs = (who == partner) | ((who != me) & (who != jnp.where(me == 0, who, -1)))
    for cols in tiles(ncols):
        out[:, cols] = jnp.where(theirs, got[:, cols], own[:, cols])
    count = panel.shape[0]
    odd = lax.rem(lax.axis_index("pcol"), 2)
    rows[pl.ds(pl.multiple_of(odd * count, count), count), :] = panel[...]
    rows[pl.ds(pl.multiple_of((1 - odd) * count, count), count), :] = beside[...]


def ordered(index, pieces, put):
    count = pieces[0].shape[0]
    for d, piece in enumerate(pieces):
        source = lax.rem(index - d + len(pieces), len(pieces))
        put(pl.ds(pl.multiple_of(source * count, count), count), piece[...])


def home_kernel(nz, owner, got, *refs):
    pieces, (out, strip) = refs[:-2], refs[-2:]
    half, ncols = got.shape
    part = half // nz
    me, _, base, _ = sides(half)
    at = pl.multiple_of(base + me // CORES * part, part)
    chip = owner[pl.ds(at, part), :] // CORES
    for cols in tiles(ncols):
        former = got[0:part, cols]
        top = former
        for z in range(1, nz):
            top = jnp.where(chip == z, got[z * part : (z + 1) * part, cols], top)
        for z in range(nz):
            out[z * part : (z + 1) * part, cols] = jnp.where(chip == z, former, top)

    def put(rows, value):
        strip[rows, :] = value

    ordered(lax.rem(lax.axis_index("pcol"), YS) // 2, pieces, put)


def pair_kernel(owner, own, got, token, out):
    half, ncols = own.shape
    me, partner, base, _ = sides(half)
    who = half_of(owner, base, half)
    mine = (who == me) | (who == jnp.where(me == 0, partner, me))
    for cols in tiles(ncols):
        out[:, cols] = jnp.where(mine, own[:, cols], got[:, cols])


def local(kernel, name, params, shapes, *blocks):
    outs = tuple(jax.ShapeDtypeStruct(shape, jnp.float32) for shape in shapes)
    return pl.pallas_call(
        kernel,
        out_shape=outs,
        in_specs=vmem(len(blocks)),
        out_specs=tuple(vmem(len(outs))),
        compiler_params=params,
        cost_estimate=cost(0, 4 * sum(block.size for block in blocks)),
        name=name,
    )(*blocks)


def parts(value):
    high = value.astype(jnp.bfloat16)
    return high, (value - high.astype(jnp.float32)).astype(jnp.bfloat16)


def split_kernel(linv, *refs):
    strips, (left, right, token) = refs[:-3], refs[-3:]
    nb = linv.shape[1]

    def put(value, out, rows):
        high, low = parts(value)
        out[rows, 0:nb] = high
        out[rows, nb : 2 * nb] = low
        out[rows, 2 * nb : 3 * nb] = high

    put(linv[...], left, slice(None))
    ordered(lax.axis_index("pcol") // YS, strips, lambda rows, value: put(value, right, rows))
    token[...] = jnp.zeros_like(token)


def split(linv, strips):
    nb = linv.shape[1]
    nrows = sum(strip.shape[0] for strip in strips)
    return pl.pallas_call(
        split_kernel,
        out_shape=(
            jax.ShapeDtypeStruct((nb, 3 * nb), jnp.bfloat16),
            jax.ShapeDtypeStruct((nrows, 3 * nb), jnp.bfloat16),
            jax.ShapeDtypeStruct((8, LANES), jnp.float32),
        ),
        in_specs=vmem(1 + len(strips)),
        out_specs=tuple(vmem(3)),
        compiler_params=ROOMY,
        cost_estimate=cost(0, 10 * nb * (nb + nrows)),
        name="split",
    )(linv, *strips)


def ready_kernel(slots, rows, counts, owner, own, got, far, win, top, swapped):
    half, ncols = own.shape
    me, partner, base, other = sides(half)
    who = half_of(owner, base, half)
    for cols in tiles(ncols):
        theirs = jnp.where(who == partner, got[:, cols], far[:, cols])
        top[:, cols] = jnp.where(who == me, own[:, cols], theirs)
    swapped[...] = win[...]

    def put(source, side, start):
        def one(i):
            swapped[pl.ds(rows[side, i], 1), :] = source[pl.ds(start + slots[side, i], 1), :]

        each(counts[side], one)

    @pl.when(me == 0)
    def _():
        put(win, 0, base)
        put(win, 1, other)

    @pl.when(me == 1)
    def _():
        put(got, 0, 0)

    @pl.when(me > 1)
    def _():
        put(far, 0, 0)


def ready(table, owner, own, got, far, window):
    return pl.pallas_call(
        ready_kernel,
        out_shape=(
            jax.ShapeDtypeStruct(own.shape, own.dtype),
            jax.ShapeDtypeStruct(window.shape, window.dtype),
        ),
        in_specs=smem(3) + vmem(5),
        out_specs=tuple(vmem(2)),
        compiler_params=PARAMS,
        cost_estimate=cost(0, 8 * window.size + 16 * own.size),
        name="ready",
    )(*table, owner, own, got, far, window)


def final_kernel(slots, rows, counts, owner, left, right, swapped, top, give, got, out, full, rhs):
    half = top.shape[0]
    nb = 2 * half
    nrows, step = out.shape
    me, _, base, other = sides(half)
    base = pl.multiple_of(base, half)
    other = pl.multiple_of(other, half)
    at = pl.multiple_of(pl.program_id(0) * step, step)
    who = half_of(owner, other, half)
    full[pl.ds(base, half), :] = top[:, pl.ds(at, step)]
    for c in range(0, step, LANES):
        cols = pl.ds(pl.multiple_of(at + c, LANES), LANES)
        full[pl.ds(other, half), c : c + LANES] = jnp.where(who == me, give[:, cols], got[:, cols])

    def product(factor, value):
        high, low = parts(value)
        rhs[0:nb, :] = high
        rhs[nb : 2 * nb, :] = high
        rhs[2 * nb : 3 * nb, :] = low
        return jnp.dot(factor[...], rhs[...], preferred_element_type=jnp.float32)

    out[...] = swapped[:, pl.ds(at, step)]

    def put(i):
        out[pl.ds(rows[1, i], 1), :] = got[pl.ds(slots[1, i], 1), pl.ds(at, step)]

    each(jnp.where(me == 0, 0, counts[1]), put)
    solved = product(left, full[...])
    out[...] = out[...] - product(right, solved)

    @pl.when(me == 0)
    def _():
        out[0:nb, :] = solved


def final(table, owner, left, right, swapped, top, give, got):
    nrows, ncols = swapped.shape
    nb = 2 * top.shape[0]
    step = min(STEP, ncols)
    return pl.pallas_call(
        final_kernel,
        grid=(ncols // step,),
        out_shape=jax.ShapeDtypeStruct(swapped.shape, swapped.dtype),
        in_specs=smem(3) + vmem(7),
        out_specs=pl.BlockSpec((nrows, step), lambda c: (0, c)),
        scratch_shapes=[pltpu.VMEM((nb, step), jnp.float32), pltpu.VMEM((3 * nb, step), jnp.bfloat16)],
        compiler_params=PARAMS,
        cost_estimate=cost(6 * (nb + nrows) * nb * ncols, 8 * nrows * ncols),
        name="final",
    )(*table, owner, left, right, swapped, top, give, got)


def on_device(nprow, npcol, window, panel, linv, pivots):
    nrows, ncols = window.shape
    nbw = pivots.shape[0]
    nz = nprow // CORES
    columns = [[z * CORES + core for z in range(nz)] for core in range(CORES)]

    def swap(value):
        return lax.ppermute(value, "prow", [(p, p ^ 1) for p in range(nprow)])

    def exchange(value):
        return lax.all_to_all(value, "prow", 0, 0, axis_index_groups=columns, tiled=True)

    def ring(value, size, stride):
        span = size * stride
        pairs = lambda d: [(c, c // span * span + (c + d * stride) % span) for c in range(npcol)]
        return [value] + [lax.ppermute(value, "pcol", pairs(d)) for d in range(1, size)]

    owner = jnp.broadcast_to((pivots // nrows)[:, None], (nbw, LANES))
    count = panel.shape[0]

    own, give, table = pick(pivots, window)
    got = swap(give)
    beside = lax.ppermute(panel, "pcol", [(c, c ^ 1) for c in range(npcol)])
    chip, rows = local(deal_kernel, "deal", ROOMY, [own.shape, (2 * count, nbw)], owner, own, got, panel, beside)
    dealt = exchange(chip)
    kernel = functools.partial(home_kernel, nz)
    line = ring(rows, YS // 2, 2)
    chosen, strip = local(kernel, "home", ROOMY, [own.shape, (YS * count, nbw)], owner, dealt, *line)
    far = exchange(chosen)
    left, right, token = split(linv, ring(strip, npcol // YS, YS))
    (paired,) = local(pair_kernel, "pair", PARAMS, [own.shape], owner, own, far, token)
    last = swap(paired)
    top, swapped = ready(table, owner, own, got, far, window)
    return final(table, owner, left, right, swapped, top, give, last)


def solution(mesh):
    return jax.shard_map(
        functools.partial(on_device, mesh.shape["prow"], mesh.shape["pcol"]),
        mesh=mesh,
        in_specs=(P("prow", "pcol"), P(("prow", "pcol"), None), P(), P()),
        out_specs=P("prow", "pcol"),
        check_vma=False,
    )
```

time: 89.4 us -> 84 us (0.940)
  local copies, waits for them, and re-layouts: 9.78 us -> 4.04 us
  Pallas kernels: 14.2 us -> 16.2 us
    unnamed x48 -> x44, local copies, waits for them, and re-layouts: 9.69 us -> 3.21 us
    ppermute x2, waiting for transfers between devices: 1.7 us -> 0.01 us  [swap(): return lax.ppermute(value, 'prow', [(p, p ^ 1) for p in range(nprow)])]
    pallas_call x1, Pallas kernels: 0.66 us -> 2.25 us  [split(): pl.pallas_call(split_kernel, out_shape=(jax.ShapeDtypeStruct((nb, 3 * nb)...]
    ppermute x1, waiting for transfers between devices: 1.11 us -> 2.53 us  [on_device(): beside = lax.ppermute(panel, 'pcol', [(c, c ^ 1) for c in range(npcol)])]
    ppermute x1, starting transfers between devices: 3.27 us -> 1.92 us  [on_device(): beside = lax.ppermute(panel, 'pcol', [(c, c ^ 1) for c in range(npcol)])]
    pallas_call x4 -> x3, Pallas kernels: 3.19 us -> 4.34 us  [local(): pl.pallas_call(kernel, out_shape=outs, in_specs=vmem(len(blocks)), out_sp...]
  transfers between devices with their start and end apart: 11 -> 11, of which waited for: 6 -> 5; matrix products, arithmetic and copies ran while one was open for 0% -> 0% of each run, Pallas kernels for 3% -> 4%
where the time goes in v3:
time: 84 us; the launch traced here: 83.2 us
  starting transfers between devices  52.6 us (63%)
  Pallas kernels  16.2 us (19%)
  waiting for transfers between devices  10.2 us (12%)
  local copies, waits for them, and re-layouts  4.04 us (5%)
    ppermute x6, starting transfers between devices, ring(): lax.ppermute(value, 'pcol', pairs(d))  22.9 us
    ppermute x2, starting transfers between devices, swap(): return lax.ppermute(value, 'prow', [(p, p ^ 1) for p in range(nprow)])  16.5 us
    all_to_all x2, starting transfers between devices, exchange(): lax.all_to_all(value, 'prow', 0, 0, axis_index_groups=columns, tiled=True)  11.2 us
    ppermute x6, waiting for transfers between devices, ring(): lax.ppermute(value, 'pcol', pairs(d))  7.62 us
    pallas_call x1, Pallas kernels, final(): pl.pallas_call(final_kernel, grid=(ncols // step,), out_shape=jax.ShapeDt...  5.2 us
    pallas_call x3, Pallas kernels, local(): pl.pallas_call(kernel, out_shape=outs, in_specs=vmem(len(blocks)), out_sp...  4.34 us
    pallas_call x1, Pallas kernels, pick(): pl.pallas_call(pick_kernel, out_shape=(block, block, table, table, jax.Sh...  3.49 us
    unnamed x44, local copies, waits for them, and re-layouts  3.21 us
  transfers between devices with their start and end apart: 11, of which 5 were waited for; matrix products, arithmetic and copies ran while one was open for 0% of the time, Pallas kernels for 4%

profile of v3, /device:TPU:1, one launch (start us, length us, event | category | flops | bytes accessed | tf_op | source)
XLA Modules:
  0.0 83.2 jit_solution(3442528173883041496)
XLA Ops:
  0.0 3.5 %pick.1 = (f32[128,1024]{1,0:T(8,128)}, f32[128,1024]{1,0:T(8,128)}, s32[2,128]{1,0:T(2,128)}, s32[2,128]{1,0:T(2,128)}, s32[2]{0:T(128)}) custom-call(s32[256]{0:T(256)} %piv.1, f32[512,1024]{1,0:T(8,128)} %win.3), custom_call_target="tpu_custom_call" | custom-call | bytes 2097152 | tf_op jit(solution)/shard_map/pick/pallas_call | solution.py:84
  3.5 9.3 %collective-permute-start = (f32[128,1024]{1,0:T(8,128)}, f32[128,1024]{1,0:T(8,128)S(1)}, u32[]{:S(2)}, u32[]{:S(2)}) collective-permute-start(f32[128,1024]{1,0:T(8,128)} %get-tuple-element.23.give), channel_id=1, source_target_pairs={{0,32},{32,0},{64,96},{96,64},{128,160},{160,128},{192,224},{224,1... | collective-permute-start | bytes 1572872 | tf_op jit(solution)/shard_map/ppermute | solution.py:305
  12.8 0.0 copy-done.19
  12.8 1.9 %collective-permute-start.1 = (f32[16,256]{1,0:T(8,128)S(1)}, f32[16,256]{1,0:T(8,128)S(1)}, u32[]{:S(2)}, u32[]{:S(2)}) collective-permute-start(f32[16,256]{1,0:T(8,128)S(1)} %copy-done.19), channel_id=1, source_target_pairs={{0,1},{1,0},{2,3},{3,2},{4,5},{5,4},{6,7},{7,6},{8,9},{9,8},{10,11... | collective-permute-start | bytes 49160 | tf_op jit(solution)/shard_map/ppermute | solution.py:320
  14.8 0.0 copy-done.21
  14.8 2.5 %collective-permute-done.1.beside = f32[16,256]{1,0:T(8,128)S(1)} collective-permute-done((f32[16,256]{1,0:T(8,128)S(1)}, f32[16,256]{1,0:T(8,128)S(1)}, u32[]{:S(2)}, u32[]{:S(2)}) %collective-permute-start.1) | collective-permute-done | bytes 16416 | tf_op jit(solution)/shard_map/ppermute | solution.py:320
  17.3 0.0 collective-permute-done.got
  17.3 0.8 broadcast_in_dim.2.owner
  18.2 0.0 copy-done.20
  18.2 0.0 copy-done.3
  18.2 2.1 %deal.1 = (f32[128,1024]{1,0:T(8,128)}, f32[32,256]{1,0:T(8,128)}) custom-call(s32[256,128]{1,0:T(8,128)} %broadcast_in_dim.2.owner, f32[128,1024]{1,0:T(8,128)} %get-tuple-element.22.own, f32[128,1024]{1,0:T(8,128)} %copy-done.3, f32[16,256]{1,0:T(8,128)} %panel.1, f32[16,256]{1,0:T(8,128)} %copy-done.20), custom_call_target="tpu_custom_call" | custom-call | bytes 1212416 | tf_op jit(solution)/shard_map/deal/pallas_call | solution.py:153
  20.3 4.6 %all-to-all-start = ((f32[8,16,1024]{2,1,0:T(8,128)}), f32[8,16,1024]{2,1,0:T(8,128)S(1)}, u32[]{:S(2)}, u32[]{:S(2)}) async-start(f32[8,16,1024]{2,1,0:T(8,128)} %bitcast.8), calls=%async_computation | async-start | bytes 1048576 | tf_op jit(solution)/shard_map/all_to_all | solution.py:308
  24.9 5.9 %collective-permute-start.4 = (f32[32,256]{1,0:T(8,128)}, f32[32,256]{1,0:T(8,128)S(1)}, u32[]{:S(2)}, u32[]{:S(2)}) collective-permute-start(f32[32,256]{1,0:T(8,128)} %get-tuple-element.25.refs_0_), channel_id=1, source_target_pairs={{0,6},{1,7},{2,0},{3,1},{4,2},{5,3},{6,4},{7,5},{8,14},{9,15},{10,... | collective-permute-start | bytes 98312 | tf_op jit(solution)/shard_map/ppermute | solution.py:313
  30.7 3.5 %collective-permute-start.3 = (f32[32,256]{1,0:T(8,128)}, f32[32,256]{1,0:T(8,128)S(1)}, u32[]{:S(2)}, u32[]{:S(2)}) collective-permute-start(f32[32,256]{1,0:T(8,128)} %get-tuple-element.25.refs_0_), channel_id=1, source_target_pairs={{0,4},{1,5},{2,6},{3,7},{4,0},{5,1},{6,2},{7,3},{8,12},{9,13},{10,... | collective-permute-start | bytes 98312 | tf_op jit(solution)/shard_map/ppermute | solution.py:313
  34.3 4.2 %collective-permute-start.2 = (f32[32,256]{1,0:T(8,128)}, f32[32,256]{1,0:T(8,128)S(1)}, u32[]{:S(2)}, u32[]{:S(2)}) collective-permute-start(f32[32,256]{1,0:T(8,128)} %get-tuple-element.25.refs_0_), channel_id=1, source_target_pairs={{0,2},{1,3},{2,4},{3,5},{4,6},{5,7},{6,0},{7,1},{8,10},{9,11},{10,... | collective-permute-start | bytes 98312 | tf_op jit(solution)/shard_map/ppermute | solution.py:313
  38.5 0.0 collective-permute-done.4.refs_3_
  38.5 0.0 copy-start.16
  38.5 1.0 %collective-permute-done.3.refs_2_ = f32[32,256]{1,0:T(8,128)S(1)} collective-permute-done((f32[32,256]{1,0:T(8,128)}, f32[32,256]{1,0:T(8,128)S(1)}, u32[]{:S(2)}, u32[]{:S(2)}) %collective-permute-start.3) | collective-permute-done | bytes 32800 | tf_op jit(solution)/shard_map/ppermute | solution.py:313
  39.5 2.0 %collective-permute-done.2.refs_1_ = f32[32,256]{1,0:T(8,128)S(1)} collective-permute-done((f32[32,256]{1,0:T(8,128)}, f32[32,256]{1,0:T(8,128)S(1)}, u32[]{:S(2)}, u32[]{:S(2)}) %collective-permute-start.2) | collective-permute-done | bytes 32800 | tf_op jit(solution)/shard_map/ppermute | solution.py:313
  41.6 0.0 all-to-all-done
  41.6 0.0 copy-done.16
  41.6 0.0 copy-done.17
  41.6 0.6 copy-done.18
  42.2 0.2 copy-done.12
  42.4 2.1 %home.1 = (f32[128,1024]{1,0:T(8,128)}, f32[128,256]{1,0:T(8,128)}) custom-call(s32[256,128]{1,0:T(8,128)} %broadcast_in_dim.2.owner, f32[128,1024]{1,0:T(8,128)} %bitcast.6, f32[32,256]{1,0:T(8,128)} %get-tuple-element.25.refs_0_, f32[32,256]{1,0:T(8,128)} %copy-done.18, f32[32,256]{1,0:T(8,128)} %copy-done.17, f32[32,256]{1,0:T(8,128)} %copy-done.16), custom_call_target="tpu_custom_call" | custom-call | bytes 786432 | tf_op jit(solution)/shard_map/home/pallas_call | solution.py:153
  44.5 6.6 %all-to-all-start.1 = ((f32[8,16,1024]{2,1,0:T(8,128)}), f32[8,16,1024]{2,1,0:T(8,128)S(1)}, u32[]{:S(2)}, u32[]{:S(2)}) async-start(f32[8,16,1024]{2,1,0:T(8,128)} %bitcast.7), calls=%async_computation.1 | async-start | bytes 1048576 | tf_op jit(solution)/shard_map/all_to_all | solution.py:308
  51.1 4.4 %collective-permute-start.7 = (f32[128,256]{1,0:T(8,128)}, f32[128,256]{1,0:T(8,128)S(1)}, u32[]{:S(2)}, u32[]{:S(2)}) collective-permute-start(f32[128,256]{1,0:T(8,128)} %get-tuple-element.26.refs_0_), channel_id=1, source_target_pairs={{0,24},{1,25},{2,26},{3,27},{4,28},{5,29},{6,30},{7,31},{8,0},{9,1... | collective-permute-start | bytes 393224 | tf_op jit(solution)/shard_map/ppermute | solution.py:313
  55.5 2.4 %collective-permute-start.6 = (f32[128,256]{1,0:T(8,128)}, f32[128,256]{1,0:T(8,128)S(1)}, u32[]{:S(2)}, u32[]{:S(2)}) collective-permute-start(f32[128,256]{1,0:T(8,128)} %get-tuple-element.26.refs_0_), channel_id=1, source_target_pairs={{0,16},{1,17},{2,18},{3,19},{4,20},{5,21},{6,22},{7,23},{8,24},{9,... | collective-permute-start | bytes 393224 | tf_op jit(solution)/shard_map/ppermute | solution.py:313
  58.0 2.5 %collective-permute-start.5 = (f32[128,256]{1,0:T(8,128)}, f32[128,256]{1,0:T(8,128)S(1)}, u32[]{:S(2)}, u32[]{:S(2)}) collective-permute-start(f32[128,256]{1,0:T(8,128)} %get-tuple-element.26.refs_0_), channel_id=1, source_target_pairs={{0,8},{1,9},{2,10},{3,11},{4,12},{5,13},{6,14},{7,15},{8,16},{9,17... | collective-permute-start | bytes 393224 | tf_op jit(solution)/shard_map/ppermute | solution.py:313
  60.5 0.0 collective-permute-done.7.refs_3_
  60.5 0.0 copy-start.13
  60.5 2.7 %collective-permute-done.6.refs_2_ = f32[128,256]{1,0:T(8,128)S(1)} collective-permute-done((f32[128,256]{1,0:T(8,128)}, f32[128,256]{1,0:T(8,128)S(1)}, u32[]{:S(2)}, u32[]{:S(2)}) %collective-permute-start.6) | collective-permute-done | bytes 131104 | tf_op jit(solution)/shard_map/ppermute | solution.py:313
  63.3 1.8 %collective-permute-done.5.refs_1_ = f32[128,256]{1,0:T(8,128)S(1)} collective-permute-done((f32[128,256]{1,0:T(8,128)}, f32[128,256]{1,0:T(8,128)S(1)}, u32[]{:S(2)}, u32[]{:S(2)}) %collective-permute-start.5) | collective-permute-done | bytes 131104 | tf_op jit(solution)/shard_map/ppermute | solution.py:313
  65.1 0.0 copy-done.13
  65.1 0.0 copy-done.14
  65.1 0.7 copy-done.15
  65.8 2.3 %split.1 = (bf16[256,768]{1,0:T(8,128)(2,1)}, bf16[512,768]{1,0:T(8,128)(2,1)}, f32[8,128]{1,0:T(8,128)}) custom-call(f32[256,256]{1,0:T(8,128)} %linv.1, f32[128,256]{1,0:T(8,128)} %get-tuple-element.26.refs_0_, f32[128,256]{1,0:T(8,128)} %copy-done.15, f32[128,256]{1,0:T(8,128)} %copy-done.14, f32[128,256]{1,0:T(8,128)} %copy-done.13), custom_call_target="tpu_custom_call" | custom-call | bytes 1966080 | tf_op jit(solution)/shard_map/split/pallas_call | solution.py:187
  68.0 0.0 all-to-all-done.1
  68.0 0.0 copy-done.1
  68.0 0.0 copy-done.2
  68.0 0.0 copy-start.8
  68.0 0.7 copy-done.8
  68.7 0.1 pair.1
  68.8 7.2 %collective-permute-start.8 = (f32[128,1024]{1,0:T(8,128)S(1)}, f32[128,1024]{1,0:T(8,128)S(1)}, u32[]{:S(2)}, u32[]{:S(2)}) collective-permute-start(f32[128,1024]{1,0:T(8,128)S(1)} %pair.1), channel_id=1, source_target_pairs={{0,32},{32,0},{64,96},{96,64},{128,160},{160,128},{192,224},{224,1... | collective-permute-start | bytes 1572872 | tf_op jit(solution)/shard_map/ppermute | solution.py:305
  76.1 1.0 %copy-done.4 = f32[128,1024]{1,0:T(8,128)S(1)} copy-done((f32[128,1024]{1,0:T(8,128)S(1)}, f32[128,1024]{1,0:T(8,128)}, u32[]{:S(2)}) %copy-start.4) | copy-done | bytes 524312
  77.1 0.9 %ready.1 = (f32[128,1024]{1,0:T(8,128)S(1)}, f32[512,1024]{1,0:T(8,128)S(1)}) custom-call(s32[2,128]{1,0:T(2,128)S(1)} %copy-done.9, s32[2,128]{1,0:T(2,128)S(1)} %copy-done.10, s32[2]{0:T(128)S(1)} %copy-done.11, s32[256,128]{1,0:T(8,128)S(1)} %copy-done.2, f32[128,1024]{1,0:T(8,128)S(1)} %copy-done.1, f32[128,1024]{1,0:T(8,128)S(1)} %copy-done.4, ...), custom_call_target="tpu_custom_call" | custom-call | bytes 6291456 | tf_op jit(solution)/shard_map/ready/pallas_call | solution.py:232
  78.0 0.0 collective-permute-done.8.got
  78.0 5.2 %final.1 = f32[512,1024]{1,0:T(8,128)} custom-call(s32[2,128]{1,0:T(2,128)S(1)} %copy-done.9, s32[2,128]{1,0:T(2,128)S(1)} %copy-done.10, s32[2]{0:T(128)S(1)} %copy-done.11, s32[256,128]{1,0:T(8,128)S(1)} %copy-done.2, bf16[256,768]{1,0:T(8,128)(2,1)S(1)} %copy-done.7, bf16[512,768]{1,0:T(8,128)(2,1)S(1)} %copy-done.5, ...), custom_call_target="tpu_custom_call" | custom-call | flops 1207959552 | bytes 4194304 | tf_op jit(solution)/shard_map/final/pallas_call | solution.py:285
  (27 shorter events, 0.1 us)
Async XLA Ops:
  0.0 14.8 %copy-start.21 = (s32[256]{0:T(256)S(1)}, s32[256]{0:T(256)}, u32[]{:S(2)}) copy-start(s32[256]{0:T(256)} %piv.1) | copy-start | bytes 3076
  0.0 12.8 %copy-start.19 = (f32[16,256]{1,0:T(8,128)S(1)}, f32[16,256]{1,0:T(8,128)}, u32[]{:S(2)}) copy-start(f32[16,256]{1,0:T(8,128)} %panel.1) | copy-start | bytes 49156
  3.5 13.8 %collective-permute-start = (f32[128,1024]{1,0:T(8,128)}, f32[128,1024]{1,0:T(8,128)S(1)}, u32[]{:S(2)}, u32[]{:S(2)}) collective-permute-start(f32[128,1024]{1,0:T(8,128)} %get-tuple-element.23.give), channel_id=1, source_target_pairs={{0,32},{32,0},{64,96},{96,64},{128,160},{160,128},{192,224},{224,1... | collective-permute-start | bytes 1572872 | tf_op jit(solution)/shard_map/ppermute | solution.py:305
  12.8 4.5 %collective-permute-start.1 = (f32[16,256]{1,0:T(8,128)S(1)}, f32[16,256]{1,0:T(8,128)S(1)}, u32[]{:S(2)}, u32[]{:S(2)}) collective-permute-start(f32[16,256]{1,0:T(8,128)S(1)} %copy-done.19), channel_id=1, source_target_pairs={{0,1},{1,0},{2,3},{3,2},{4,5},{5,4},{6,7},{7,6},{8,9},{9,8},{10,11... | collective-permute-start | bytes 49160 | tf_op jit(solution)/shard_map/ppermute | solution.py:320
  17.3 0.8 %copy-start.20 = (f32[16,256]{1,0:T(8,128)}, f32[16,256]{1,0:T(8,128)S(1)}, u32[]{:S(2)}) copy-start(f32[16,256]{1,0:T(8,128)S(1)} %collective-permute-done.1.beside) | copy-start | bytes 49156
  17.3 0.8 copy-start.3
  20.3 47.7 %copy-start.1 = (f32[128,1024]{1,0:T(8,128)S(1)}, f32[128,1024]{1,0:T(8,128)}, u32[]{:S(2)}) copy-start(f32[128,1024]{1,0:T(8,128)} %get-tuple-element.22.own) | copy-start | bytes 1572868
  20.3 47.7 %copy-start.2 = (s32[256,128]{1,0:T(8,128)S(1)}, s32[256,128]{1,0:T(8,128)}, u32[]{:S(2)}) copy-start(s32[256,128]{1,0:T(8,128)} %broadcast_in_dim.2.owner) | copy-start | bytes 393220
  20.3 21.3 %all-to-all-start = ((f32[8,16,1024]{2,1,0:T(8,128)}), f32[8,16,1024]{2,1,0:T(8,128)S(1)}, u32[]{:S(2)}, u32[]{:S(2)}) async-start(f32[8,16,1024]{2,1,0:T(8,128)} %bitcast.8), calls=%async_computation | async-start | bytes 1048576 | tf_op jit(solution)/shard_map/all_to_all | solution.py:308
  24.9 13.6 %collective-permute-start.4 = (f32[32,256]{1,0:T(8,128)}, f32[32,256]{1,0:T(8,128)S(1)}, u32[]{:S(2)}, u32[]{:S(2)}) collective-permute-start(f32[32,256]{1,0:T(8,128)} %get-tuple-element.25.refs_0_), channel_id=1, source_target_pairs={{0,6},{1,7},{2,0},{3,1},{4,2},{5,3},{6,4},{7,5},{8,14},{9,15},{10,... | collective-permute-start | bytes 98312 | tf_op jit(solution)/shard_map/ppermute | solution.py:313
  30.7 8.8 %collective-permute-start.3 = (f32[32,256]{1,0:T(8,128)}, f32[32,256]{1,0:T(8,128)S(1)}, u32[]{:S(2)}, u32[]{:S(2)}) collective-permute-start(f32[32,256]{1,0:T(8,128)} %get-tuple-element.25.refs_0_), channel_id=1, source_target_pairs={{0,4},{1,5},{2,6},{3,7},{4,0},{5,1},{6,2},{7,3},{8,12},{9,13},{10,... | collective-permute-start | bytes 98312 | tf_op jit(solution)/shard_map/ppermute | solution.py:313
  34.3 7.3 %collective-permute-start.2 = (f32[32,256]{1,0:T(8,128)}, f32[32,256]{1,0:T(8,128)S(1)}, u32[]{:S(2)}, u32[]{:S(2)}) collective-permute-start(f32[32,256]{1,0:T(8,128)} %get-tuple-element.25.refs_0_), channel_id=1, source_target_pairs={{0,2},{1,3},{2,4},{3,5},{4,6},{5,7},{6,0},{7,1},{8,10},{9,11},{10,... | collective-permute-start | bytes 98312 | tf_op jit(solution)/shard_map/ppermute | solution.py:313
  38.5 3.0 %copy-start.16 = (f32[32,256]{1,0:T(8,128)}, f32[32,256]{1,0:T(8,128)S(1)}, u32[]{:S(2)}) copy-start(f32[32,256]{1,0:T(8,128)S(1)} %collective-permute-done.4.refs_3_) | copy-start | bytes 98308
  39.5 2.1 %copy-start.17 = (f32[32,256]{1,0:T(8,128)}, f32[32,256]{1,0:T(8,128)S(1)}, u32[]{:S(2)}) copy-start(f32[32,256]{1,0:T(8,128)S(1)} %collective-permute-done.3.refs_2_) | copy-start | bytes 98308
  41.6 0.6 copy-start.18
  41.6 0.8 copy-start.12
  42.4 33.6 %copy-start = (f32[512,1024]{1,0:T(8,128)S(1)}, f32[512,1024]{1,0:T(8,128)}, u32[]{:S(2)}) copy-start(f32[512,1024]{1,0:T(8,128)} %win.3) | copy-start | bytes 6291460
  42.4 33.7 %copy-start.9 = (s32[2,128]{1,0:T(2,128)S(1)}, s32[2,128]{1,0:T(2,128)}, u32[]{:S(2)}) copy-start(s32[2,128]{1,0:T(2,128)} %get-tuple-element.19.slots) | copy-start | bytes 3076
  42.4 33.7 %copy-start.10 = (s32[2,128]{1,0:T(2,128)S(1)}, s32[2,128]{1,0:T(2,128)}, u32[]{:S(2)}) copy-start(s32[2,128]{1,0:T(2,128)} %get-tuple-element.20.rows) | copy-start | bytes 3076
  42.4 33.7 %copy-start.11 = (s32[2]{0:T(128)S(1)}, s32[2]{0:T(128)}, u32[]{:S(2)}) copy-start(s32[2]{0:T(128)} %get-tuple-element.21.counts) | copy-start | bytes 28
  44.5 23.5 %all-to-all-start.1 = ((f32[8,16,1024]{2,1,0:T(8,128)}), f32[8,16,1024]{2,1,0:T(8,128)S(1)}, u32[]{:S(2)}, u32[]{:S(2)}) async-start(f32[8,16,1024]{2,1,0:T(8,128)} %bitcast.7), calls=%async_computation.1 | async-start | bytes 1048576 | tf_op jit(solution)/shard_map/all_to_all | solution.py:308
  51.1 9.3 %collective-permute-start.7 = (f32[128,256]{1,0:T(8,128)}, f32[128,256]{1,0:T(8,128)S(1)}, u32[]{:S(2)}, u32[]{:S(2)}) collective-permute-start(f32[128,256]{1,0:T(8,128)} %get-tuple-element.26.refs_0_), channel_id=1, source_target_pairs={{0,24},{1,25},{2,26},{3,27},{4,28},{5,29},{6,30},{7,31},{8,0},{9,1... | collective-permute-start | bytes 393224 | tf_op jit(solution)/shard_map/ppermute | solution.py:313
  55.5 7.7 %collective-permute-start.6 = (f32[128,256]{1,0:T(8,128)}, f32[128,256]{1,0:T(8,128)S(1)}, u32[]{:S(2)}, u32[]{:S(2)}) collective-permute-start(f32[128,256]{1,0:T(8,128)} %get-tuple-element.26.refs_0_), channel_id=1, source_target_pairs={{0,16},{1,17},{2,18},{3,19},{4,20},{5,21},{6,22},{7,23},{8,24},{9,... | collective-permute-start | bytes 393224 | tf_op jit(solution)/shard_map/ppermute | solution.py:313
  58.0 7.1 %collective-permute-start.5 = (f32[128,256]{1,0:T(8,128)}, f32[128,256]{1,0:T(8,128)S(1)}, u32[]{:S(2)}, u32[]{:S(2)}) collective-permute-start(f32[128,256]{1,0:T(8,128)} %get-tuple-element.26.refs_0_), channel_id=1, source_target_pairs={{0,8},{1,9},{2,10},{3,11},{4,12},{5,13},{6,14},{7,15},{8,16},{9,17... | collective-permute-start | bytes 393224 | tf_op jit(solution)/shard_map/ppermute | solution.py:313
  60.5 4.6 %copy-start.13 = (f32[128,256]{1,0:T(8,128)}, f32[128,256]{1,0:T(8,128)S(1)}, u32[]{:S(2)}) copy-start(f32[128,256]{1,0:T(8,128)S(1)} %collective-permute-done.7.refs_3_) | copy-start | bytes 393220
  63.2 1.9 %copy-start.14 = (f32[128,256]{1,0:T(8,128)}, f32[128,256]{1,0:T(8,128)S(1)}, u32[]{:S(2)}) copy-start(f32[128,256]{1,0:T(8,128)S(1)} %collective-permute-done.6.refs_2_) | copy-start | bytes 393220
  65.1 0.7 copy-start.15
  68.0 0.7 copy-start.8
  68.7 9.3 %copy-start.5 = (bf16[512,768]{1,0:T(8,128)(2,1)S(1)}, bf16[512,768]{1,0:T(8,128)(2,1)}, u32[]{:S(2)}) copy-start(bf16[512,768]{1,0:T(8,128)(2,1)} %get-tuple-element.28.right) | copy-start | bytes 2359300
  68.7 9.3 %copy-start.6 = (f32[128,1024]{1,0:T(8,128)S(1)}, f32[128,1024]{1,0:T(8,128)}, u32[]{:S(2)}) copy-start(f32[128,1024]{1,0:T(8,128)} %get-tuple-element.23.give) | copy-start | bytes 1572868
  68.7 9.3 %copy-start.7 = (bf16[256,768]{1,0:T(8,128)(2,1)S(1)}, bf16[256,768]{1,0:T(8,128)(2,1)}, u32[]{:S(2)}) copy-start(bf16[256,768]{1,0:T(8,128)(2,1)} %get-tuple-element.27.left) | copy-start | bytes 1179652
  68.8 9.2 %collective-permute-start.8 = (f32[128,1024]{1,0:T(8,128)S(1)}, f32[128,1024]{1,0:T(8,128)S(1)}, u32[]{:S(2)}, u32[]{:S(2)}) collective-permute-start(f32[128,1024]{1,0:T(8,128)S(1)} %pair.1), channel_id=1, source_target_pairs={{0,32},{32,0},{64,96},{96,64},{128,160},{160,128},{192,224},{224,1... | collective-permute-start | bytes 1572872 | tf_op jit(solution)/shard_map/ppermute | solution.py:305
  76.0 1.0 %copy-start.4 = (f32[128,1024]{1,0:T(8,128)S(1)}, f32[128,1024]{1,0:T(8,128)}, u32[]{:S(2)}) copy-start(f32[128,1024]{1,0:T(8,128)} %copy-done.3) | copy-start | bytes 1572868

commit v4 on v3

--- a/solution.py
+++ b/solution.py
@@ -8,7 +8,6 @@
 from jax.sharding import PartitionSpec as P
 
 CORES = 2
-YS = 8
 LANES = 128
 STEP = 256
 PARAMS = pltpu.CompilerParams(vmem_limit_bytes=32 * 1024 * 1024)
@@ -46,13 +45,16 @@
     lax.fori_loop(0, (count + 3) // 4, four, 0)
 
 
-def pick_kernel(piv, win, own, give, slots, rows, counts, held, sem):
+def pick_kernel(piv, win, panel, own, give, spread, slots, rows, counts, held, sem):
     nrows = win.shape[0]
     half = own.shape[0]
     me, _, base, other = sides(half)
     first = me * nrows
     load = pltpu.make_async_copy(win, held, sem)
     load.start()
+    count = panel.shape[0]
+    spread[...] = jnp.zeros_like(spread)
+    spread[pl.ds(pl.multiple_of(lax.axis_index("pcol") * count, count), count), :] = panel[...]
 
     def step(i, totals):
         new = []
@@ -76,50 +78,39 @@
         each(totals[side], put)
 
 
-def pick(pivots, window):
+def pick(pivots, window, panel):
     half = pivots.shape[0] // CORES
     ncols = window.shape[1]
     block = jax.ShapeDtypeStruct((half, ncols), window.dtype)
     table = jax.ShapeDtypeStruct((CORES, half), jnp.int32)
+    spread = jax.ShapeDtypeStruct((window.shape[0], panel.shape[1]), panel.dtype)
     out = pl.pallas_call(
         pick_kernel,
-        out_shape=(block, block, table, table, jax.ShapeDtypeStruct((CORES,), jnp.int32)),
-        in_specs=smem(1) + [pl.BlockSpec(memory_space=pl.ANY)],
-        out_specs=tuple(vmem(2) + smem(3)),
+        out_shape=(block, block, spread, table, table, jax.ShapeDtypeStruct((CORES,), jnp.int32)),
+        in_specs=smem(1) + [pl.BlockSpec(memory_space=pl.ANY)] + vmem(1),
+        out_specs=tuple(vmem(3) + smem(3)),
         scratch_shapes=[pltpu.VMEM(window.shape, window.dtype), pltpu.SemaphoreType.DMA],
         compiler_params=ROOMY,
         cost_estimate=cost(0, 16 * half * ncols),
         name="pick",
-    )(pivots, window)
-    return out[0], out[1], out[2:]
+    )(pivots, window, panel)
+    return out[0], out[1], out[2], out[3:]
 
 
 def half_of(owner, base, half):
     return owner[pl.ds(pl.multiple_of(base, half), half), :]
 
 
-def deal_kernel(owner, own, got, panel, beside, out, rows):
+def deal_kernel(owner, own, got, out):
     half, ncols = own.shape
     me, partner, base, _ = sides(half)
     who = half_of(owner, base, half)
     theirs = (who == partner) | ((who != me) & (who != jnp.where(me == 0, who, -1)))
     for cols in tiles(ncols):
         out[:, cols] = jnp.where(theirs, got[:, cols], own[:, cols])
-    count = panel.shape[0]
-    odd = lax.rem(lax.axis_index("pcol"), 2)
-    rows[pl.ds(pl.multiple_of(odd * count, count), count), :] = panel[...]
-    rows[pl.ds(pl.multiple_of((1 - odd) * count, count), count), :] = beside[...]
-
-
-def ordered(index, pieces, put):
-    count = pieces[0].shape[0]
-    for d, piece in enumerate(pieces):
-        source = lax.rem(index - d + len(pieces), len(pieces))
-        put(pl.ds(pl.multiple_of(source * count, count), count), piece[...])
-
-
-def home_kernel(nz, owner, got, *refs):
-    pieces, (out, strip) = refs[:-2], refs[-2:]
+
+
+def home_kernel(nz, owner, got, out):
     half, ncols = got.shape
     part = half // nz
     me, _, base, _ = sides(half)
@@ -133,13 +124,8 @@
         for z in range(nz):
             out[z * part : (z + 1) * part, cols] = jnp.where(chip == z, former, top)
 
-    def put(rows, value):
-        strip[rows, :] = value
-
-    ordered(lax.rem(lax.axis_index("pcol"), YS) // 2, pieces, put)
-
-
-def pair_kernel(owner, own, got, token, out):
+
+def pair_kernel(owner, own, got, out):
     half, ncols = own.shape
     me, partner, base, _ = sides(half)
     who = half_of(owner, base, half)
@@ -166,37 +152,26 @@
     return high, (value - high.astype(jnp.float32)).astype(jnp.bfloat16)
 
 
-def split_kernel(linv, *refs):
-    strips, (left, right, token) = refs[:-3], refs[-3:]
-    nb = linv.shape[1]
-
-    def put(value, out, rows):
-        high, low = parts(value)
-        out[rows, 0:nb] = high
-        out[rows, nb : 2 * nb] = low
-        out[rows, 2 * nb : 3 * nb] = high
-
-    put(linv[...], left, slice(None))
-    ordered(lax.axis_index("pcol") // YS, strips, lambda rows, value: put(value, right, rows))
-    token[...] = jnp.zeros_like(token)
-
-
-def split(linv, strips):
-    nb = linv.shape[1]
-    nrows = sum(strip.shape[0] for strip in strips)
+def split_kernel(linv, panel, left, right):
+    for source, out in ((linv, left), (panel, right)):
+        nb = source.shape[1]
+        high, low = parts(source[...])
+        out[:, 0:nb] = high
+        out[:, nb : 2 * nb] = low
+        out[:, 2 * nb : 3 * nb] = high
+
+
+def split(linv, panel):
+    shapes = [jax.ShapeDtypeStruct((a.shape[0], 3 * a.shape[1]), jnp.bfloat16) for a in (linv, panel)]
     return pl.pallas_call(
         split_kernel,
-        out_shape=(
-            jax.ShapeDtypeStruct((nb, 3 * nb), jnp.bfloat16),
-            jax.ShapeDtypeStruct((nrows, 3 * nb), jnp.bfloat16),
-            jax.ShapeDtypeStruct((8, LANES), jnp.float32),
-        ),
-        in_specs=vmem(1 + len(strips)),
-        out_specs=tuple(vmem(3)),
-        compiler_params=ROOMY,
-        cost_estimate=cost(0, 10 * nb * (nb + nrows)),
+        out_shape=tuple(shapes),
+        in_specs=vmem(2),
+        out_specs=tuple(vmem(2)),
+        compiler_params=PARAMS,
+        cost_estimate=cost(0, 10 * (linv.size + panel.size)),
         name="split",
-    )(linv, *strips)
+    )(linv, panel)
 
 
 def ready_kernel(slots, rows, counts, owner, own, got, far, win, top, swapped):
@@ -295,7 +270,7 @@
     )(*table, owner, left, right, swapped, top, give, got)
 
 
-def on_device(nprow, npcol, window, panel, linv, pivots):
+def on_device(nprow, window, panel, linv, pivots):
     nrows, ncols = window.shape
     nbw = pivots.shape[0]
     nz = nprow // CORES
@@ -307,33 +282,25 @@
     def exchange(value):
         return lax.all_to_all(value, "prow", 0, 0, axis_index_groups=columns, tiled=True)
 
-    def ring(value, size, stride):
-        span = size * stride
-        pairs = lambda d: [(c, c // span * span + (c + d * stride) % span) for c in range(npcol)]
-        return [value] + [lax.ppermute(value, "pcol", pairs(d)) for d in range(1, size)]
-
     owner = jnp.broadcast_to((pivots // nrows)[:, None], (nbw, LANES))
-    count = panel.shape[0]
-
-    own, give, table = pick(pivots, window)
+
+    own, give, spread, table = pick(pivots, window, panel)
+    whole = lax.psum(spread, "pcol")
     got = swap(give)
-    beside = lax.ppermute(panel, "pcol", [(c, c ^ 1) for c in range(npcol)])
-    chip, rows = local(deal_kernel, "deal", ROOMY, [own.shape, (2 * count, nbw)], owner, own, got, panel, beside)
+    (chip,) = local(deal_kernel, "deal", PARAMS, [own.shape], owner, own, got)
     dealt = exchange(chip)
-    kernel = functools.partial(home_kernel, nz)
-    line = ring(rows, YS // 2, 2)
-    chosen, strip = local(kernel, "home", ROOMY, [own.shape, (YS * count, nbw)], owner, dealt, *line)
+    (chosen,) = local(functools.partial(home_kernel, nz), "home", PARAMS, [own.shape], owner, dealt)
     far = exchange(chosen)
-    left, right, token = split(linv, ring(strip, npcol // YS, YS))
-    (paired,) = local(pair_kernel, "pair", PARAMS, [own.shape], owner, own, far, token)
+    (paired,) = local(pair_kernel, "pair", PARAMS, [own.shape], owner, own, far)
     last = swap(paired)
+    left, right = split(linv, whole)
     top, swapped = ready(table, owner, own, got, far, window)
     return final(table, owner, left, right, swapped, top, give, last)
 
 
 def solution(mesh):
     return jax.shard_map(
-        functools.partial(on_device, mesh.shape["prow"], mesh.shape["pcol"]),
+        functools.partial(on_device, mesh.shape["prow"]),
         mesh=mesh,
         in_specs=(P("prow", "pcol"), P(("prow", "pcol"), None), P(), P()),
         out_specs=P("prow", "pcol"),

time: 84 us -> 228 us (2.71)
  waiting for transfers between devices: 10.2 us -> 157 us
  starting transfers between devices: 52.6 us -> 16.7 us
  blocking collectives: 0 us -> 21.3 us
  between operations: 0.27 us -> 13.6 us
  Pallas kernels: 16.2 us -> 13 us
    psum x0 -> x1, waiting for transfers between devices: none -> 139 us  [on_device(): whole = lax.psum(spread, 'pcol')]
    ppermute x7 -> x0, starting transfers between devices: 24.9 us -> none  [the longest x6 22.9 us: ring(): lax.ppermute(value, 'pcol', pairs(d))]
    all_to_all x0 -> x1, blocking collectives: none -> 21.3 us  [exchange(): lax.all_to_all(value, 'prow', 0, 0, axis_index_groups=columns, tiled=True)]
    all_to_all x2 -> x1, waiting for transfers between devices: 0.01 us -> 15.1 us  [exchange(): lax.all_to_all(value, 'prow', 0, 0, axis_index_groups=columns, tiled=True)]
    ppermute x7 -> x0, waiting for transfers between devices: 10.1 us -> none  [the longest x6 7.62 us: ring(): lax.ppermute(value, 'pcol', pairs(d))]
    all_to_all x2 -> x1, starting transfers between devices: 11.2 us -> 3.64 us  [exchange(): lax.all_to_all(value, 'prow', 0, 0, axis_index_groups=columns, tiled=True)]
    ppermute x2, starting transfers between devices: 16.5 us -> 13 us  [swap(): return lax.ppermute(value, 'prow', [(p, p ^ 1) for p in range(nprow)])]
    pallas_call x3, Pallas kernels: 4.34 us -> 1.01 us  [local(): pl.pallas_call(kernel, out_shape=outs, in_specs=vmem(len(blocks)), out_sp...]
  transfers between devices with their start and end apart: 11 -> 4, of which waited for: 5 -> 3; matrix products, arithmetic and copies ran while one was open for 0% -> 0% of each run, Pallas kernels for 4% -> 1%
where the time goes in v4:
time: 228 us; the launch traced here: 226 us
  waiting for transfers between devices  157 us (69%)
  blocking collectives  21.3 us (9%)
  starting transfers between devices  16.7 us (7%)
  between operations  13.6 us (6%)
  Pallas kernels  13 us (6%)
  local copies, waits for them, and re-layouts  4.16 us (2%)
    psum x1, waiting for transfers between devices, on_device(): whole = lax.psum(spread, 'pcol')  139 us
    all_to_all x1, blocking collectives, exchange(): lax.all_to_all(value, 'prow', 0, 0, axis_index_groups=columns, tiled=True)  21.3 us
    all_to_all x1, waiting for transfers between devices, exchange(): lax.all_to_all(value, 'prow', 0, 0, axis_index_groups=columns, tiled=True)  15.1 us
    ppermute x2, starting transfers between devices, swap(): return lax.ppermute(value, 'prow', [(p, p ^ 1) for p in range(nprow)])  13 us
    pallas_call x1, Pallas kernels, final(): pl.pallas_call(final_kernel, grid=(ncols // step,), out_shape=jax.ShapeDt...  6.7 us
  transfers between devices with their start and end apart: 4, of which 3 were waited for; matrix products, arithmetic and copies ran while one was open for 0% of the time, Pallas kernels for 1%

profile of v4, /device:TPU:1, one launch (start us, length us, event | category | flops | bytes accessed | tf_op | source)
XLA Modules:
  0.0 225.6 jit_solution(11059024361591845315)
XLA Ops:
  6.5 0.0 copy-start.12
  6.5 4.1 %pick.1 = (f32[128,1024]{1,0:T(8,128)}, f32[128,1024]{1,0:T(8,128)}, f32[512,256]{1,0:T(8,128)}, s32[2,128]{1,0:T(2,128)}, s32[2,128]{1,0:T(2,128)}, /*index=5*/s32[2]{0:T(128)}) custom-call(s32[256]{0:T(256)} %piv.1, f32[512,1024]{1,0:T(8,128)} %win.3, f32[16,256]{1,0:T(8,128)} %panel.1), custom_call_target="tpu_custom_call" | custom-call | bytes 2097152 | tf_op jit(solution)/shard_map/pick/pallas_call | solution.py:87
  10.6 8.7 %collective-permute-start = (f32[128,1024]{1,0:T(8,128)}, f32[128,1024]{1,0:T(8,128)S(1)}, u32[]{:S(2)}, u32[]{:S(2)}) collective-permute-start(f32[128,1024]{1,0:T(8,128)} %get-tuple-element.22.give), channel_id=1, source_target_pairs={{0,32},{32,0},{64,96},{96,64},{128,160},{160,128},{192,224},{224,1... | collective-permute-start | bytes 1572872 | tf_op jit(solution)/shard_map/ppermute | solution.py:280
  19.3 0.0 copy-done.12
  19.3 1.7 collective-permute-done.got
  21.0 0.0 copy-start.3
  21.0 0.1 broadcast_in_dim.2.owner
  21.1 0.0 copy-start.1
  21.1 1.1 copy-done.1
  22.3 0.1 deal.1
  22.3 0.0 copy-start.2
  22.4 21.3 %all_to_all.22 = f32[8,16,1024]{2,1,0:T(8,128)S(1)} all-to-all(f32[8,16,1024]{2,1,0:T(8,128)S(1)} %bitcast.8), channel_id=1, replica_groups={{0,64,128,192,256,320,384,448},{32,96,160,224,288,352,416,480},{1,65,12..., dimensions={0} | all-to-all | bytes 1048576 | tf_op jit(solution)/shard_map/all_to_all | solution.py:283
  43.7 0.0 copy-done.3
  43.7 0.0 copy-start.8
  43.7 0.1 home.1
  43.8 0.0 copy-start.5
  43.8 0.8 copy-done.5
  44.6 0.0 copy-start
  44.6 0.0 copy-start.9
  44.6 0.0 copy-start.10
  44.6 0.0 copy-start.11
  44.6 3.6 %all-to-all-start.1 = ((f32[8,16,1024]{2,1,0:T(8,128)}), f32[8,16,1024]{2,1,0:T(8,128)S(1)}, u32[]{:S(2)}, u32[]{:S(2)}) async-start(f32[8,16,1024]{2,1,0:T(8,128)} %bitcast.6), calls=%async_computation.1 | async-start | bytes 1048576 | tf_op jit(solution)/shard_map/all_to_all | solution.py:283
  48.2 0.0 all-reduce.2.cloned.1.call-start
  48.3 0.7 all-reduce.2.cloned.1.call-update
  49.0 15.1 %all-to-all-done.1 = f32[8,16,1024]{2,1,0:T(8,128)S(1)} async-done(((f32[8,16,1024]{2,1,0:T(8,128)}), f32[8,16,1024]{2,1,0:T(8,128)S(1)}, u32[]{:S(2)}, u32[]{:S(2)}) %all-to-all-start.1) | async-done | bytes 524320 | tf_op jit(solution)/shard_map/all_to_all | solution.py:283
  64.1 0.0 copy-done.2
  64.1 0.9 pair.1
  65.0 4.4 %collective-permute-start.1 = (f32[128,1024]{1,0:T(8,128)}, f32[128,1024]{1,0:T(8,128)}, u32[]{:S(2)}, u32[]{:S(2)}) collective-permute-start(f32[128,1024]{1,0:T(8,128)} %pair.1), channel_id=1, source_target_pairs={{0,32},{32,0},{64,96},{96,64},{128,160},{160,128},{192,224},{224,1... | collective-permute-start | bytes 1572872 | tf_op jit(solution)/shard_map/ppermute | solution.py:280
  69.4 139.4 %all-reduce.2.cloned.1.call-done.panel = f32[512,256]{1,0:T(8,128)} async-done(((f32[512,256]{1,0:T(8,128)}), f32[512,256]{1,0:T(8,128)}) %all-reduce.2.cloned.1.call-update) | async-done | bytes 524304 | tf_op jit(solution)/shard_map/psum | solution.py:288
  208.7 0.0 copy-done.8
  208.7 0.0 copy-start.6
  208.7 1.0 copy-done.6
  209.8 0.0 copy-start.7
  209.8 0.2 split.1
  209.9 0.0 copy-done
  209.9 0.0 copy-done.9
  210.0 0.0 copy-done.10
  210.0 0.0 copy-done.11
  210.0 0.0 copy-start.4
  210.0 1.0 copy-done.4
  211.0 1.0 ready.1
  212.1 0.0 collective-permute-done.1.got
  212.1 0.0 copy-done.7
  212.1 6.7 %final.1 = f32[512,1024]{1,0:T(8,128)} custom-call(s32[2,128]{1,0:T(2,128)S(1)} %copy-done.9, s32[2,128]{1,0:T(2,128)S(1)} %copy-done.10, s32[2]{0:T(128)S(1)} %copy-done.11, s32[256,128]{1,0:T(8,128)S(1)} %broadcast_in_dim.2.owner, bf16[256,768]{1,0:T(8,128)(2,1)S(1)} %get-tuple-element.19.left, bf16[512,768]{1,0:T(8,128)(2,1)S(1)} %get-tuple-element.20.right, ...), custom_call_target="tpu_custom_call" | custom-call | flops 1207959552 | bytes 4194304 | tf_op jit(solution)/shard_map/final/pallas_call | solution.py:260
  (1 shorter events, 0.0 us)
Async XLA Ops:
  6.5 12.8 %copy-start.12 = (s32[256]{0:T(256)S(1)}, s32[256]{0:T(256)}, u32[]{:S(2)}) copy-start(s32[256]{0:T(256)} %piv.1) | copy-start | bytes 3076
  10.6 10.4 %collective-permute-start = (f32[128,1024]{1,0:T(8,128)}, f32[128,1024]{1,0:T(8,128)S(1)}, u32[]{:S(2)}, u32[]{:S(2)}) collective-permute-start(f32[128,1024]{1,0:T(8,128)} %get-tuple-element.22.give), channel_id=1, source_target_pairs={{0,32},{32,0},{64,96},{96,64},{128,160},{160,128},{192,224},{224,1... | collective-permute-start | bytes 1572872 | tf_op jit(solution)/shard_map/ppermute | solution.py:280
  21.0 22.7 %copy-start.3 = (f32[128,1024]{1,0:T(8,128)}, f32[128,1024]{1,0:T(8,128)S(1)}, u32[]{:S(2)}) copy-start(f32[128,1024]{1,0:T(8,128)S(1)} %collective-permute-done.got) | copy-start | bytes 1572868
  21.1 1.1 copy-start.1
  22.3 41.8 %copy-start.2 = (f32[128,1024]{1,0:T(8,128)S(1)}, f32[128,1024]{1,0:T(8,128)}, u32[]{:S(2)}) copy-start(f32[128,1024]{1,0:T(8,128)} %get-tuple-element.21.own) | copy-start | bytes 1572868
  43.7 165.1 %copy-start.8 = (f32[256,256]{1,0:T(8,128)S(1)}, f32[256,256]{1,0:T(8,128)}, u32[]{:S(2)}) copy-start(f32[256,256]{1,0:T(8,128)} %linv.1) | copy-start | bytes 786436
  43.8 0.8 copy-start.5
  44.6 165.4 %copy-start = (f32[512,1024]{1,0:T(8,128)S(1)}, f32[512,1024]{1,0:T(8,128)}, u32[]{:S(2)}) copy-start(f32[512,1024]{1,0:T(8,128)} %win.3) | copy-start | bytes 6291460
  44.6 165.4 %copy-start.9 = (s32[2,128]{1,0:T(2,128)S(1)}, s32[2,128]{1,0:T(2,128)}, u32[]{:S(2)}) copy-start(s32[2,128]{1,0:T(2,128)} %get-tuple-element.15.slots) | copy-start | bytes 3076
  44.6 165.4 %copy-start.10 = (s32[2,128]{1,0:T(2,128)S(1)}, s32[2,128]{1,0:T(2,128)}, u32[]{:S(2)}) copy-start(s32[2,128]{1,0:T(2,128)} %get-tuple-element.16.rows) | copy-start | bytes 3076
  44.6 165.4 %copy-start.11 = (s32[2]{0:T(128)S(1)}, s32[2]{0:T(128)}, u32[]{:S(2)}) copy-start(s32[2]{0:T(128)} %get-tuple-element.17.counts) | copy-start | bytes 28
  44.6 19.5 %all-to-all-start.1 = ((f32[8,16,1024]{2,1,0:T(8,128)}), f32[8,16,1024]{2,1,0:T(8,128)S(1)}, u32[]{:S(2)}, u32[]{:S(2)}) async-start(f32[8,16,1024]{2,1,0:T(8,128)} %bitcast.6), calls=%async_computation.1 | async-start | bytes 1048576 | tf_op jit(solution)/shard_map/all_to_all | solution.py:283
  48.2 160.5 %all-reduce.2.cloned.1.call-start = ((), (), s32[]{:S(2)}) async-start(), calls=%async_computation.2 | async-start | bytes 1048576 | tf_op jit(solution)/shard_map/psum | solution.py:288
  65.0 147.1 %collective-permute-start.1 = (f32[128,1024]{1,0:T(8,128)}, f32[128,1024]{1,0:T(8,128)}, u32[]{:S(2)}, u32[]{:S(2)}) collective-permute-start(f32[128,1024]{1,0:T(8,128)} %pair.1), channel_id=1, source_target_pairs={{0,32},{32,0},{64,96},{96,64},{128,160},{160,128},{192,224},{224,1... | collective-permute-start | bytes 1572872 | tf_op jit(solution)/shard_map/ppermute | solution.py:280
  208.7 1.0 copy-start.6
  209.8 2.3 %copy-start.7 = (f32[128,1024]{1,0:T(8,128)S(1)}, f32[128,1024]{1,0:T(8,128)}, u32[]{:S(2)}) copy-start(f32[128,1024]{1,0:T(8,128)} %get-tuple-element.22.give) | copy-start | bytes 1572868
  210.0 1.0 copy-start.4
Sparse Core Ops, SparseCore 0:
  52.5 156.2 all-reduce.1

commit v5 on v3

--- a/solution.py
+++ b/solution.py
@@ -10,7 +10,7 @@
 CORES = 2
 YS = 8
 LANES = 128
-STEP = 256
+STEP = 512
 PARAMS = pltpu.CompilerParams(vmem_limit_bytes=32 * 1024 * 1024)
 ROOMY = pltpu.CompilerParams(vmem_limit_bytes=58 * 1024 * 1024)
 
@@ -105,10 +105,21 @@
     theirs = (who == partner) | ((who != me) & (who != jnp.where(me == 0, who, -1)))
     for cols in tiles(ncols):
         out[:, cols] = jnp.where(theirs, got[:, cols], own[:, cols])
-    count = panel.shape[0]
-    odd = lax.rem(lax.axis_index("pcol"), 2)
-    rows[pl.ds(pl.multiple_of(odd * count, count), count), :] = panel[...]
-    rows[pl.ds(pl.multiple_of((1 - odd) * count, count), count), :] = beside[...]
+    stack(4, panel, beside, rows)
+
+
+def bit(weight):
+    return lax.rem(lax.axis_index("pcol") // weight, 2)
+
+
+def stack(weight, mine, theirs, out):
+    count = mine.shape[0]
+    for block, side in ((mine, bit(weight)), (theirs, 1 - bit(weight))):
+        out[pl.ds(pl.multiple_of(side * count, count), count), :] = block[...]
+
+
+def join_kernel(mine, theirs, out):
+    stack(1, mine, theirs, out)
 
 
 def ordered(index, pieces, put):
@@ -118,8 +129,7 @@
         put(pl.ds(pl.multiple_of(source * count, count), count), piece[...])
 
 
-def home_kernel(nz, owner, got, *refs):
-    pieces, (out, strip) = refs[:-2], refs[-2:]
+def home_kernel(nz, owner, got, mine, theirs, out, strip):
     half, ncols = got.shape
     part = half // nz
     me, _, base, _ = sides(half)
@@ -133,13 +143,15 @@
         for z in range(nz):
             out[z * part : (z + 1) * part, cols] = jnp.where(chip == z, former, top)
 
-    def put(rows, value):
-        strip[rows, :] = value
-
-    ordered(lax.rem(lax.axis_index("pcol"), YS) // 2, pieces, put)
-
-
-def pair_kernel(owner, own, got, token, out):
+    count = mine.shape[0] // 4
+    for block, side in ((mine, bit(2)), (theirs, 1 - bit(2))):
+        for i in range(4):
+            at = pl.multiple_of((4 * (i % 2) + 2 * side + i // 2) * count, count)
+            strip[pl.ds(at, count), :] = block[i * count : (i + 1) * count, :]
+
+
+def pair_kernel(owner, own, got, *refs):
+    out = refs[-1]
     half, ncols = own.shape
     me, partner, base, _ = sides(half)
     who = half_of(owner, base, half)
@@ -148,17 +160,17 @@
         out[:, cols] = jnp.where(mine, own[:, cols], got[:, cols])
 
 
-def local(kernel, name, params, shapes, *blocks):
+def local(kernel, name, params, shapes, *blocks, after=()):
     outs = tuple(jax.ShapeDtypeStruct(shape, jnp.float32) for shape in shapes)
     return pl.pallas_call(
         kernel,
         out_shape=outs,
-        in_specs=vmem(len(blocks)),
+        in_specs=vmem(len(blocks)) + [pl.BlockSpec(memory_space=pl.ANY)] * len(after),
         out_specs=tuple(vmem(len(outs))),
         compiler_params=params,
         cost_estimate=cost(0, 4 * sum(block.size for block in blocks)),
         name=name,
-    )(*blocks)
+    )(*blocks, *after)
 
 
 def parts(value):
@@ -167,7 +179,7 @@
 
 
 def split_kernel(linv, *refs):
-    strips, (left, right, token) = refs[:-3], refs[-3:]
+    strips, (left, right) = refs[:-2], refs[-2:]
     nb = linv.shape[1]
 
     def put(value, out, rows):
@@ -178,7 +190,6 @@
 
     put(linv[...], left, slice(None))
     ordered(lax.axis_index("pcol") // YS, strips, lambda rows, value: put(value, right, rows))
-    token[...] = jnp.zeros_like(token)
 
 
 def split(linv, strips):
@@ -189,11 +200,10 @@
         out_shape=(
             jax.ShapeDtypeStruct((nb, 3 * nb), jnp.bfloat16),
             jax.ShapeDtypeStruct((nrows, 3 * nb), jnp.bfloat16),
-            jax.ShapeDtypeStruct((8, LANES), jnp.float32),
         ),
         in_specs=vmem(1 + len(strips)),
-        out_specs=tuple(vmem(3)),
-        compiler_params=ROOMY,
+        out_specs=tuple(vmem(2)),
+        compiler_params=PARAMS,
         cost_estimate=cost(0, 10 * nb * (nb + nrows)),
         name="split",
     )(linv, *strips)
@@ -307,6 +317,9 @@
     def exchange(value):
         return lax.all_to_all(value, "prow", 0, 0, axis_index_groups=columns, tiled=True)
 
+    def across(value, weight):
+        return lax.ppermute(value, "pcol", [(c, c ^ weight) for c in range(npcol)])
+
     def ring(value, size, stride):
         span = size * stride
         pairs = lambda d: [(c, c // span * span + (c + d * stride) % span) for c in range(npcol)]
@@ -317,16 +330,17 @@
 
     own, give, table = pick(pivots, window)
     got = swap(give)
-    beside = lax.ppermute(panel, "pcol", [(c, c ^ 1) for c in range(npcol)])
-    chip, rows = local(deal_kernel, "deal", ROOMY, [own.shape, (2 * count, nbw)], owner, own, got, panel, beside)
+    beside = across(panel, 4)
+    chip, rows = local(deal_kernel, "deal", PARAMS, [own.shape, (2 * count, nbw)], owner, own, got, panel, beside)
     dealt = exchange(chip)
-    kernel = functools.partial(home_kernel, nz)
-    line = ring(rows, YS // 2, 2)
-    chosen, strip = local(kernel, "home", ROOMY, [own.shape, (YS * count, nbw)], owner, dealt, *line)
+    (mine,) = local(join_kernel, "join", PARAMS, [(4 * count, nbw)], rows, across(rows, 1))
+    kernel, shapes = functools.partial(home_kernel, nz), [own.shape, (YS * count, nbw)]
+    chosen, strip = local(kernel, "home", ROOMY, shapes, owner, dealt, mine, across(mine, 2))
     far = exchange(chosen)
-    left, right, token = split(linv, ring(strip, npcol // YS, YS))
-    (paired,) = local(pair_kernel, "pair", PARAMS, [own.shape], owner, own, far, token)
+    strips = ring(strip, npcol // YS, YS)
+    (paired,) = local(pair_kernel, "pair", PARAMS, [own.shape], owner, own, far, after=strips[1:])
     last = swap(paired)
+    left, right = split(linv, strips)
     top, swapped = ready(table, owner, own, got, far, window)
     return final(table, owner, left, right, swapped, top, give, last)
 

time: 84 us -> 79.3 us (0.944)
  waiting for transfers between devices: 10.2 us -> 22.8 us
  starting transfers between devices: 52.6 us -> 40.8 us
  Pallas kernels: 16.2 us -> 11.2 us
  local copies, waits for them, and re-layouts: 4.04 us -> 3 us
    ppermute x6 -> x3, starting transfers between devices: 22.9 us -> 9.33 us  [ring(): lax.ppermute(value, 'pcol', pairs(d))]
    ppermute x1 -> x3, starting transfers between devices: 1.92 us -> 10 us  [across(): return lax.ppermute(value, 'pcol', [(c, c ^ weight) for c in range(npcol)])]
    ppermute x1 -> x3, waiting for transfers between devices: 2.53 us -> 10.6 us  [across(): return lax.ppermute(value, 'pcol', [(c, c ^ weight) for c in range(npcol)])]
    all_to_all x2, waiting for transfers between devices: 0.01 us -> 5.46 us  [exchange(): lax.all_to_all(value, 'prow', 0, 0, axis_index_groups=columns, tiled=True)]
    ppermute x2, starting transfers between devices: 16.5 us -> 13.1 us  [swap(): return lax.ppermute(value, 'prow', [(p, p ^ 1) for p in range(nprow)])]
    all_to_all x2, starting transfers between devices: 11.2 us -> 8.37 us  [exchange(): lax.all_to_all(value, 'prow', 0, 0, axis_index_groups=columns, tiled=True)]
    pallas_call x1, Pallas kernels: 2.25 us -> 0.13 us  [split(): pl.pallas_call(split_kernel, out_shape=(jax.ShapeDtypeStruct((nb, 3 * nb)...]
    pallas_call x3 -> x4, Pallas kernels: 4.34 us -> 2.92 us  [local(): pl.pallas_call(kernel, out_shape=outs, in_specs=vmem(len(blocks)) + [pl.B...]
  transfers between devices with their start and end apart: 11 -> 10, of which waited for: 5 -> 8; matrix products, arithmetic and copies ran while one was open for 0% -> 0% of each run, Pallas kernels for 4% -> 1%
where the time goes in v5:
time: 79.3 us; the launch traced here: 78.1 us
  starting transfers between devices  40.8 us (51%)
  waiting for transfers between devices  22.8 us (29%)
  Pallas kernels  11.2 us (14%)
  local copies, waits for them, and re-layouts  3 us (4%)
    ppermute x2, starting transfers between devices, swap(): return lax.ppermute(value, 'prow', [(p, p ^ 1) for p in range(nprow)])  13.1 us
    ppermute x3, waiting for transfers between devices, across(): return lax.ppermute(value, 'pcol', [(c, c ^ weight) for c in range(npcol)])  10.6 us
    ppermute x3, starting transfers between devices, across(): return lax.ppermute(value, 'pcol', [(c, c ^ weight) for c in range(npcol)])  10 us
    ppermute x3, starting transfers between devices, ring(): lax.ppermute(value, 'pcol', pairs(d))  9.33 us
    all_to_all x2, starting transfers between devices, exchange(): lax.all_to_all(value, 'prow', 0, 0, axis_index_groups=columns, tiled=True)  8.37 us
    ppermute x3, waiting for transfers between devices, ring(): lax.ppermute(value, 'pcol', pairs(d))  6.36 us
    all_to_all x2, waiting for transfers between devices, exchange(): lax.all_to_all(value, 'prow', 0, 0, axis_index_groups=columns, tiled=True)  5.46 us
    pallas_call x1, Pallas kernels, final(): pl.pallas_call(final_kernel, grid=(ncols // step,), out_shape=jax.ShapeDt...  3.82 us
  transfers between devices with their start and end apart: 10, of which 8 were waited for; matrix products, arithmetic and copies ran while one was open for 0% of the time, Pallas kernels for 1%

profile of v5, /device:TPU:1, one launch (start us, length us, event | category | flops | bytes accessed | tf_op | source)
XLA Modules:
  0.0 78.1 jit_solution(3015747589263056603)
XLA Ops:
  0.0 3.5 %pick.1 = (f32[128,1024]{1,0:T(8,128)}, f32[128,1024]{1,0:T(8,128)}, s32[2,128]{1,0:T(2,128)}, s32[2,128]{1,0:T(2,128)}, s32[2]{0:T(128)}) custom-call(s32[256]{0:T(256)} %piv.1, f32[512,1024]{1,0:T(8,128)} %win.3), custom_call_target="tpu_custom_call" | custom-call | bytes 2097152 | tf_op jit(solution)/shard_map/pick/pallas_call | solution.py:84
  3.5 9.1 %collective-permute-start = (f32[128,1024]{1,0:T(8,128)}, f32[128,1024]{1,0:T(8,128)S(1)}, u32[]{:S(2)}, u32[]{:S(2)}) collective-permute-start(f32[128,1024]{1,0:T(8,128)} %get-tuple-element.22.give), channel_id=1, source_target_pairs={{0,32},{32,0},{64,96},{96,64},{128,160},{160,128},{192,224},{224,1... | collective-permute-start | bytes 1572872 | tf_op jit(solution)/shard_map/ppermute | solution.py:315
  12.6 0.0 copy-done.12
  12.6 2.1 %collective-permute-start.1 = (f32[16,256]{1,0:T(8,128)S(1)}, f32[16,256]{1,0:T(8,128)S(1)}, u32[]{:S(2)}, u32[]{:S(2)}) collective-permute-start(f32[16,256]{1,0:T(8,128)S(1)} %copy-done.12), channel_id=1, source_target_pairs={{0,4},{1,5},{2,6},{3,7},{4,0},{5,1},{6,2},{7,3},{8,12},{9,13},{10,... | collective-permute-start | bytes 49160 | tf_op jit(solution)/shard_map/ppermute | solution.py:321
  14.7 0.0 copy-done.18
  14.8 6.3 %collective-permute-done.1.beside = f32[16,256]{1,0:T(8,128)S(1)} collective-permute-done((f32[16,256]{1,0:T(8,128)S(1)}, f32[16,256]{1,0:T(8,128)S(1)}, u32[]{:S(2)}, u32[]{:S(2)}) %collective-permute-start.1) | collective-permute-done | bytes 16416 | tf_op jit(solution)/shard_map/ppermute | solution.py:321
  21.0 0.0 collective-permute-done.got
  21.0 0.1 broadcast_in_dim.2.owner
  21.1 0.0 copy-start.3
  21.1 0.0 copy-start.1
  21.2 1.2 %copy-done.1 = f32[128,1024]{1,0:T(8,128)S(1)} copy-done((f32[128,1024]{1,0:T(8,128)S(1)}, f32[128,1024]{1,0:T(8,128)}, u32[]{:S(2)}) %copy-start.1) | copy-done | bytes 524312
  22.3 0.9 %deal.1 = (f32[128,1024]{1,0:T(8,128)}, f32[32,256]{1,0:T(8,128)S(1)}) custom-call(s32[256,128]{1,0:T(8,128)S(1)} %broadcast_in_dim.2.owner, f32[128,1024]{1,0:T(8,128)S(1)} %copy-done.1, f32[128,1024]{1,0:T(8,128)S(1)} %collective-permute-done.got, f32[16,256]{1,0:T(8,128)S(1)} %copy-done.12, f32[16,256]{1,0:T(8,128)S(1)} %collective-permute-done.1.beside), custom_call_target="tpu_custom_call" | custom-call | bytes 1212416 | tf_op jit(solution)/shard_map/deal/pallas_call | solution.py:165
  23.2 0.0 copy-done.6
  23.2 4.7 %all-to-all-start = ((f32[8,16,1024]{2,1,0:T(8,128)}), f32[8,16,1024]{2,1,0:T(8,128)S(1)}, u32[]{:S(2)}, u32[]{:S(2)}) async-start(f32[8,16,1024]{2,1,0:T(8,128)} %bitcast), calls=%async_computation | async-start | bytes 1048576 | tf_op jit(solution)/shard_map/all_to_all | solution.py:318
  28.0 3.0 %collective-permute-start.2 = (f32[32,256]{1,0:T(8,128)S(1)}, f32[32,256]{1,0:T(8,128)S(1)}, u32[]{:S(2)}, u32[]{:S(2)}) collective-permute-start(f32[32,256]{1,0:T(8,128)S(1)} %get-tuple-element.24.mine), channel_id=1, source_target_pairs={{0,1},{1,0},{2,3},{3,2},{4,5},{5,4},{6,7},{7,6},{8,9},{9,8},{10,11... | collective-permute-start | bytes 98312 | tf_op jit(solution)/shard_map/ppermute | solution.py:321
  31.0 1.6 %collective-permute-done.2.theirs = f32[32,256]{1,0:T(8,128)S(1)} collective-permute-done((f32[32,256]{1,0:T(8,128)S(1)}, f32[32,256]{1,0:T(8,128)S(1)}, u32[]{:S(2)}, u32[]{:S(2)}) %collective-permute-start.2) | collective-permute-done | bytes 32800 | tf_op jit(solution)/shard_map/ppermute | solution.py:321
  32.6 0.0 copy-start.10
  32.6 4.9 %collective-permute-start.3 = (f32[64,256]{1,0:T(8,128)S(1)}, f32[64,256]{1,0:T(8,128)S(1)}, u32[]{:S(2)}, u32[]{:S(2)}) collective-permute-start(f32[64,256]{1,0:T(8,128)S(1)} %join.1.mine), channel_id=1, source_target_pairs={{0,2},{1,3},{2,0},{3,1},{4,6},{5,7},{6,4},{7,5},{8,10},{9,11},{10,... | collective-permute-start | bytes 196616 | tf_op jit(solution)/shard_map/ppermute | solution.py:321
  37.6 2.6 %collective-permute-done.3.theirs = f32[64,256]{1,0:T(8,128)S(1)} collective-permute-done((f32[64,256]{1,0:T(8,128)S(1)}, f32[64,256]{1,0:T(8,128)S(1)}, u32[]{:S(2)}, u32[]{:S(2)}) %collective-permute-start.3) | collective-permute-done | bytes 65568 | tf_op jit(solution)/shard_map/ppermute | solution.py:321
  40.2 4.8 %all-to-all-done = f32[8,16,1024]{2,1,0:T(8,128)S(1)} async-done(((f32[8,16,1024]{2,1,0:T(8,128)}), f32[8,16,1024]{2,1,0:T(8,128)S(1)}, u32[]{:S(2)}, u32[]{:S(2)}) %all-to-all-start) | async-done | bytes 524320 | tf_op jit(solution)/shard_map/all_to_all | solution.py:318
  45.0 0.0 copy-done.3
  45.0 0.0 copy-done.10
  45.0 0.0 copy-done.17
  45.0 0.8 copy-done.16
  45.8 1.9 %home.1 = (f32[128,1024]{1,0:T(8,128)}, f32[128,256]{1,0:T(8,128)}) custom-call(s32[256,128]{1,0:T(8,128)} %copy-done.3, f32[128,1024]{1,0:T(8,128)} %bitcast.6, f32[64,256]{1,0:T(8,128)} %copy-done.10, f32[64,256]{1,0:T(8,128)} %copy-done.17), custom_call_target="tpu_custom_call" | custom-call | bytes 786432 | tf_op jit(solution)/shard_map/home/pallas_call | solution.py:165
  47.7 3.6 %all-to-all-start.1 = ((f32[8,16,1024]{2,1,0:T(8,128)}), f32[8,16,1024]{2,1,0:T(8,128)S(1)}, u32[]{:S(2)}, u32[]{:S(2)}) async-start(f32[8,16,1024]{2,1,0:T(8,128)} %bitcast.7), calls=%async_computation.1 | async-start | bytes 1048576 | tf_op jit(solution)/shard_map/all_to_all | solution.py:318
  51.3 4.4 %collective-permute-start.6 = (f32[128,256]{1,0:T(8,128)}, f32[128,256]{1,0:T(8,128)S(1)}, u32[]{:S(2)}, u32[]{:S(2)}) collective-permute-start(f32[128,256]{1,0:T(8,128)} %get-tuple-element.25.refs_0_), channel_id=1, source_target_pairs={{0,24},{1,25},{2,26},{3,27},{4,28},{5,29},{6,30},{7,31},{8,0},{9,1... | collective-permute-start | bytes 393224 | tf_op jit(solution)/shard_map/ppermute | solution.py:326
  55.7 2.4 %collective-permute-start.5 = (f32[128,256]{1,0:T(8,128)}, f32[128,256]{1,0:T(8,128)S(1)}, u32[]{:S(2)}, u32[]{:S(2)}) collective-permute-start(f32[128,256]{1,0:T(8,128)} %get-tuple-element.25.refs_0_), channel_id=1, source_target_pairs={{0,16},{1,17},{2,18},{3,19},{4,20},{5,21},{6,22},{7,23},{8,24},{9,... | collective-permute-start | bytes 393224 | tf_op jit(solution)/shard_map/ppermute | solution.py:326
  58.2 2.5 %collective-permute-start.4 = (f32[128,256]{1,0:T(8,128)}, f32[128,256]{1,0:T(8,128)S(1)}, u32[]{:S(2)}, u32[]{:S(2)}) collective-permute-start(f32[128,256]{1,0:T(8,128)} %get-tuple-element.25.refs_0_), channel_id=1, source_target_pairs={{0,8},{1,9},{2,10},{3,11},{4,12},{5,13},{6,14},{7,15},{8,16},{9,17... | collective-permute-start | bytes 393224 | tf_op jit(solution)/shard_map/ppermute | solution.py:326
  60.7 0.0 collective-permute-done.6.refs_3_.refs_2_
  60.7 2.8 %collective-permute-done.5.refs_2_.refs_1_ = f32[128,256]{1,0:T(8,128)S(1)} collective-permute-done((f32[128,256]{1,0:T(8,128)}, f32[128,256]{1,0:T(8,128)S(1)}, u32[]{:S(2)}, u32[]{:S(2)}) %collective-permute-start.5) | collective-permute-done | bytes 131104 | tf_op jit(solution)/shard_map/ppermute | solution.py:326
  63.5 3.6 %collective-permute-done.4.refs_1_.refs_0_ = f32[128,256]{1,0:T(8,128)S(1)} collective-permute-done((f32[128,256]{1,0:T(8,128)}, f32[128,256]{1,0:T(8,128)S(1)}, u32[]{:S(2)}, u32[]{:S(2)}) %collective-permute-start.4) | collective-permute-done | bytes 131104 | tf_op jit(solution)/shard_map/ppermute | solution.py:326
  67.1 0.7 all-to-all-done.1
  67.8 0.0 copy-done.2
  67.8 0.9 %copy-done.4 = s32[256,128]{1,0:T(8,128)S(1)} copy-done((s32[256,128]{1,0:T(8,128)S(1)}, s32[256,128]{1,0:T(8,128)}, u32[]{:S(2)}) %copy-start.4) | copy-done | bytes 131096
  68.7 0.1 pair.1
  68.8 4.0 %collective-permute-start.7 = (f32[128,1024]{1,0:T(8,128)S(1)}, f32[128,1024]{1,0:T(8,128)S(1)}, u32[]{:S(2)}, u32[]{:S(2)}) collective-permute-start(f32[128,1024]{1,0:T(8,128)S(1)} %pair.1), channel_id=1, source_target_pairs={{0,32},{32,0},{64,96},{96,64},{128,160},{160,128},{192,224},{224,1... | collective-permute-start | bytes 1572872 | tf_op jit(solution)/shard_map/ppermute | solution.py:315
  72.8 0.0 copy-done.9
  72.8 0.0 copy-done.11
  72.8 0.1 split.1
  72.9 0.0 copy-start.8
  72.9 0.0 copy-done.13
  72.9 0.0 copy-done.14
  73.0 0.0 copy-done.15
  73.0 0.0 copy-done
  73.0 0.9 %ready.1 = (f32[128,1024]{1,0:T(8,128)S(1)}, f32[512,1024]{1,0:T(8,128)S(1)}) custom-call(s32[2,128]{1,0:T(2,128)S(1)} %copy-done.13, s32[2,128]{1,0:T(2,128)S(1)} %copy-done.14, s32[2]{0:T(128)S(1)} %copy-done.15, s32[256,128]{1,0:T(8,128)S(1)} %copy-done.5, f32[128,1024]{1,0:T(8,128)S(1)} %copy-done.2, f32[128,1024]{1,0:T(8,128)S(1)} %copy-done.7, ...), custom_call_target="tpu_custom_call" | custom-call | bytes 6291456 | tf_op jit(solution)/shard_map/ready/pallas_call | solution.py:242
  73.9 0.4 collective-permute-done.7.got
  74.3 3.8 %final.1 = f32[512,1024]{1,0:T(8,128)} custom-call(s32[2,128]{1,0:T(2,128)S(1)} %copy-done.13, s32[2,128]{1,0:T(2,128)S(1)} %copy-done.14, s32[2]{0:T(128)S(1)} %copy-done.15, s32[256,128]{1,0:T(8,128)S(1)} %copy-done.5, bf16[256,768]{1,0:T(8,128)(2,1)S(1)} %get-tuple-element.26.left, bf16[512,768]{1,0:T(8,128)(2,1)S(1)} %get-tuple-element.27.right, ...), custom_call_target="tpu_custom_call" | custom-call | flops 1207959552 | bytes 4194304 | tf_op jit(solution)/shard_map/final/pallas_call | solution.py:295
  (20 shorter events, 0.0 us)
Async XLA Ops:
  0.0 14.7 %copy-start.18 = (s32[256]{0:T(256)S(1)}, s32[256]{0:T(256)}, u32[]{:S(2)}) copy-start(s32[256]{0:T(256)} %piv.1) | copy-start | bytes 3076
  0.0 12.6 %copy-start.12 = (f32[16,256]{1,0:T(8,128)S(1)}, f32[16,256]{1,0:T(8,128)}, u32[]{:S(2)}) copy-start(f32[16,256]{1,0:T(8,128)} %panel.1) | copy-start | bytes 49156
  3.5 17.5 %collective-permute-start = (f32[128,1024]{1,0:T(8,128)}, f32[128,1024]{1,0:T(8,128)S(1)}, u32[]{:S(2)}, u32[]{:S(2)}) collective-permute-start(f32[128,1024]{1,0:T(8,128)} %get-tuple-element.22.give), channel_id=1, source_target_pairs={{0,32},{32,0},{64,96},{96,64},{128,160},{160,128},{192,224},{224,1... | collective-permute-start | bytes 1572872 | tf_op jit(solution)/shard_map/ppermute | solution.py:315
  12.6 8.4 %collective-permute-start.1 = (f32[16,256]{1,0:T(8,128)S(1)}, f32[16,256]{1,0:T(8,128)S(1)}, u32[]{:S(2)}, u32[]{:S(2)}) collective-permute-start(f32[16,256]{1,0:T(8,128)S(1)} %copy-done.12), channel_id=1, source_target_pairs={{0,4},{1,5},{2,6},{3,7},{4,0},{5,1},{6,2},{7,3},{8,12},{9,13},{10,... | collective-permute-start | bytes 49160 | tf_op jit(solution)/shard_map/ppermute | solution.py:321
  21.0 2.2 %copy-start.6 = (f32[128,1024]{1,0:T(8,128)}, f32[128,1024]{1,0:T(8,128)S(1)}, u32[]{:S(2)}) copy-start(f32[128,1024]{1,0:T(8,128)S(1)} %collective-permute-done.got) | copy-start | bytes 1572868
  21.1 23.8 %copy-start.3 = (s32[256,128]{1,0:T(8,128)}, s32[256,128]{1,0:T(8,128)S(1)}, u32[]{:S(2)}) copy-start(s32[256,128]{1,0:T(8,128)S(1)} %broadcast_in_dim.2.owner) | copy-start | bytes 393220
  21.1 1.2 %copy-start.1 = (f32[128,1024]{1,0:T(8,128)S(1)}, f32[128,1024]{1,0:T(8,128)}, u32[]{:S(2)}) copy-start(f32[128,1024]{1,0:T(8,128)} %get-tuple-element.21.own) | copy-start | bytes 1572868
  22.3 45.4 %copy-start.2 = (f32[128,1024]{1,0:T(8,128)S(1)}, f32[128,1024]{1,0:T(8,128)}, u32[]{:S(2)}) copy-start(f32[128,1024]{1,0:T(8,128)} %get-tuple-element.21.own) | copy-start | bytes 1572868
  23.2 21.8 %all-to-all-start = ((f32[8,16,1024]{2,1,0:T(8,128)}), f32[8,16,1024]{2,1,0:T(8,128)S(1)}, u32[]{:S(2)}, u32[]{:S(2)}) async-start(f32[8,16,1024]{2,1,0:T(8,128)} %bitcast), calls=%async_computation | async-start | bytes 1048576 | tf_op jit(solution)/shard_map/all_to_all | solution.py:318
  28.0 4.6 %collective-permute-start.2 = (f32[32,256]{1,0:T(8,128)S(1)}, f32[32,256]{1,0:T(8,128)S(1)}, u32[]{:S(2)}, u32[]{:S(2)}) collective-permute-start(f32[32,256]{1,0:T(8,128)S(1)} %get-tuple-element.24.mine), channel_id=1, source_target_pairs={{0,1},{1,0},{2,3},{3,2},{4,5},{5,4},{6,7},{7,6},{8,9},{9,8},{10,11... | collective-permute-start | bytes 98312 | tf_op jit(solution)/shard_map/ppermute | solution.py:321
  32.6 12.4 %copy-start.10 = (f32[64,256]{1,0:T(8,128)}, f32[64,256]{1,0:T(8,128)S(1)}, u32[]{:S(2)}) copy-start(f32[64,256]{1,0:T(8,128)S(1)} %join.1.mine) | copy-start | bytes 196612
  32.6 7.6 %collective-permute-start.3 = (f32[64,256]{1,0:T(8,128)S(1)}, f32[64,256]{1,0:T(8,128)S(1)}, u32[]{:S(2)}, u32[]{:S(2)}) collective-permute-start(f32[64,256]{1,0:T(8,128)S(1)} %join.1.mine), channel_id=1, source_target_pairs={{0,2},{1,3},{2,0},{3,1},{4,6},{5,7},{6,4},{7,5},{8,10},{9,11},{10,... | collective-permute-start | bytes 196616 | tf_op jit(solution)/shard_map/ppermute | solution.py:321
  40.2 4.8 %copy-start.17 = (f32[64,256]{1,0:T(8,128)}, f32[64,256]{1,0:T(8,128)S(1)}, u32[]{:S(2)}) copy-start(f32[64,256]{1,0:T(8,128)S(1)} %collective-permute-done.3.theirs) | copy-start | bytes 196612
  45.0 0.8 %copy-start.16 = (f32[8,16,1024]{2,1,0:T(8,128)}, f32[8,16,1024]{2,1,0:T(8,128)S(1)}, u32[]{:S(2)}) copy-start(f32[8,16,1024]{2,1,0:T(8,128)S(1)} %all-to-all-done) | copy-start | bytes 1572868
  45.8 27.2 %copy-start.13 = (s32[2,128]{1,0:T(2,128)S(1)}, s32[2,128]{1,0:T(2,128)}, u32[]{:S(2)}) copy-start(s32[2,128]{1,0:T(2,128)} %get-tuple-element.18.slots) | copy-start | bytes 3076
  45.8 27.2 %copy-start.14 = (s32[2,128]{1,0:T(2,128)S(1)}, s32[2,128]{1,0:T(2,128)}, u32[]{:S(2)}) copy-start(s32[2,128]{1,0:T(2,128)} %get-tuple-element.19.rows) | copy-start | bytes 3076
  45.8 27.2 %copy-start.15 = (s32[2]{0:T(128)S(1)}, s32[2]{0:T(128)}, u32[]{:S(2)}) copy-start(s32[2]{0:T(128)} %get-tuple-element.20.counts) | copy-start | bytes 28
  47.7 25.3 %copy-start = (f32[512,1024]{1,0:T(8,128)S(1)}, f32[512,1024]{1,0:T(8,128)}, u32[]{:S(2)}) copy-start(f32[512,1024]{1,0:T(8,128)} %win.3) | copy-start | bytes 6291460
  47.7 20.0 %all-to-all-start.1 = ((f32[8,16,1024]{2,1,0:T(8,128)}), f32[8,16,1024]{2,1,0:T(8,128)S(1)}, u32[]{:S(2)}, u32[]{:S(2)}) async-start(f32[8,16,1024]{2,1,0:T(8,128)} %bitcast.7), calls=%async_computation.1 | async-start | bytes 1048576 | tf_op jit(solution)/shard_map/all_to_all | solution.py:318
  51.3 9.4 %collective-permute-start.6 = (f32[128,256]{1,0:T(8,128)}, f32[128,256]{1,0:T(8,128)S(1)}, u32[]{:S(2)}, u32[]{:S(2)}) collective-permute-start(f32[128,256]{1,0:T(8,128)} %get-tuple-element.25.refs_0_), channel_id=1, source_target_pairs={{0,24},{1,25},{2,26},{3,27},{4,28},{5,29},{6,30},{7,31},{8,0},{9,1... | collective-permute-start | bytes 393224 | tf_op jit(solution)/shard_map/ppermute | solution.py:326
  55.7 7.7 %collective-permute-start.5 = (f32[128,256]{1,0:T(8,128)}, f32[128,256]{1,0:T(8,128)S(1)}, u32[]{:S(2)}, u32[]{:S(2)}) collective-permute-start(f32[128,256]{1,0:T(8,128)} %get-tuple-element.25.refs_0_), channel_id=1, source_target_pairs={{0,16},{1,17},{2,18},{3,19},{4,20},{5,21},{6,22},{7,23},{8,24},{9,... | collective-permute-start | bytes 393224 | tf_op jit(solution)/shard_map/ppermute | solution.py:326
  58.2 8.9 %collective-permute-start.4 = (f32[128,256]{1,0:T(8,128)}, f32[128,256]{1,0:T(8,128)S(1)}, u32[]{:S(2)}, u32[]{:S(2)}) collective-permute-start(f32[128,256]{1,0:T(8,128)} %get-tuple-element.25.refs_0_), channel_id=1, source_target_pairs={{0,8},{1,9},{2,10},{3,11},{4,12},{5,13},{6,14},{7,15},{8,16},{9,17... | collective-permute-start | bytes 393224 | tf_op jit(solution)/shard_map/ppermute | solution.py:326
  67.8 0.9 %copy-start.4 = (s32[256,128]{1,0:T(8,128)S(1)}, s32[256,128]{1,0:T(8,128)}, u32[]{:S(2)}) copy-start(s32[256,128]{1,0:T(8,128)} %copy-done.3) | copy-start | bytes 393220
  68.7 4.1 %copy-start.9 = (f32[256,256]{1,0:T(8,128)S(1)}, f32[256,256]{1,0:T(8,128)}, u32[]{:S(2)}) copy-start(f32[256,256]{1,0:T(8,128)} %linv.1) | copy-start | bytes 786436
  68.7 4.1 %copy-start.11 = (f32[128,256]{1,0:T(8,128)S(1)}, f32[128,256]{1,0:T(8,128)}, u32[]{:S(2)}) copy-start(f32[128,256]{1,0:T(8,128)} %get-tuple-element.25.refs_0_) | copy-start | bytes 393220
  68.7 4.3 %copy-start.5 = (s32[256,128]{1,0:T(8,128)S(1)}, s32[256,128]{1,0:T(8,128)}, u32[]{:S(2)}) copy-start(s32[256,128]{1,0:T(8,128)} %copy-done.3) | copy-start | bytes 393220
  68.7 4.3 %copy-start.7 = (f32[128,1024]{1,0:T(8,128)S(1)}, f32[128,1024]{1,0:T(8,128)}, u32[]{:S(2)}) copy-start(f32[128,1024]{1,0:T(8,128)} %copy-done.6) | copy-start | bytes 1572868
  68.8 5.5 %collective-permute-start.7 = (f32[128,1024]{1,0:T(8,128)S(1)}, f32[128,1024]{1,0:T(8,128)S(1)}, u32[]{:S(2)}, u32[]{:S(2)}) collective-permute-start(f32[128,1024]{1,0:T(8,128)S(1)} %pair.1), channel_id=1, source_target_pairs={{0,32},{32,0},{64,96},{96,64},{128,160},{160,128},{192,224},{224,1... | collective-permute-start | bytes 1572872 | tf_op jit(solution)/shard_map/ppermute | solution.py:315
  72.9 1.4 %copy-start.8 = (f32[128,1024]{1,0:T(8,128)S(1)}, f32[128,1024]{1,0:T(8,128)}, u32[]{:S(2)}) copy-start(f32[128,1024]{1,0:T(8,128)} %get-tuple-element.22.give) | copy-start | bytes 1572868

commit v6 on v5

--- a/solution.py
+++ b/solution.py
@@ -129,12 +129,15 @@
         put(pl.ds(pl.multiple_of(source * count, count), count), piece[...])
 
 
-def home_kernel(nz, owner, got, mine, theirs, out, strip):
+def home_kernel(nz, nrows, piv, got, mine, theirs, out, strip):
     half, ncols = got.shape
     part = half // nz
     me, _, base, _ = sides(half)
-    at = pl.multiple_of(base + me // CORES * part, part)
-    chip = owner[pl.ds(at, part), :] // CORES
+    at = base + me // CORES * part
+    slot = lax.broadcasted_iota(jnp.int32, (part, LANES), 0)
+    chip = jnp.zeros((part, LANES), jnp.int32)
+    for i in range(part):
+        chip = jnp.where(slot == i, piv[at + i] // (nrows * CORES), chip)
     for cols in tiles(ncols):
         former = got[0:part, cols]
         top = former
@@ -160,17 +163,17 @@
         out[:, cols] = jnp.where(mine, own[:, cols], got[:, cols])
 
 
-def local(kernel, name, params, shapes, *blocks, after=()):
+def local(kernel, name, params, shapes, *blocks, scalars=(), after=()):
     outs = tuple(jax.ShapeDtypeStruct(shape, jnp.float32) for shape in shapes)
     return pl.pallas_call(
         kernel,
         out_shape=outs,
-        in_specs=vmem(len(blocks)) + [pl.BlockSpec(memory_space=pl.ANY)] * len(after),
+        in_specs=smem(len(scalars)) + vmem(len(blocks)) + [pl.BlockSpec(memory_space=pl.ANY)] * len(after),
         out_specs=tuple(vmem(len(outs))),
         compiler_params=params,
         cost_estimate=cost(0, 4 * sum(block.size for block in blocks)),
         name=name,
-    )(*blocks, *after)
+    )(*scalars, *blocks, *after)
 
 
 def parts(value):
@@ -329,13 +332,15 @@
     count = panel.shape[0]
 
     own, give, table = pick(pivots, window)
+    give, beside = lax.optimization_barrier((give, across(panel, 4)))
     got = swap(give)
-    beside = across(panel, 4)
     chip, rows = local(deal_kernel, "deal", PARAMS, [own.shape, (2 * count, nbw)], owner, own, got, panel, beside)
     dealt = exchange(chip)
     (mine,) = local(join_kernel, "join", PARAMS, [(4 * count, nbw)], rows, across(rows, 1))
-    kernel, shapes = functools.partial(home_kernel, nz), [own.shape, (YS * count, nbw)]
-    chosen, strip = local(kernel, "home", ROOMY, shapes, owner, dealt, mine, across(mine, 2))
+    kernel, shapes = functools.partial(home_kernel, nz, nrows), [own.shape, (YS * count, nbw)]
+    chosen, strip = local(
+        kernel, "home", ROOMY, shapes, dealt, mine, across(mine, 2), scalars=(pivots,)
+    )
     far = exchange(chosen)
     strips = ring(strip, npcol // YS, YS)
     (paired,) = local(pair_kernel, "pair", PARAMS, [own.shape], owner, own, far, after=strips[1:])

time: 79.3 us -> 81 us (1.021)
  starting transfers between devices: 40.8 us -> 41.7 us
    ppermute x2, starting transfers between devices: 13.1 us -> 9.17 us  [swap(): return lax.ppermute(value, 'prow', [(p, p ^ 1) for p in range(nprow)])]
    ppermute x3, waiting for transfers between devices: 10.6 us -> 6.97 us  [across(): return lax.ppermute(value, 'pcol', [(c, c ^ weight) for c in range(npcol)])]
    ppermute x3, starting transfers between devices: 10 us -> 13.3 us  [across(): return lax.ppermute(value, 'pcol', [(c, c ^ weight) for c in range(npcol)])]
    all_to_all x2, waiting for transfers between devices: 5.46 us -> 7.68 us  [exchange(): lax.all_to_all(value, 'prow', 0, 0, axis_index_groups=columns, tiled=True)]
    ppermute x2, waiting for transfers between devices: 0.4 us -> 2 us  [swap(): return lax.ppermute(value, 'prow', [(p, p ^ 1) for p in range(nprow)])]
    all_to_all x2, starting transfers between devices: 8.37 us -> 9.94 us  [exchange(): lax.all_to_all(value, 'prow', 0, 0, axis_index_groups=columns, tiled=True)]
  transfers between devices with their start and end apart: 10 -> 10, of which waited for: 8 -> 8; matrix products, arithmetic and copies ran while one was open for 0% -> 0% of each run, Pallas kernels for 1% -> 6%
where the time goes in v6:
time: 81 us; the launch traced here: 80.3 us
  starting transfers between devices  41.7 us (51%)
  waiting for transfers between devices  22.9 us (28%)
  Pallas kernels  11.8 us (15%)
  local copies, waits for them, and re-layouts  3.67 us (5%)
    ppermute x3, starting transfers between devices, across(): return lax.ppermute(value, 'pcol', [(c, c ^ weight) for c in range(npcol)])  13.3 us
    all_to_all x2, starting transfers between devices, exchange(): lax.all_to_all(value, 'prow', 0, 0, axis_index_groups=columns, tiled=True)  9.94 us
    ppermute x3, starting transfers between devices, ring(): lax.ppermute(value, 'pcol', pairs(d))  9.33 us
    ppermute x2, starting transfers between devices, swap(): return lax.ppermute(value, 'prow', [(p, p ^ 1) for p in range(nprow)])  9.17 us
    all_to_all x2, waiting for transfers between devices, exchange(): lax.all_to_all(value, 'prow', 0, 0, axis_index_groups=columns, tiled=True)  7.68 us
    ppermute x3, waiting for transfers between devices, across(): return lax.ppermute(value, 'pcol', [(c, c ^ weight) for c in range(npcol)])  6.97 us
    ppermute x3, waiting for transfers between devices, ring(): lax.ppermute(value, 'pcol', pairs(d))  6.27 us
    pallas_call x1, Pallas kernels, final(): pl.pallas_call(final_kernel, grid=(ncols // step,), out_shape=jax.ShapeDt...  4.07 us
  transfers between devices with their start and end apart: 10, of which 8 were waited for; matrix products, arithmetic and copies ran while one was open for 0% of the time, Pallas kernels for 6%

profile of v6, /device:TPU:1, one launch (start us, length us, event | category | flops | bytes accessed | tf_op | source)
XLA Modules:
  0.0 80.3 jit_solution(15229381471101024803)
XLA Ops:
  0.0 8.4 %collective-permute-start = (f32[16,256]{1,0:T(8,128)}, f32[16,256]{1,0:T(8,128)S(1)}, u32[]{:S(2)}, u32[]{:S(2)}) collective-permute-start(f32[16,256]{1,0:T(8,128)} %panel.1), channel_id=1, source_target_pairs={{0,4},{1,5},{2,6},{3,7},{4,0},{5,1},{6,2},{7,3},{8,12},{9,13},{10,... | collective-permute-start | bytes 49160 | tf_op jit(solution)/shard_map/ppermute | solution.py:324
  8.4 3.6 %pick.1 = (f32[128,1024]{1,0:T(8,128)}, f32[128,1024]{1,0:T(8,128)}, s32[2,128]{1,0:T(2,128)}, s32[2,128]{1,0:T(2,128)}, s32[2]{0:T(128)}) custom-call(s32[256]{0:T(256)} %piv.3, f32[512,1024]{1,0:T(8,128)} %win.3), custom_call_target="tpu_custom_call" | custom-call | bytes 2097152 | tf_op jit(solution)/shard_map/pick/pallas_call | solution.py:84
  12.0 0.0 collective-permute-done.beside
  12.0 6.6 %collective-permute-start.1 = (f32[128,1024]{1,0:T(8,128)}, f32[128,1024]{1,0:T(8,128)S(1)}, u32[]{:S(2)}, u32[]{:S(2)}) collective-permute-start(f32[128,1024]{1,0:T(8,128)} %get-tuple-element.25.give), channel_id=1, source_target_pairs={{0,32},{32,0},{64,96},{96,64},{128,160},{160,128},{192,224},{224,1... | collective-permute-start | bytes 1572872 | tf_op jit(solution)/shard_map/ppermute | solution.py:318
  18.7 0.0 copy-done.18
  18.7 1.7 %collective-permute-done.1.got = f32[128,1024]{1,0:T(8,128)S(1)} collective-permute-done((f32[128,1024]{1,0:T(8,128)}, f32[128,1024]{1,0:T(8,128)S(1)}, u32[]{:S(2)}, u32[]{:S(2)}) %collective-permute-start.1) | collective-permute-done | bytes 524320 | tf_op jit(solution)/shard_map/ppermute | solution.py:318
  20.4 0.1 broadcast_in_dim.2.owner
  20.5 0.0 copy-done.12
  20.5 0.0 copy-start.1
  20.5 1.1 %copy-done.1 = f32[128,1024]{1,0:T(8,128)S(1)} copy-done((f32[128,1024]{1,0:T(8,128)S(1)}, f32[128,1024]{1,0:T(8,128)}, u32[]{:S(2)}) %copy-start.1) | copy-done | bytes 524312
  21.6 0.9 %deal.1 = (f32[128,1024]{1,0:T(8,128)}, f32[32,256]{1,0:T(8,128)S(1)}) custom-call(s32[256,128]{1,0:T(8,128)S(1)} %broadcast_in_dim.2.owner, f32[128,1024]{1,0:T(8,128)S(1)} %copy-done.1, f32[128,1024]{1,0:T(8,128)S(1)} %collective-permute-done.1.got, f32[16,256]{1,0:T(8,128)S(1)} %copy-done.12, f32[16,256]{1,0:T(8,128)S(1)} %collective-permute-done.beside), custom_call_target="tpu_custom_call" | custom-call | bytes 1212416 | tf_op jit(solution)/shard_map/deal/pallas_call | solution.py:168
  22.5 6.3 %all-to-all-start = ((f32[8,16,1024]{2,1,0:T(8,128)}), f32[8,16,1024]{2,1,0:T(8,128)S(1)}, u32[]{:S(2)}, u32[]{:S(2)}) async-start(f32[8,16,1024]{2,1,0:T(8,128)} %bitcast), calls=%async_computation | async-start | bytes 1048576 | tf_op jit(solution)/shard_map/all_to_all | solution.py:321
  28.8 2.3 %collective-permute-start.2 = (f32[32,256]{1,0:T(8,128)S(1)}, f32[32,256]{1,0:T(8,128)S(1)}, u32[]{:S(2)}, u32[]{:S(2)}) collective-permute-start(f32[32,256]{1,0:T(8,128)S(1)} %get-tuple-element.28.mine), channel_id=1, source_target_pairs={{0,1},{1,0},{2,3},{3,2},{4,5},{5,4},{6,7},{7,6},{8,9},{9,8},{10,11... | collective-permute-start | bytes 98312 | tf_op jit(solution)/shard_map/ppermute | solution.py:324
  31.1 2.6 %collective-permute-done.2.theirs = f32[32,256]{1,0:T(8,128)S(1)} collective-permute-done((f32[32,256]{1,0:T(8,128)S(1)}, f32[32,256]{1,0:T(8,128)S(1)}, u32[]{:S(2)}, u32[]{:S(2)}) %collective-permute-start.2) | collective-permute-done | bytes 32800 | tf_op jit(solution)/shard_map/ppermute | solution.py:324
  33.8 0.0 copy-start.10
  33.8 2.6 %collective-permute-start.3 = (f32[64,256]{1,0:T(8,128)S(1)}, f32[64,256]{1,0:T(8,128)S(1)}, u32[]{:S(2)}, u32[]{:S(2)}) collective-permute-start(f32[64,256]{1,0:T(8,128)S(1)} %join.1.mine), channel_id=1, source_target_pairs={{0,2},{1,3},{2,0},{3,1},{4,6},{5,7},{6,4},{7,5},{8,10},{9,11},{10,... | collective-permute-start | bytes 196616 | tf_op jit(solution)/shard_map/ppermute | solution.py:324
  36.3 4.3 %collective-permute-done.3.theirs = f32[64,256]{1,0:T(8,128)S(1)} collective-permute-done((f32[64,256]{1,0:T(8,128)S(1)}, f32[64,256]{1,0:T(8,128)S(1)}, u32[]{:S(2)}, u32[]{:S(2)}) %collective-permute-start.3) | collective-permute-done | bytes 65568 | tf_op jit(solution)/shard_map/ppermute | solution.py:324
  40.7 6.1 %all-to-all-done = f32[8,16,1024]{2,1,0:T(8,128)S(1)} async-done(((f32[8,16,1024]{2,1,0:T(8,128)}), f32[8,16,1024]{2,1,0:T(8,128)S(1)}, u32[]{:S(2)}, u32[]{:S(2)}) %all-to-all-start) | async-done | bytes 524320 | tf_op jit(solution)/shard_map/all_to_all | solution.py:321
  46.8 0.0 copy-done.10
  46.8 0.0 copy-done.17
  46.8 0.8 copy-done.16
  47.6 2.0 %home.1 = (f32[128,1024]{1,0:T(8,128)}, f32[128,256]{1,0:T(8,128)}) custom-call(s32[256]{0:T(256)} %piv.3, f32[128,1024]{1,0:T(8,128)} %bitcast.6, f32[64,256]{1,0:T(8,128)} %copy-done.10, f32[64,256]{1,0:T(8,128)} %copy-done.17), custom_call_target="tpu_custom_call" | custom-call | bytes 655360 | tf_op jit(solution)/shard_map/home/pallas_call | solution.py:168
  49.6 0.0 copy-done.3
  49.6 3.6 %all-to-all-start.1 = ((f32[8,16,1024]{2,1,0:T(8,128)}), f32[8,16,1024]{2,1,0:T(8,128)S(1)}, u32[]{:S(2)}, u32[]{:S(2)}) async-start(f32[8,16,1024]{2,1,0:T(8,128)} %bitcast.7), calls=%async_computation.1 | async-start | bytes 1048576 | tf_op jit(solution)/shard_map/all_to_all | solution.py:321
  53.2 4.4 %collective-permute-start.6 = (f32[128,256]{1,0:T(8,128)}, f32[128,256]{1,0:T(8,128)S(1)}, u32[]{:S(2)}, u32[]{:S(2)}) collective-permute-start(f32[128,256]{1,0:T(8,128)} %get-tuple-element.29.refs_0_), channel_id=1, source_target_pairs={{0,24},{1,25},{2,26},{3,27},{4,28},{5,29},{6,30},{7,31},{8,0},{9,1... | collective-permute-start | bytes 393224 | tf_op jit(solution)/shard_map/ppermute | solution.py:329
  57.6 2.4 %collective-permute-start.5 = (f32[128,256]{1,0:T(8,128)}, f32[128,256]{1,0:T(8,128)S(1)}, u32[]{:S(2)}, u32[]{:S(2)}) collective-permute-start(f32[128,256]{1,0:T(8,128)} %get-tuple-element.29.refs_0_), channel_id=1, source_target_pairs={{0,16},{1,17},{2,18},{3,19},{4,20},{5,21},{6,22},{7,23},{8,24},{9,... | collective-permute-start | bytes 393224 | tf_op jit(solution)/shard_map/ppermute | solution.py:329
  60.1 2.5 %collective-permute-start.4 = (f32[128,256]{1,0:T(8,128)}, f32[128,256]{1,0:T(8,128)S(1)}, u32[]{:S(2)}, u32[]{:S(2)}) collective-permute-start(f32[128,256]{1,0:T(8,128)} %get-tuple-element.29.refs_0_), channel_id=1, source_target_pairs={{0,8},{1,9},{2,10},{3,11},{4,12},{5,13},{6,14},{7,15},{8,16},{9,17... | collective-permute-start | bytes 393224 | tf_op jit(solution)/shard_map/ppermute | solution.py:329
  62.6 0.0 collective-permute-done.6.refs_3_.refs_2_
  62.6 2.9 %collective-permute-done.5.refs_2_.refs_1_ = f32[128,256]{1,0:T(8,128)S(1)} collective-permute-done((f32[128,256]{1,0:T(8,128)}, f32[128,256]{1,0:T(8,128)S(1)}, u32[]{:S(2)}, u32[]{:S(2)}) %collective-permute-start.5) | collective-permute-done | bytes 131104 | tf_op jit(solution)/shard_map/ppermute | solution.py:329
  65.5 3.4 %collective-permute-done.4.refs_1_.refs_0_ = f32[128,256]{1,0:T(8,128)S(1)} collective-permute-done((f32[128,256]{1,0:T(8,128)}, f32[128,256]{1,0:T(8,128)S(1)}, u32[]{:S(2)}, u32[]{:S(2)}) %collective-permute-start.4) | collective-permute-done | bytes 131104 | tf_op jit(solution)/shard_map/ppermute | solution.py:329
  68.9 0.6 copy-done.5
  69.5 1.6 %all-to-all-done.1 = f32[8,16,1024]{2,1,0:T(8,128)S(1)} async-done(((f32[8,16,1024]{2,1,0:T(8,128)}), f32[8,16,1024]{2,1,0:T(8,128)S(1)}, u32[]{:S(2)}, u32[]{:S(2)}) %all-to-all-start.1) | async-done | bytes 524320 | tf_op jit(solution)/shard_map/all_to_all | solution.py:321
  71.1 0.0 copy-done.2
  71.1 1.0 %copy-done.6 = f32[128,256]{1,0:T(8,128)S(1)} copy-done((f32[128,256]{1,0:T(8,128)S(1)}, f32[128,256]{1,0:T(8,128)}, u32[]{:S(2)}) %copy-start.6) | copy-done | bytes 131096
  72.1 0.1 pair.1
  72.2 2.5 %collective-permute-start.7 = (f32[128,1024]{1,0:T(8,128)S(1)}, f32[128,1024]{1,0:T(8,128)S(1)}, u32[]{:S(2)}, u32[]{:S(2)}) collective-permute-start(f32[128,1024]{1,0:T(8,128)S(1)} %pair.1), channel_id=1, source_target_pairs={{0,32},{32,0},{64,96},{96,64},{128,160},{160,128},{192,224},{224,1... | collective-permute-start | bytes 1572872 | tf_op jit(solution)/shard_map/ppermute | solution.py:318
  74.7 0.0 copy-done.7
  74.7 0.0 copy-done.9
  74.7 0.0 copy-done.11
  74.7 0.1 split.1
  74.9 0.0 copy-start.8
  74.9 0.0 copy-done.13
  74.9 0.0 copy-done.14
  74.9 0.0 copy-done.15
  74.9 1.0 %ready.1 = (f32[128,1024]{1,0:T(8,128)S(1)}, f32[512,1024]{1,0:T(8,128)S(1)}) custom-call(s32[2,128]{1,0:T(2,128)S(1)} %copy-done.13, s32[2,128]{1,0:T(2,128)S(1)} %copy-done.14, s32[2]{0:T(128)S(1)} %copy-done.15, s32[256,128]{1,0:T(8,128)S(1)} %broadcast_in_dim.2.owner, f32[128,1024]{1,0:T(8,128)S(1)} %copy-done.2, f32[128,1024]{1,0:T(8,128)S(1)} %copy-done.4, ...), custom_call_target="tpu_custom_call" | custom-call | bytes 6291456 | tf_op jit(solution)/shard_map/ready/pallas_call | solution.py:245
  75.9 0.3 collective-permute-done.7.got
  76.2 0.0 copy-done.8
  76.2 4.1 %final.1 = f32[512,1024]{1,0:T(8,128)} custom-call(s32[2,128]{1,0:T(2,128)S(1)} %copy-done.13, s32[2,128]{1,0:T(2,128)S(1)} %copy-done.14, s32[2]{0:T(128)S(1)} %copy-done.15, s32[256,128]{1,0:T(8,128)S(1)} %broadcast_in_dim.2.owner, bf16[256,768]{1,0:T(8,128)(2,1)S(1)} %get-tuple-element.30.left, bf16[512,768]{1,0:T(8,128)(2,1)S(1)} %get-tuple-element.31.right, ...), custom_call_target="tpu_custom_call" | custom-call | flops 1207959552 | bytes 4194304 | tf_op jit(solution)/shard_map/final/pallas_call | solution.py:298
  (20 shorter events, 0.0 us)
Async XLA Ops:
  0.0 20.5 %copy-start.12 = (f32[16,256]{1,0:T(8,128)S(1)}, f32[16,256]{1,0:T(8,128)}, u32[]{:S(2)}) copy-start(f32[16,256]{1,0:T(8,128)} %panel.1) | copy-start | bytes 49156
  0.0 18.7 %copy-start.18 = (s32[256]{0:T(256)S(1)}, s32[256]{0:T(256)}, u32[]{:S(2)}) copy-start(s32[256]{0:T(256)} %piv.3) | copy-start | bytes 3076
  0.0 12.0 %collective-permute-start = (f32[16,256]{1,0:T(8,128)}, f32[16,256]{1,0:T(8,128)S(1)}, u32[]{:S(2)}, u32[]{:S(2)}) collective-permute-start(f32[16,256]{1,0:T(8,128)} %panel.1), channel_id=1, source_target_pairs={{0,4},{1,5},{2,6},{3,7},{4,0},{5,1},{6,2},{7,3},{8,12},{9,13},{10,... | collective-permute-start | bytes 49160 | tf_op jit(solution)/shard_map/ppermute | solution.py:324
  12.0 8.4 %collective-permute-start.1 = (f32[128,1024]{1,0:T(8,128)}, f32[128,1024]{1,0:T(8,128)S(1)}, u32[]{:S(2)}, u32[]{:S(2)}) collective-permute-start(f32[128,1024]{1,0:T(8,128)} %get-tuple-element.25.give), channel_id=1, source_target_pairs={{0,32},{32,0},{64,96},{96,64},{128,160},{160,128},{192,224},{224,1... | collective-permute-start | bytes 1572872 | tf_op jit(solution)/shard_map/ppermute | solution.py:318
  20.4 29.2 %copy-start.3 = (f32[128,1024]{1,0:T(8,128)}, f32[128,1024]{1,0:T(8,128)S(1)}, u32[]{:S(2)}) copy-start(f32[128,1024]{1,0:T(8,128)S(1)} %collective-permute-done.1.got) | copy-start | bytes 1572868
  20.5 1.1 %copy-start.1 = (f32[128,1024]{1,0:T(8,128)S(1)}, f32[128,1024]{1,0:T(8,128)}, u32[]{:S(2)}) copy-start(f32[128,1024]{1,0:T(8,128)} %get-tuple-element.23.own) | copy-start | bytes 1572868
  21.6 49.5 %copy-start.2 = (f32[128,1024]{1,0:T(8,128)S(1)}, f32[128,1024]{1,0:T(8,128)}, u32[]{:S(2)}) copy-start(f32[128,1024]{1,0:T(8,128)} %get-tuple-element.23.own) | copy-start | bytes 1572868
  22.5 24.3 %all-to-all-start = ((f32[8,16,1024]{2,1,0:T(8,128)}), f32[8,16,1024]{2,1,0:T(8,128)S(1)}, u32[]{:S(2)}, u32[]{:S(2)}) async-start(f32[8,16,1024]{2,1,0:T(8,128)} %bitcast), calls=%async_computation | async-start | bytes 1048576 | tf_op jit(solution)/shard_map/all_to_all | solution.py:321
  28.8 4.9 %collective-permute-start.2 = (f32[32,256]{1,0:T(8,128)S(1)}, f32[32,256]{1,0:T(8,128)S(1)}, u32[]{:S(2)}, u32[]{:S(2)}) collective-permute-start(f32[32,256]{1,0:T(8,128)S(1)} %get-tuple-element.28.mine), channel_id=1, source_target_pairs={{0,1},{1,0},{2,3},{3,2},{4,5},{5,4},{6,7},{7,6},{8,9},{9,8},{10,11... | collective-permute-start | bytes 98312 | tf_op jit(solution)/shard_map/ppermute | solution.py:324
  33.8 13.0 %copy-start.10 = (f32[64,256]{1,0:T(8,128)}, f32[64,256]{1,0:T(8,128)S(1)}, u32[]{:S(2)}) copy-start(f32[64,256]{1,0:T(8,128)S(1)} %join.1.mine) | copy-start | bytes 196612
  33.8 6.9 %collective-permute-start.3 = (f32[64,256]{1,0:T(8,128)S(1)}, f32[64,256]{1,0:T(8,128)S(1)}, u32[]{:S(2)}, u32[]{:S(2)}) collective-permute-start(f32[64,256]{1,0:T(8,128)S(1)} %join.1.mine), channel_id=1, source_target_pairs={{0,2},{1,3},{2,0},{3,1},{4,6},{5,7},{6,4},{7,5},{8,10},{9,11},{10,... | collective-permute-start | bytes 196616 | tf_op jit(solution)/shard_map/ppermute | solution.py:324
  40.7 6.1 %copy-start.17 = (f32[64,256]{1,0:T(8,128)}, f32[64,256]{1,0:T(8,128)S(1)}, u32[]{:S(2)}) copy-start(f32[64,256]{1,0:T(8,128)S(1)} %collective-permute-done.3.theirs) | copy-start | bytes 196612
  46.8 0.8 copy-start.16
  47.6 27.3 %copy-start.13 = (s32[2,128]{1,0:T(2,128)S(1)}, s32[2,128]{1,0:T(2,128)}, u32[]{:S(2)}) copy-start(s32[2,128]{1,0:T(2,128)} %get-tuple-element.20.slots) | copy-start | bytes 3076
  47.6 27.3 %copy-start.14 = (s32[2,128]{1,0:T(2,128)S(1)}, s32[2,128]{1,0:T(2,128)}, u32[]{:S(2)}) copy-start(s32[2,128]{1,0:T(2,128)} %get-tuple-element.21.rows) | copy-start | bytes 3076
  47.6 27.4 %copy-start.15 = (s32[2]{0:T(128)S(1)}, s32[2]{0:T(128)}, u32[]{:S(2)}) copy-start(s32[2]{0:T(128)} %get-tuple-element.22.counts) | copy-start | bytes 28
  49.6 25.3 %copy-start = (f32[512,1024]{1,0:T(8,128)S(1)}, f32[512,1024]{1,0:T(8,128)}, u32[]{:S(2)}) copy-start(f32[512,1024]{1,0:T(8,128)} %win.3) | copy-start | bytes 6291460
  49.6 21.5 %all-to-all-start.1 = ((f32[8,16,1024]{2,1,0:T(8,128)}), f32[8,16,1024]{2,1,0:T(8,128)S(1)}, u32[]{:S(2)}, u32[]{:S(2)}) async-start(f32[8,16,1024]{2,1,0:T(8,128)} %bitcast.7), calls=%async_computation.1 | async-start | bytes 1048576 | tf_op jit(solution)/shard_map/all_to_all | solution.py:321
  53.2 9.4 %collective-permute-start.6 = (f32[128,256]{1,0:T(8,128)}, f32[128,256]{1,0:T(8,128)S(1)}, u32[]{:S(2)}, u32[]{:S(2)}) collective-permute-start(f32[128,256]{1,0:T(8,128)} %get-tuple-element.29.refs_0_), channel_id=1, source_target_pairs={{0,24},{1,25},{2,26},{3,27},{4,28},{5,29},{6,30},{7,31},{8,0},{9,1... | collective-permute-start | bytes 393224 | tf_op jit(solution)/shard_map/ppermute | solution.py:329
  57.6 7.9 %collective-permute-start.5 = (f32[128,256]{1,0:T(8,128)}, f32[128,256]{1,0:T(8,128)S(1)}, u32[]{:S(2)}, u32[]{:S(2)}) collective-permute-start(f32[128,256]{1,0:T(8,128)} %get-tuple-element.29.refs_0_), channel_id=1, source_target_pairs={{0,16},{1,17},{2,18},{3,19},{4,20},{5,21},{6,22},{7,23},{8,24},{9,... | collective-permute-start | bytes 393224 | tf_op jit(solution)/shard_map/ppermute | solution.py:329
  60.1 8.8 %collective-permute-start.4 = (f32[128,256]{1,0:T(8,128)}, f32[128,256]{1,0:T(8,128)S(1)}, u32[]{:S(2)}, u32[]{:S(2)}) collective-permute-start(f32[128,256]{1,0:T(8,128)} %get-tuple-element.29.refs_0_), channel_id=1, source_target_pairs={{0,8},{1,9},{2,10},{3,11},{4,12},{5,13},{6,14},{7,15},{8,16},{9,17... | collective-permute-start | bytes 393224 | tf_op jit(solution)/shard_map/ppermute | solution.py:329
  68.9 0.6 copy-start.5
  71.1 3.8 %copy-start.4 = (f32[128,1024]{1,0:T(8,128)S(1)}, f32[128,1024]{1,0:T(8,128)}, u32[]{:S(2)}) copy-start(f32[128,1024]{1,0:T(8,128)} %copy-done.3) | copy-start | bytes 1572868
  71.1 1.0 %copy-start.6 = (f32[128,256]{1,0:T(8,128)S(1)}, f32[128,256]{1,0:T(8,128)}, u32[]{:S(2)}) copy-start(f32[128,256]{1,0:T(8,128)} %copy-done.5) | copy-start | bytes 393220
  72.1 2.6 %copy-start.7 = (f32[128,256]{1,0:T(8,128)S(1)}, f32[128,256]{1,0:T(8,128)}, u32[]{:S(2)}) copy-start(f32[128,256]{1,0:T(8,128)} %copy-done.5) | copy-start | bytes 393220
  72.1 2.6 %copy-start.9 = (f32[256,256]{1,0:T(8,128)S(1)}, f32[256,256]{1,0:T(8,128)}, u32[]{:S(2)}) copy-start(f32[256,256]{1,0:T(8,128)} %linv.1) | copy-start | bytes 786436
  72.1 2.6 %copy-start.11 = (f32[128,256]{1,0:T(8,128)S(1)}, f32[128,256]{1,0:T(8,128)}, u32[]{:S(2)}) copy-start(f32[128,256]{1,0:T(8,128)} %get-tuple-element.29.refs_0_) | copy-start | bytes 393220
  72.2 4.1 %collective-permute-start.7 = (f32[128,1024]{1,0:T(8,128)S(1)}, f32[128,1024]{1,0:T(8,128)S(1)}, u32[]{:S(2)}, u32[]{:S(2)}) collective-permute-start(f32[128,1024]{1,0:T(8,128)S(1)} %pair.1), channel_id=1, source_target_pairs={{0,32},{32,0},{64,96},{96,64},{128,160},{160,128},{192,224},{224,1... | collective-permute-start | bytes 1572872 | tf_op jit(solution)/shard_map/ppermute | solution.py:318
  74.9 1.3 %copy-start.8 = (f32[128,1024]{1,0:T(8,128)S(1)}, f32[128,1024]{1,0:T(8,128)}, u32[]{:S(2)}) copy-start(f32[128,1024]{1,0:T(8,128)} %get-tuple-element.25.give) | copy-start | bytes 1572868

commit v7 on v6

--- a/solution.py
+++ b/solution.py
@@ -98,14 +98,13 @@
     return owner[pl.ds(pl.multiple_of(base, half), half), :]
 
 
-def deal_kernel(owner, own, got, panel, beside, out, rows):
+def deal_kernel(owner, own, got, out):
     half, ncols = own.shape
     me, partner, base, _ = sides(half)
     who = half_of(owner, base, half)
     theirs = (who == partner) | ((who != me) & (who != jnp.where(me == 0, who, -1)))
     for cols in tiles(ncols):
         out[:, cols] = jnp.where(theirs, got[:, cols], own[:, cols])
-    stack(4, panel, beside, rows)
 
 
 def bit(weight):
@@ -118,8 +117,8 @@
         out[pl.ds(pl.multiple_of(side * count, count), count), :] = block[...]
 
 
-def join_kernel(mine, theirs, out):
-    stack(1, mine, theirs, out)
+def join_kernel(weight, mine, theirs, *refs):
+    stack(weight, mine, theirs, refs[-1])
 
 
 def ordered(index, pieces, put):
@@ -153,6 +152,10 @@
             strip[pl.ds(at, count), :] = block[i * count : (i + 1) * count, :]
 
 
+def mark_kernel(*refs):
+    refs[-1][...] = jnp.zeros_like(refs[-1])
+
+
 def pair_kernel(owner, own, got, *refs):
     out = refs[-1]
     half, ncols = own.shape
@@ -332,18 +335,21 @@
     count = panel.shape[0]
 
     own, give, table = pick(pivots, window)
-    give, beside = lax.optimization_barrier((give, across(panel, 4)))
     got = swap(give)
-    chip, rows = local(deal_kernel, "deal", PARAMS, [own.shape, (2 * count, nbw)], owner, own, got, panel, beside)
+    beside = across(panel, 4)
+    (chip,) = local(deal_kernel, "deal", PARAMS, [own.shape], owner, own, got)
     dealt = exchange(chip)
-    (mine,) = local(join_kernel, "join", PARAMS, [(4 * count, nbw)], rows, across(rows, 1))
+    first, second = functools.partial(join_kernel, 4), functools.partial(join_kernel, 1)
+    (rows,) = local(first, "join", PARAMS, [(2 * count, nbw)], panel, beside, after=(chip,))
+    (mine,) = local(second, "join", PARAMS, [(4 * count, nbw)], rows, across(rows, 1))
     kernel, shapes = functools.partial(home_kernel, nz, nrows), [own.shape, (YS * count, nbw)]
     chosen, strip = local(
         kernel, "home", ROOMY, shapes, dealt, mine, across(mine, 2), scalars=(pivots,)
     )
     far = exchange(chosen)
     strips = ring(strip, npcol // YS, YS)
-    (paired,) = local(pair_kernel, "pair", PARAMS, [own.shape], owner, own, far, after=strips[1:])
+    token = local(mark_kernel, "mark", PARAMS, [(8, LANES)], after=strips[1:])
+    (paired,) = local(pair_kernel, "pair", PARAMS, [own.shape], owner, own, far, after=token)
     last = swap(paired)
     left, right = split(linv, strips)
     top, swapped = ready(table, owner, own, got, far, window)

time: 81 us -> 82.1 us (1.014)
  waiting for transfers between devices: 22.9 us -> 11.1 us
  starting transfers between devices: 41.7 us -> 52.3 us
  local copies, waits for them, and re-layouts: 3.67 us -> 5.48 us
    all_to_all x2, waiting for transfers between devices: 7.68 us -> 0.01 us  [exchange(): lax.all_to_all(value, 'prow', 0, 0, axis_index_groups=columns, tiled=True)]
    ppermute x2, starting transfers between devices: 9.17 us -> 16.6 us  [swap(): return lax.ppermute(value, 'prow', [(p, p ^ 1) for p in range(nprow)])]
    ppermute x3, waiting for transfers between devices: 6.97 us -> 4.51 us  [across(): return lax.ppermute(value, 'pcol', [(c, c ^ weight) for c in range(npcol)])]
    unnamed x38 -> x36, local copies, waits for them, and re-layouts: 3.58 us -> 5.39 us
    all_to_all x2, starting transfers between devices: 9.94 us -> 11.7 us  [exchange(): lax.all_to_all(value, 'prow', 0, 0, axis_index_groups=columns, tiled=True)]
    ppermute x3, waiting for transfers between devices: 6.27 us -> 4.9 us  [ring(): lax.ppermute(value, 'pcol', pairs(d))]
    ppermute x3, starting transfers between devices: 13.3 us -> 14.6 us  [across(): return lax.ppermute(value, 'pcol', [(c, c ^ weight) for c in range(npcol)])]
    pallas_call x4 -> x6, Pallas kernels: 2.99 us -> 3.02 us  [local(): pl.pallas_call(kernel, out_shape=outs, in_specs=smem(len(scalars)) + vmem...]
  transfers between devices with their start and end apart: 10 -> 10, of which waited for: 8 -> 6; matrix products, arithmetic and copies ran while one was open for 0% -> 0% of each run, Pallas kernels for 6% -> 1%
where the time goes in v7:
time: 82.1 us; the launch traced here: 81.4 us
  starting transfers between devices  52.3 us (64%)
  Pallas kernels  12.3 us (15%)
  waiting for transfers between devices  11.1 us (14%)
  local copies, waits for them, and re-layouts  5.48 us (7%)
    ppermute x2, starting transfers between devices, swap(): return lax.ppermute(value, 'prow', [(p, p ^ 1) for p in range(nprow)])  16.6 us
    ppermute x3, starting transfers between devices, across(): return lax.ppermute(value, 'pcol', [(c, c ^ weight) for c in range(npcol)])  14.6 us
    all_to_all x2, starting transfers between devices, exchange(): lax.all_to_all(value, 'prow', 0, 0, axis_index_groups=columns, tiled=True)  11.7 us
    ppermute x3, starting transfers between devices, ring(): lax.ppermute(value, 'pcol', pairs(d))  9.32 us
    unnamed x36, local copies, waits for them, and re-layouts  5.39 us
    ppermute x3, waiting for transfers between devices, ring(): lax.ppermute(value, 'pcol', pairs(d))  4.9 us
    ppermute x3, waiting for transfers between devices, across(): return lax.ppermute(value, 'pcol', [(c, c ^ weight) for c in range(npcol)])  4.51 us
    pallas_call x1, Pallas kernels, final(): pl.pallas_call(final_kernel, grid=(ncols // step,), out_shape=jax.ShapeDt...  4.24 us
  transfers between devices with their start and end apart: 10, of which 6 were waited for; matrix products, arithmetic and copies ran while one was open for 0% of the time, Pallas kernels for 1%

profile of v7, /device:TPU:1, one launch (start us, length us, event | category | flops | bytes accessed | tf_op | source)
XLA Modules:
  0.0 81.4 jit_solution(8977650079347541523)
XLA Ops:
  0.0 3.8 %pick.1 = (f32[128,1024]{1,0:T(8,128)}, f32[128,1024]{1,0:T(8,128)}, s32[2,128]{1,0:T(2,128)}, s32[2,128]{1,0:T(2,128)}, s32[2]{0:T(128)}) custom-call(s32[256]{0:T(256)} %piv.3, f32[512,1024]{1,0:T(8,128)} %win.3), custom_call_target="tpu_custom_call" | custom-call | bytes 2097152 | tf_op jit(solution)/shard_map/pick/pallas_call | solution.py:84
  3.8 8.7 %collective-permute-start = (f32[128,1024]{1,0:T(8,128)}, f32[128,1024]{1,0:T(8,128)S(1)}, u32[]{:S(2)}, u32[]{:S(2)}) collective-permute-start(f32[128,1024]{1,0:T(8,128)} %get-tuple-element.20.give), channel_id=1, source_target_pairs={{0,32},{32,0},{64,96},{96,64},{128,160},{160,128},{192,224},{224,1... | collective-permute-start | bytes 1572872 | tf_op jit(solution)/shard_map/ppermute | solution.py:321
  12.6 0.0 copy-done.17
  12.6 1.7 %collective-permute-done.got = f32[128,1024]{1,0:T(8,128)S(1)} collective-permute-done((f32[128,1024]{1,0:T(8,128)}, f32[128,1024]{1,0:T(8,128)S(1)}, u32[]{:S(2)}, u32[]{:S(2)}) %collective-permute-start) | collective-permute-done | bytes 524320 | tf_op jit(solution)/shard_map/ppermute | solution.py:321
  14.3 0.1 broadcast_in_dim.2.owner
  14.4 0.0 copy-start.1
  14.4 1.1 %copy-done.1 = f32[128,1024]{1,0:T(8,128)S(1)} copy-done((f32[128,1024]{1,0:T(8,128)S(1)}, f32[128,1024]{1,0:T(8,128)}, u32[]{:S(2)}) %copy-start.1) | copy-done | bytes 524312
  15.5 0.9 %deal.1.refs_0_ = f32[128,1024]{1,0:T(8,128)} custom-call(s32[256,128]{1,0:T(8,128)S(1)} %broadcast_in_dim.2.owner, f32[128,1024]{1,0:T(8,128)S(1)} %copy-done.1, f32[128,1024]{1,0:T(8,128)S(1)} %collective-permute-done.got), custom_call_target="tpu_custom_call" | custom-call | bytes 1179648 | tf_op jit(solution)/shard_map/deal/pallas_call | solution.py:171
  16.4 0.0 copy-done.3
  16.4 4.9 %all-to-all-start = ((f32[8,16,1024]{2,1,0:T(8,128)}), f32[8,16,1024]{2,1,0:T(8,128)S(1)}, u32[]{:S(2)}, u32[]{:S(2)}) async-start(f32[8,16,1024]{2,1,0:T(8,128)} %bitcast), calls=%async_computation | async-start | bytes 1048576 | tf_op jit(solution)/shard_map/all_to_all | solution.py:324
  21.4 0.0 copy-done.11
  21.4 7.5 %collective-permute-start.1 = (f32[16,256]{1,0:T(8,128)S(1)}, f32[16,256]{1,0:T(8,128)S(1)}, u32[]{:S(2)}, u32[]{:S(2)}) collective-permute-start(f32[16,256]{1,0:T(8,128)S(1)} %copy-done.11), channel_id=1, source_target_pairs={{0,4},{1,5},{2,6},{3,7},{4,0},{5,1},{6,2},{7,3},{8,12},{9,13},{10,... | collective-permute-start | bytes 49160 | tf_op jit(solution)/shard_map/ppermute | solution.py:327
  28.8 1.1 %collective-permute-done.1.theirs = f32[16,256]{1,0:T(8,128)S(1)} collective-permute-done((f32[16,256]{1,0:T(8,128)S(1)}, f32[16,256]{1,0:T(8,128)S(1)}, u32[]{:S(2)}, u32[]{:S(2)}) %collective-permute-start.1) | collective-permute-done | bytes 16416 | tf_op jit(solution)/shard_map/ppermute | solution.py:327
  30.0 3.0 %collective-permute-start.2 = (f32[32,256]{1,0:T(8,128)S(1)}, f32[32,256]{1,0:T(8,128)S(1)}, u32[]{:S(2)}, u32[]{:S(2)}) collective-permute-start(f32[32,256]{1,0:T(8,128)S(1)} %join.2.mine), channel_id=1, source_target_pairs={{0,1},{1,0},{2,3},{3,2},{4,5},{5,4},{6,7},{7,6},{8,9},{9,8},{10,11... | collective-permute-start | bytes 98312 | tf_op jit(solution)/shard_map/ppermute | solution.py:327
  33.0 1.6 %collective-permute-done.2.theirs = f32[32,256]{1,0:T(8,128)S(1)} collective-permute-done((f32[32,256]{1,0:T(8,128)S(1)}, f32[32,256]{1,0:T(8,128)S(1)}, u32[]{:S(2)}, u32[]{:S(2)}) %collective-permute-start.2) | collective-permute-done | bytes 32800 | tf_op jit(solution)/shard_map/ppermute | solution.py:327
  34.6 0.0 copy-start.9
  34.6 4.2 %collective-permute-start.3 = (f32[64,256]{1,0:T(8,128)S(1)}, f32[64,256]{1,0:T(8,128)S(1)}, u32[]{:S(2)}, u32[]{:S(2)}) collective-permute-start(f32[64,256]{1,0:T(8,128)S(1)} %join.3.mine), channel_id=1, source_target_pairs={{0,2},{1,3},{2,0},{3,1},{4,6},{5,7},{6,4},{7,5},{8,10},{9,11},{10,... | collective-permute-start | bytes 196616 | tf_op jit(solution)/shard_map/ppermute | solution.py:327
  38.8 1.7 %collective-permute-done.3.theirs = f32[64,256]{1,0:T(8,128)S(1)} collective-permute-done((f32[64,256]{1,0:T(8,128)S(1)}, f32[64,256]{1,0:T(8,128)S(1)}, u32[]{:S(2)}, u32[]{:S(2)}) %collective-permute-start.3) | collective-permute-done | bytes 65568 | tf_op jit(solution)/shard_map/ppermute | solution.py:327
  40.5 0.0 all-to-all-done
  40.5 0.0 copy-done.9
  40.6 0.6 copy-done.16
  41.2 0.2 copy-done.15
  41.4 2.0 %home.1 = (f32[128,1024]{1,0:T(8,128)}, f32[128,256]{1,0:T(8,128)}) custom-call(s32[256]{0:T(256)} %piv.3, f32[128,1024]{1,0:T(8,128)} %bitcast.6, f32[64,256]{1,0:T(8,128)} %copy-done.9, f32[64,256]{1,0:T(8,128)} %copy-done.16), custom_call_target="tpu_custom_call" | custom-call | bytes 655360 | tf_op jit(solution)/shard_map/home/pallas_call | solution.py:171
  43.4 0.0 copy-start.14
  43.4 6.8 %all-to-all-start.1 = ((f32[8,16,1024]{2,1,0:T(8,128)}), f32[8,16,1024]{2,1,0:T(8,128)S(1)}, u32[]{:S(2)}, u32[]{:S(2)}) async-start(f32[8,16,1024]{2,1,0:T(8,128)} %bitcast.7), calls=%async_computation.1 | async-start | bytes 1048576 | tf_op jit(solution)/shard_map/all_to_all | solution.py:324
  50.2 4.4 %collective-permute-start.6 = (f32[128,256]{1,0:T(8,128)}, f32[128,256]{1,0:T(8,128)S(1)}, u32[]{:S(2)}, u32[]{:S(2)}) collective-permute-start(f32[128,256]{1,0:T(8,128)} %get-tuple-element.21.refs_0_), channel_id=1, source_target_pairs={{0,24},{1,25},{2,26},{3,27},{4,28},{5,29},{6,30},{7,31},{8,0},{9,1... | collective-permute-start | bytes 393224 | tf_op jit(solution)/shard_map/ppermute | solution.py:332
  54.6 2.4 %collective-permute-start.5 = (f32[128,256]{1,0:T(8,128)}, f32[128,256]{1,0:T(8,128)S(1)}, u32[]{:S(2)}, u32[]{:S(2)}) collective-permute-start(f32[128,256]{1,0:T(8,128)} %get-tuple-element.21.refs_0_), channel_id=1, source_target_pairs={{0,16},{1,17},{2,18},{3,19},{4,20},{5,21},{6,22},{7,23},{8,24},{9,... | collective-permute-start | bytes 393224 | tf_op jit(solution)/shard_map/ppermute | solution.py:332
  57.0 2.5 %collective-permute-start.4 = (f32[128,256]{1,0:T(8,128)}, f32[128,256]{1,0:T(8,128)S(1)}, u32[]{:S(2)}, u32[]{:S(2)}) collective-permute-start(f32[128,256]{1,0:T(8,128)} %get-tuple-element.21.refs_0_), channel_id=1, source_target_pairs={{0,8},{1,9},{2,10},{3,11},{4,12},{5,13},{6,14},{7,15},{8,16},{9,17... | collective-permute-start | bytes 393224 | tf_op jit(solution)/shard_map/ppermute | solution.py:332
  59.5 0.0 collective-permute-done.6.refs_3_.refs_2_
  59.5 2.8 %collective-permute-done.5.refs_2_.refs_1_ = f32[128,256]{1,0:T(8,128)S(1)} collective-permute-done((f32[128,256]{1,0:T(8,128)}, f32[128,256]{1,0:T(8,128)S(1)}, u32[]{:S(2)}, u32[]{:S(2)}) %collective-permute-start.5) | collective-permute-done | bytes 131104 | tf_op jit(solution)/shard_map/ppermute | solution.py:332
  62.3 2.1 %collective-permute-done.4.refs_1_.refs_0_ = f32[128,256]{1,0:T(8,128)S(1)} collective-permute-done((f32[128,256]{1,0:T(8,128)}, f32[128,256]{1,0:T(8,128)S(1)}, u32[]{:S(2)}, u32[]{:S(2)}) %collective-permute-start.4) | collective-permute-done | bytes 131104 | tf_op jit(solution)/shard_map/ppermute | solution.py:332
  64.4 0.7 copy-done.5
  65.1 0.0 all-to-all-done.1
  65.1 0.0 copy-done.2
  65.1 0.1 pair.1
  65.2 7.9 %collective-permute-start.7 = (f32[128,1024]{1,0:T(8,128)S(1)}, f32[128,1024]{1,0:T(8,128)S(1)}, u32[]{:S(2)}, u32[]{:S(2)}) collective-permute-start(f32[128,1024]{1,0:T(8,128)S(1)} %pair.1), channel_id=1, source_target_pairs={{0,32},{32,0},{64,96},{96,64},{128,160},{160,128},{192,224},{224,1... | collective-permute-start | bytes 1572872 | tf_op jit(solution)/shard_map/ppermute | solution.py:321
  73.1 0.0 copy-start.6
  73.1 0.9 %copy-done.6 = f32[128,256]{1,0:T(8,128)S(1)} copy-done((f32[128,256]{1,0:T(8,128)S(1)}, f32[128,256]{1,0:T(8,128)}, u32[]{:S(2)}) %copy-start.6) | copy-done | bytes 131096
  74.0 0.9 %copy-done.8 = f32[256,256]{1,0:T(8,128)S(1)} copy-done((f32[256,256]{1,0:T(8,128)S(1)}, f32[256,256]{1,0:T(8,128)}, u32[]{:S(2)}) %copy-start.8) | copy-done | bytes 262168
  75.0 0.9 %copy-done.10 = f32[128,256]{1,0:T(8,128)S(1)} copy-done((f32[128,256]{1,0:T(8,128)S(1)}, f32[128,256]{1,0:T(8,128)}, u32[]{:S(2)}) %copy-start.10) | copy-done | bytes 131096
  75.9 0.1 split.1
  76.0 0.0 copy-start.7
  76.0 0.0 copy-done
  76.0 0.0 copy-done.12
  76.1 1.0 %ready.1 = (f32[128,1024]{1,0:T(8,128)S(1)}, f32[512,1024]{1,0:T(8,128)S(1)}) custom-call(s32[2,128]{1,0:T(2,128)S(1)} %copy-done.12, s32[2,128]{1,0:T(2,128)S(1)} %copy-done.13, s32[2]{0:T(128)S(1)} %copy-done.14, s32[256,128]{1,0:T(8,128)S(1)} %broadcast_in_dim.2.owner, f32[128,1024]{1,0:T(8,128)S(1)} %copy-done.2, f32[128,1024]{1,0:T(8,128)S(1)} %copy-done.4, ...), custom_call_target="tpu_custom_call" | custom-call | bytes 6291456 | tf_op jit(solution)/shard_map/ready/pallas_call | solution.py:248
  77.1 0.0 collective-permute-done.7.got
  77.1 0.0 copy-done.7
  77.1 4.2 %final.1 = f32[512,1024]{1,0:T(8,128)} custom-call(s32[2,128]{1,0:T(2,128)S(1)} %copy-done.12, s32[2,128]{1,0:T(2,128)S(1)} %copy-done.13, s32[2]{0:T(128)S(1)} %copy-done.14, s32[256,128]{1,0:T(8,128)S(1)} %broadcast_in_dim.2.owner, bf16[256,768]{1,0:T(8,128)(2,1)S(1)} %get-tuple-element.22.left, bf16[512,768]{1,0:T(8,128)(2,1)S(1)} %get-tuple-element.23.right, ...), custom_call_target="tpu_custom_call" | custom-call | flops 1207959552 | bytes 4194304 | tf_op jit(solution)/shard_map/final/pallas_call | solution.py:301
  (20 shorter events, 0.1 us)
Async XLA Ops:
  0.0 12.6 %copy-start.17 = (s32[256]{0:T(256)S(1)}, s32[256]{0:T(256)}, u32[]{:S(2)}) copy-start(s32[256]{0:T(256)} %piv.3) | copy-start | bytes 3076
  0.0 21.4 %copy-start.11 = (f32[16,256]{1,0:T(8,128)S(1)}, f32[16,256]{1,0:T(8,128)}, u32[]{:S(2)}) copy-start(f32[16,256]{1,0:T(8,128)} %mine.1) | copy-start | bytes 49156
  3.8 10.5 %collective-permute-start = (f32[128,1024]{1,0:T(8,128)}, f32[128,1024]{1,0:T(8,128)S(1)}, u32[]{:S(2)}, u32[]{:S(2)}) collective-permute-start(f32[128,1024]{1,0:T(8,128)} %get-tuple-element.20.give), channel_id=1, source_target_pairs={{0,32},{32,0},{64,96},{96,64},{128,160},{160,128},{192,224},{224,1... | collective-permute-start | bytes 1572872 | tf_op jit(solution)/shard_map/ppermute | solution.py:321
  14.3 2.1 %copy-start.3 = (f32[128,1024]{1,0:T(8,128)}, f32[128,1024]{1,0:T(8,128)S(1)}, u32[]{:S(2)}) copy-start(f32[128,1024]{1,0:T(8,128)S(1)} %collective-permute-done.got) | copy-start | bytes 1572868
  14.4 1.1 %copy-start.1 = (f32[128,1024]{1,0:T(8,128)S(1)}, f32[128,1024]{1,0:T(8,128)}, u32[]{:S(2)}) copy-start(f32[128,1024]{1,0:T(8,128)} %get-tuple-element.19.own) | copy-start | bytes 1572868
  16.4 48.7 %copy-start.2 = (f32[128,1024]{1,0:T(8,128)S(1)}, f32[128,1024]{1,0:T(8,128)}, u32[]{:S(2)}) copy-start(f32[128,1024]{1,0:T(8,128)} %get-tuple-element.19.own) | copy-start | bytes 1572868
  16.4 24.1 %all-to-all-start = ((f32[8,16,1024]{2,1,0:T(8,128)}), f32[8,16,1024]{2,1,0:T(8,128)S(1)}, u32[]{:S(2)}, u32[]{:S(2)}) async-start(f32[8,16,1024]{2,1,0:T(8,128)} %bitcast), calls=%async_computation | async-start | bytes 1048576 | tf_op jit(solution)/shard_map/all_to_all | solution.py:324
  21.4 8.6 %collective-permute-start.1 = (f32[16,256]{1,0:T(8,128)S(1)}, f32[16,256]{1,0:T(8,128)S(1)}, u32[]{:S(2)}, u32[]{:S(2)}) collective-permute-start(f32[16,256]{1,0:T(8,128)S(1)} %copy-done.11), channel_id=1, source_target_pairs={{0,4},{1,5},{2,6},{3,7},{4,0},{5,1},{6,2},{7,3},{8,12},{9,13},{10,... | collective-permute-start | bytes 49160 | tf_op jit(solution)/shard_map/ppermute | solution.py:327
  30.0 4.6 %collective-permute-start.2 = (f32[32,256]{1,0:T(8,128)S(1)}, f32[32,256]{1,0:T(8,128)S(1)}, u32[]{:S(2)}, u32[]{:S(2)}) collective-permute-start(f32[32,256]{1,0:T(8,128)S(1)} %join.2.mine), channel_id=1, source_target_pairs={{0,1},{1,0},{2,3},{3,2},{4,5},{5,4},{6,7},{7,6},{8,9},{9,8},{10,11... | collective-permute-start | bytes 98312 | tf_op jit(solution)/shard_map/ppermute | solution.py:327
  34.6 5.9 %copy-start.9 = (f32[64,256]{1,0:T(8,128)}, f32[64,256]{1,0:T(8,128)S(1)}, u32[]{:S(2)}) copy-start(f32[64,256]{1,0:T(8,128)S(1)} %join.3.mine) | copy-start | bytes 196612
  34.6 5.9 %collective-permute-start.3 = (f32[64,256]{1,0:T(8,128)S(1)}, f32[64,256]{1,0:T(8,128)S(1)}, u32[]{:S(2)}, u32[]{:S(2)}) collective-permute-start(f32[64,256]{1,0:T(8,128)S(1)} %join.3.mine), channel_id=1, source_target_pairs={{0,2},{1,3},{2,0},{3,1},{4,6},{5,7},{6,4},{7,5},{8,10},{9,11},{10,... | collective-permute-start | bytes 196616 | tf_op jit(solution)/shard_map/ppermute | solution.py:327
  40.5 0.6 copy-start.16
  40.5 0.8 copy-start.15
  43.4 32.6 %copy-start = (f32[512,1024]{1,0:T(8,128)S(1)}, f32[512,1024]{1,0:T(8,128)}, u32[]{:S(2)}) copy-start(f32[512,1024]{1,0:T(8,128)} %win.3) | copy-start | bytes 6291460
  43.4 32.6 %copy-start.12 = (s32[2,128]{1,0:T(2,128)S(1)}, s32[2,128]{1,0:T(2,128)}, u32[]{:S(2)}) copy-start(s32[2,128]{1,0:T(2,128)} %get-tuple-element.16.slots) | copy-start | bytes 3076
  43.4 32.7 %copy-start.13 = (s32[2,128]{1,0:T(2,128)S(1)}, s32[2,128]{1,0:T(2,128)}, u32[]{:S(2)}) copy-start(s32[2,128]{1,0:T(2,128)} %get-tuple-element.17.rows) | copy-start | bytes 3076
  43.4 32.7 %copy-start.14 = (s32[2]{0:T(128)S(1)}, s32[2]{0:T(128)}, u32[]{:S(2)}) copy-start(s32[2]{0:T(128)} %get-tuple-element.18.counts) | copy-start | bytes 28
  43.4 21.7 %all-to-all-start.1 = ((f32[8,16,1024]{2,1,0:T(8,128)}), f32[8,16,1024]{2,1,0:T(8,128)S(1)}, u32[]{:S(2)}, u32[]{:S(2)}) async-start(f32[8,16,1024]{2,1,0:T(8,128)} %bitcast.7), calls=%async_computation.1 | async-start | bytes 1048576 | tf_op jit(solution)/shard_map/all_to_all | solution.py:324
  50.2 9.3 %collective-permute-start.6 = (f32[128,256]{1,0:T(8,128)}, f32[128,256]{1,0:T(8,128)S(1)}, u32[]{:S(2)}, u32[]{:S(2)}) collective-permute-start(f32[128,256]{1,0:T(8,128)} %get-tuple-element.21.refs_0_), channel_id=1, source_target_pairs={{0,24},{1,25},{2,26},{3,27},{4,28},{5,29},{6,30},{7,31},{8,0},{9,1... | collective-permute-start | bytes 393224 | tf_op jit(solution)/shard_map/ppermute | solution.py:332
  54.6 7.7 %collective-permute-start.5 = (f32[128,256]{1,0:T(8,128)}, f32[128,256]{1,0:T(8,128)S(1)}, u32[]{:S(2)}, u32[]{:S(2)}) collective-permute-start(f32[128,256]{1,0:T(8,128)} %get-tuple-element.21.refs_0_), channel_id=1, source_target_pairs={{0,16},{1,17},{2,18},{3,19},{4,20},{5,21},{6,22},{7,23},{8,24},{9,... | collective-permute-start | bytes 393224 | tf_op jit(solution)/shard_map/ppermute | solution.py:332
  57.0 7.4 %collective-permute-start.4 = (f32[128,256]{1,0:T(8,128)}, f32[128,256]{1,0:T(8,128)S(1)}, u32[]{:S(2)}, u32[]{:S(2)}) collective-permute-start(f32[128,256]{1,0:T(8,128)} %get-tuple-element.21.refs_0_), channel_id=1, source_target_pairs={{0,8},{1,9},{2,10},{3,11},{4,12},{5,13},{6,14},{7,15},{8,16},{9,17... | collective-permute-start | bytes 393224 | tf_op jit(solution)/shard_map/ppermute | solution.py:332
  64.4 0.7 copy-start.5
  65.1 11.0 %copy-start.4 = (f32[128,1024]{1,0:T(8,128)S(1)}, f32[128,1024]{1,0:T(8,128)}, u32[]{:S(2)}) copy-start(f32[128,1024]{1,0:T(8,128)} %copy-done.3) | copy-start | bytes 1572868
  65.2 11.9 %collective-permute-start.7 = (f32[128,1024]{1,0:T(8,128)S(1)}, f32[128,1024]{1,0:T(8,128)S(1)}, u32[]{:S(2)}, u32[]{:S(2)}) collective-permute-start(f32[128,1024]{1,0:T(8,128)S(1)} %pair.1), channel_id=1, source_target_pairs={{0,32},{32,0},{64,96},{96,64},{128,160},{160,128},{192,224},{224,1... | collective-permute-start | bytes 1572872 | tf_op jit(solution)/shard_map/ppermute | solution.py:321
  73.1 0.9 %copy-start.6 = (f32[128,256]{1,0:T(8,128)S(1)}, f32[128,256]{1,0:T(8,128)}, u32[]{:S(2)}) copy-start(f32[128,256]{1,0:T(8,128)} %copy-done.5) | copy-start | bytes 393220
  74.0 0.9 %copy-start.8 = (f32[256,256]{1,0:T(8,128)S(1)}, f32[256,256]{1,0:T(8,128)}, u32[]{:S(2)}) copy-start(f32[256,256]{1,0:T(8,128)} %linv.1) | copy-start | bytes 786436
  75.0 0.9 %copy-start.10 = (f32[128,256]{1,0:T(8,128)S(1)}, f32[128,256]{1,0:T(8,128)}, u32[]{:S(2)}) copy-start(f32[128,256]{1,0:T(8,128)} %get-tuple-element.21.refs_0_) | copy-start | bytes 393220
  76.0 1.1 %copy-start.7 = (f32[128,1024]{1,0:T(8,128)S(1)}, f32[128,1024]{1,0:T(8,128)}, u32[]{:S(2)}) copy-start(f32[128,1024]{1,0:T(8,128)} %get-tuple-element.20.give) | copy-start | bytes 1572868

commit v8 on v5

--- a/solution.py
+++ b/solution.py
@@ -105,7 +105,7 @@
     theirs = (who == partner) | ((who != me) & (who != jnp.where(me == 0, who, -1)))
     for cols in tiles(ncols):
         out[:, cols] = jnp.where(theirs, got[:, cols], own[:, cols])
-    stack(4, panel, beside, rows)
+    stack(1, panel, beside, rows)
 
 
 def bit(weight):
@@ -119,7 +119,7 @@
 
 
 def join_kernel(mine, theirs, out):
-    stack(1, mine, theirs, out)
+    stack(2, mine, theirs, out)
 
 
 def ordered(index, pieces, put):
@@ -143,11 +143,7 @@
         for z in range(nz):
             out[z * part : (z + 1) * part, cols] = jnp.where(chip == z, former, top)
 
-    count = mine.shape[0] // 4
-    for block, side in ((mine, bit(2)), (theirs, 1 - bit(2))):
-        for i in range(4):
-            at = pl.multiple_of((4 * (i % 2) + 2 * side + i // 2) * count, count)
-            strip[pl.ds(at, count), :] = block[i * count : (i + 1) * count, :]
+    stack(4, mine, theirs, strip)
 
 
 def pair_kernel(owner, own, got, *refs):
@@ -330,12 +326,12 @@
 
     own, give, table = pick(pivots, window)
     got = swap(give)
-    beside = across(panel, 4)
+    beside = across(panel, 1)
     chip, rows = local(deal_kernel, "deal", PARAMS, [own.shape, (2 * count, nbw)], owner, own, got, panel, beside)
     dealt = exchange(chip)
-    (mine,) = local(join_kernel, "join", PARAMS, [(4 * count, nbw)], rows, across(rows, 1))
+    (mine,) = local(join_kernel, "join", PARAMS, [(4 * count, nbw)], rows, across(rows, 2))
     kernel, shapes = functools.partial(home_kernel, nz), [own.shape, (YS * count, nbw)]
-    chosen, strip = local(kernel, "home", ROOMY, shapes, owner, dealt, mine, across(mine, 2))
+    chosen, strip = local(kernel, "home", ROOMY, shapes, owner, dealt, mine, across(mine, 4))
     far = exchange(chosen)
     strips = ring(strip, npcol // YS, YS)
     (paired,) = local(pair_kernel, "pair", PARAMS, [own.shape], owner, own, far, after=strips[1:])

time: 79.3 us -> 77.9 us (0.982)
  waiting for transfers between devices: 22.8 us -> 12.3 us
  starting transfers between devices: 40.8 us -> 50.7 us
    ppermute x3, waiting for transfers between devices: 10.6 us -> 5.61 us  [across(): return lax.ppermute(value, 'pcol', [(c, c ^ weight) for c in range(npcol)])]
    all_to_all x2, waiting for transfers between devices: 5.46 us -> 1.38 us  [exchange(): lax.all_to_all(value, 'prow', 0, 0, axis_index_groups=columns, tiled=True)]
    ppermute x2, starting transfers between devices: 13.1 us -> 17.1 us  [swap(): return lax.ppermute(value, 'prow', [(p, p ^ 1) for p in range(nprow)])]
    ppermute x3, starting transfers between devices: 10 us -> 13.9 us  [across(): return lax.ppermute(value, 'pcol', [(c, c ^ weight) for c in range(npcol)])]
    all_to_all x2, starting transfers between devices: 8.37 us -> 10.3 us  [exchange(): lax.all_to_all(value, 'prow', 0, 0, axis_index_groups=columns, tiled=True)]
    ppermute x3, waiting for transfers between devices: 6.36 us -> 4.9 us  [ring(): lax.ppermute(value, 'pcol', pairs(d))]
  transfers between devices with their start and end apart: 10 -> 10, of which waited for: 8 -> 7; matrix products, arithmetic and copies ran while one was open for 0% -> 0% of each run, Pallas kernels for 1% -> 1%
where the time goes in v8:
time: 77.9 us; the launch traced here: 77.4 us
  starting transfers between devices  50.7 us (65%)
  waiting for transfers between devices  12.3 us (16%)
  Pallas kernels  11.2 us (14%)
  local copies, waits for them, and re-layouts  3 us (4%)
    ppermute x2, starting transfers between devices, swap(): return lax.ppermute(value, 'prow', [(p, p ^ 1) for p in range(nprow)])  17.1 us
    ppermute x3, starting transfers between devices, across(): return lax.ppermute(value, 'pcol', [(c, c ^ weight) for c in range(npcol)])  13.9 us
    all_to_all x2, starting transfers between devices, exchange(): lax.all_to_all(value, 'prow', 0, 0, axis_index_groups=columns, tiled=True)  10.3 us
    ppermute x3, starting transfers between devices, ring(): lax.ppermute(value, 'pcol', pairs(d))  9.32 us
    ppermute x3, waiting for transfers between devices, across(): return lax.ppermute(value, 'pcol', [(c, c ^ weight) for c in range(npcol)])  5.61 us
    ppermute x3, waiting for transfers between devices, ring(): lax.ppermute(value, 'pcol', pairs(d))  4.9 us
    pallas_call x1, Pallas kernels, final(): pl.pallas_call(final_kernel, grid=(ncols // step,), out_shape=jax.ShapeDt...  3.77 us
    pallas_call x1, Pallas kernels, pick(): pl.pallas_call(pick_kernel, out_shape=(block, block, table, table, jax.Sh...  3.47 us
  transfers between devices with their start and end apart: 10, of which 7 were waited for; matrix products, arithmetic and copies ran while one was open for 0% of the time, Pallas kernels for 1%

profile of v8, /device:TPU:1, one launch (start us, length us, event | category | flops | bytes accessed | tf_op | source)
XLA Modules:
  0.0 77.4 jit_solution(9664754018272508625)
XLA Ops:
  0.0 3.5 %pick.1 = (f32[128,1024]{1,0:T(8,128)}, f32[128,1024]{1,0:T(8,128)}, s32[2,128]{1,0:T(2,128)}, s32[2,128]{1,0:T(2,128)}, s32[2]{0:T(128)}) custom-call(s32[256]{0:T(256)} %piv.1, f32[512,1024]{1,0:T(8,128)} %win.3), custom_call_target="tpu_custom_call" | custom-call | bytes 2097152 | tf_op jit(solution)/shard_map/pick/pallas_call | solution.py:84
  3.5 9.3 %collective-permute-start = (f32[128,1024]{1,0:T(8,128)}, f32[128,1024]{1,0:T(8,128)S(1)}, u32[]{:S(2)}, u32[]{:S(2)}) collective-permute-start(f32[128,1024]{1,0:T(8,128)} %get-tuple-element.22.give), channel_id=1, source_target_pairs={{0,32},{32,0},{64,96},{96,64},{128,160},{160,128},{192,224},{224,1... | collective-permute-start | bytes 1572872 | tf_op jit(solution)/shard_map/ppermute | solution.py:311
  12.8 0.0 copy-done.12
  12.8 1.9 %collective-permute-start.1 = (f32[16,256]{1,0:T(8,128)S(1)}, f32[16,256]{1,0:T(8,128)S(1)}, u32[]{:S(2)}, u32[]{:S(2)}) collective-permute-start(f32[16,256]{1,0:T(8,128)S(1)} %copy-done.12), channel_id=1, source_target_pairs={{0,1},{1,0},{2,3},{3,2},{4,5},{5,4},{6,7},{7,6},{8,9},{9,8},{10,11... | collective-permute-start | bytes 49160 | tf_op jit(solution)/shard_map/ppermute | solution.py:317
  14.8 0.0 copy-done.18
  14.8 2.5 %collective-permute-done.1.beside = f32[16,256]{1,0:T(8,128)S(1)} collective-permute-done((f32[16,256]{1,0:T(8,128)S(1)}, f32[16,256]{1,0:T(8,128)S(1)}, u32[]{:S(2)}, u32[]{:S(2)}) %collective-permute-start.1) | collective-permute-done | bytes 16416 | tf_op jit(solution)/shard_map/ppermute | solution.py:317
  17.3 0.0 collective-permute-done.got
  17.3 0.1 broadcast_in_dim.2.owner
  17.4 0.0 copy-start.3
  17.4 0.0 copy-start.1
  17.4 1.2 %copy-done.1 = f32[128,1024]{1,0:T(8,128)S(1)} copy-done((f32[128,1024]{1,0:T(8,128)S(1)}, f32[128,1024]{1,0:T(8,128)}, u32[]{:S(2)}) %copy-start.1) | copy-done | bytes 524312
  18.6 0.9 %deal.1 = (f32[128,1024]{1,0:T(8,128)}, f32[32,256]{1,0:T(8,128)S(1)}) custom-call(s32[256,128]{1,0:T(8,128)S(1)} %broadcast_in_dim.2.owner, f32[128,1024]{1,0:T(8,128)S(1)} %copy-done.1, f32[128,1024]{1,0:T(8,128)S(1)} %collective-permute-done.got, f32[16,256]{1,0:T(8,128)S(1)} %copy-done.12, f32[16,256]{1,0:T(8,128)S(1)} %collective-permute-done.1.beside), custom_call_target="tpu_custom_call" | custom-call | bytes 1212416 | tf_op jit(solution)/shard_map/deal/pallas_call | solution.py:161
  19.5 0.0 copy-done.6
  19.5 4.6 %all-to-all-start = ((f32[8,16,1024]{2,1,0:T(8,128)}), f32[8,16,1024]{2,1,0:T(8,128)S(1)}, u32[]{:S(2)}, u32[]{:S(2)}) async-start(f32[8,16,1024]{2,1,0:T(8,128)} %bitcast), calls=%async_computation | async-start | bytes 1048576 | tf_op jit(solution)/shard_map/all_to_all | solution.py:314
  24.1 4.2 %collective-permute-start.2 = (f32[32,256]{1,0:T(8,128)S(1)}, f32[32,256]{1,0:T(8,128)S(1)}, u32[]{:S(2)}, u32[]{:S(2)}) collective-permute-start(f32[32,256]{1,0:T(8,128)S(1)} %get-tuple-element.24.mine), channel_id=1, source_target_pairs={{0,2},{1,3},{2,0},{3,1},{4,6},{5,7},{6,4},{7,5},{8,10},{9,11},{10,... | collective-permute-start | bytes 98312 | tf_op jit(solution)/shard_map/ppermute | solution.py:317
  28.3 1.3 %collective-permute-done.2.theirs = f32[32,256]{1,0:T(8,128)S(1)} collective-permute-done((f32[32,256]{1,0:T(8,128)S(1)}, f32[32,256]{1,0:T(8,128)S(1)}, u32[]{:S(2)}, u32[]{:S(2)}) %collective-permute-start.2) | collective-permute-done | bytes 32800 | tf_op jit(solution)/shard_map/ppermute | solution.py:317
  29.7 0.0 copy-start.10
  29.7 7.8 %collective-permute-start.3 = (f32[64,256]{1,0:T(8,128)S(1)}, f32[64,256]{1,0:T(8,128)S(1)}, u32[]{:S(2)}, u32[]{:S(2)}) collective-permute-start(f32[64,256]{1,0:T(8,128)S(1)} %join.1.mine), channel_id=1, source_target_pairs={{0,4},{1,5},{2,6},{3,7},{4,0},{5,1},{6,2},{7,3},{8,12},{9,13},{10,... | collective-permute-start | bytes 196616 | tf_op jit(solution)/shard_map/ppermute | solution.py:317
  37.5 1.7 %collective-permute-done.3.theirs = f32[64,256]{1,0:T(8,128)S(1)} collective-permute-done((f32[64,256]{1,0:T(8,128)S(1)}, f32[64,256]{1,0:T(8,128)S(1)}, u32[]{:S(2)}, u32[]{:S(2)}) %collective-permute-start.3) | collective-permute-done | bytes 65568 | tf_op jit(solution)/shard_map/ppermute | solution.py:317
  39.2 1.4 %all-to-all-done = f32[8,16,1024]{2,1,0:T(8,128)S(1)} async-done(((f32[8,16,1024]{2,1,0:T(8,128)}), f32[8,16,1024]{2,1,0:T(8,128)S(1)}, u32[]{:S(2)}, u32[]{:S(2)}) %all-to-all-start) | async-done | bytes 524320 | tf_op jit(solution)/shard_map/all_to_all | solution.py:314
  40.6 0.0 copy-done.3
  40.6 0.0 copy-done.10
  40.6 0.0 copy-done.17
  40.6 0.8 copy-done.16
  41.4 1.9 %home.1 = (f32[128,1024]{1,0:T(8,128)}, f32[128,256]{1,0:T(8,128)}) custom-call(s32[256,128]{1,0:T(8,128)} %copy-done.3, f32[128,1024]{1,0:T(8,128)} %bitcast.6, f32[64,256]{1,0:T(8,128)} %copy-done.10, f32[64,256]{1,0:T(8,128)} %copy-done.17), custom_call_target="tpu_custom_call" | custom-call | bytes 786432 | tf_op jit(solution)/shard_map/home/pallas_call | solution.py:161
  43.3 5.7 %all-to-all-start.1 = ((f32[8,16,1024]{2,1,0:T(8,128)}), f32[8,16,1024]{2,1,0:T(8,128)S(1)}, u32[]{:S(2)}, u32[]{:S(2)}) async-start(f32[8,16,1024]{2,1,0:T(8,128)} %bitcast.7), calls=%async_computation.1 | async-start | bytes 1048576 | tf_op jit(solution)/shard_map/all_to_all | solution.py:314
  49.1 4.4 %collective-permute-start.6 = (f32[128,256]{1,0:T(8,128)}, f32[128,256]{1,0:T(8,128)S(1)}, u32[]{:S(2)}, u32[]{:S(2)}) collective-permute-start(f32[128,256]{1,0:T(8,128)} %get-tuple-element.25.refs_0_), channel_id=1, source_target_pairs={{0,24},{1,25},{2,26},{3,27},{4,28},{5,29},{6,30},{7,31},{8,0},{9,1... | collective-permute-start | bytes 393224 | tf_op jit(solution)/shard_map/ppermute | solution.py:322
  53.4 2.4 %collective-permute-start.5 = (f32[128,256]{1,0:T(8,128)}, f32[128,256]{1,0:T(8,128)S(1)}, u32[]{:S(2)}, u32[]{:S(2)}) collective-permute-start(f32[128,256]{1,0:T(8,128)} %get-tuple-element.25.refs_0_), channel_id=1, source_target_pairs={{0,16},{1,17},{2,18},{3,19},{4,20},{5,21},{6,22},{7,23},{8,24},{9,... | collective-permute-start | bytes 393224 | tf_op jit(solution)/shard_map/ppermute | solution.py:322
  55.9 2.5 %collective-permute-start.4 = (f32[128,256]{1,0:T(8,128)}, f32[128,256]{1,0:T(8,128)S(1)}, u32[]{:S(2)}, u32[]{:S(2)}) collective-permute-start(f32[128,256]{1,0:T(8,128)} %get-tuple-element.25.refs_0_), channel_id=1, source_target_pairs={{0,8},{1,9},{2,10},{3,11},{4,12},{5,13},{6,14},{7,15},{8,16},{9,17... | collective-permute-start | bytes 393224 | tf_op jit(solution)/shard_map/ppermute | solution.py:322
  58.4 0.0 collective-permute-done.6.refs_3_.refs_2_
  58.4 2.8 %collective-permute-done.5.refs_2_.refs_1_ = f32[128,256]{1,0:T(8,128)S(1)} collective-permute-done((f32[128,256]{1,0:T(8,128)}, f32[128,256]{1,0:T(8,128)S(1)}, u32[]{:S(2)}, u32[]{:S(2)}) %collective-permute-start.5) | collective-permute-done | bytes 131104 | tf_op jit(solution)/shard_map/ppermute | solution.py:322
  61.2 2.1 %collective-permute-done.4.refs_1_.refs_0_ = f32[128,256]{1,0:T(8,128)S(1)} collective-permute-done((f32[128,256]{1,0:T(8,128)}, f32[128,256]{1,0:T(8,128)S(1)}, u32[]{:S(2)}, u32[]{:S(2)}) %collective-permute-start.4) | collective-permute-done | bytes 131104 | tf_op jit(solution)/shard_map/ppermute | solution.py:322
  63.3 0.0 all-to-all-done.1
  63.3 0.0 copy-done.2
  63.3 0.9 %copy-done.4 = s32[256,128]{1,0:T(8,128)S(1)} copy-done((s32[256,128]{1,0:T(8,128)S(1)}, s32[256,128]{1,0:T(8,128)}, u32[]{:S(2)}) %copy-start.4) | copy-done | bytes 131096
  64.2 0.1 pair.1
  64.3 7.8 %collective-permute-start.7 = (f32[128,1024]{1,0:T(8,128)S(1)}, f32[128,1024]{1,0:T(8,128)S(1)}, u32[]{:S(2)}, u32[]{:S(2)}) collective-permute-start(f32[128,1024]{1,0:T(8,128)S(1)} %pair.1), channel_id=1, source_target_pairs={{0,32},{32,0},{64,96},{96,64},{128,160},{160,128},{192,224},{224,1... | collective-permute-start | bytes 1572872 | tf_op jit(solution)/shard_map/ppermute | solution.py:311
  72.1 0.0 copy-done.9
  72.1 0.0 copy-done.11
  72.1 0.1 split.1
  72.3 0.0 copy-start.8
  72.3 0.0 copy-done.13
  72.3 0.0 copy-done.14
  72.3 0.0 copy-done.15
  72.3 0.0 copy-done
  72.3 0.9 %ready.1 = (f32[128,1024]{1,0:T(8,128)S(1)}, f32[512,1024]{1,0:T(8,128)S(1)}) custom-call(s32[2,128]{1,0:T(2,128)S(1)} %copy-done.13, s32[2,128]{1,0:T(2,128)S(1)} %copy-done.14, s32[2]{0:T(128)S(1)} %copy-done.15, s32[256,128]{1,0:T(8,128)S(1)} %copy-done.5, f32[128,1024]{1,0:T(8,128)S(1)} %copy-done.2, f32[128,1024]{1,0:T(8,128)S(1)} %copy-done.7, ...), custom_call_target="tpu_custom_call" | custom-call | bytes 6291456 | tf_op jit(solution)/shard_map/ready/pallas_call | solution.py:238
  73.2 0.4 collective-permute-done.7.got
  73.6 3.8 %final.1 = f32[512,1024]{1,0:T(8,128)} custom-call(s32[2,128]{1,0:T(2,128)S(1)} %copy-done.13, s32[2,128]{1,0:T(2,128)S(1)} %copy-done.14, s32[2]{0:T(128)S(1)} %copy-done.15, s32[256,128]{1,0:T(8,128)S(1)} %copy-done.5, bf16[256,768]{1,0:T(8,128)(2,1)S(1)} %get-tuple-element.26.left, bf16[512,768]{1,0:T(8,128)(2,1)S(1)} %get-tuple-element.27.right, ...), custom_call_target="tpu_custom_call" | custom-call | flops 1207959552 | bytes 4194304 | tf_op jit(solution)/shard_map/final/pallas_call | solution.py:291
  (20 shorter events, 0.0 us)
Async XLA Ops:
  0.0 14.8 %copy-start.18 = (s32[256]{0:T(256)S(1)}, s32[256]{0:T(256)}, u32[]{:S(2)}) copy-start(s32[256]{0:T(256)} %piv.1) | copy-start | bytes 3076
  0.0 12.8 %copy-start.12 = (f32[16,256]{1,0:T(8,128)S(1)}, f32[16,256]{1,0:T(8,128)}, u32[]{:S(2)}) copy-start(f32[16,256]{1,0:T(8,128)} %panel.1) | copy-start | bytes 49156
  3.5 13.8 %collective-permute-start = (f32[128,1024]{1,0:T(8,128)}, f32[128,1024]{1,0:T(8,128)S(1)}, u32[]{:S(2)}, u32[]{:S(2)}) collective-permute-start(f32[128,1024]{1,0:T(8,128)} %get-tuple-element.22.give), channel_id=1, source_target_pairs={{0,32},{32,0},{64,96},{96,64},{128,160},{160,128},{192,224},{224,1... | collective-permute-start | bytes 1572872 | tf_op jit(solution)/shard_map/ppermute | solution.py:311
  12.8 4.5 %collective-permute-start.1 = (f32[16,256]{1,0:T(8,128)S(1)}, f32[16,256]{1,0:T(8,128)S(1)}, u32[]{:S(2)}, u32[]{:S(2)}) collective-permute-start(f32[16,256]{1,0:T(8,128)S(1)} %copy-done.12), channel_id=1, source_target_pairs={{0,1},{1,0},{2,3},{3,2},{4,5},{5,4},{6,7},{7,6},{8,9},{9,8},{10,11... | collective-permute-start | bytes 49160 | tf_op jit(solution)/shard_map/ppermute | solution.py:317
  17.3 2.2 %copy-start.6 = (f32[128,1024]{1,0:T(8,128)}, f32[128,1024]{1,0:T(8,128)S(1)}, u32[]{:S(2)}) copy-start(f32[128,1024]{1,0:T(8,128)S(1)} %collective-permute-done.got) | copy-start | bytes 1572868
  17.4 23.2 %copy-start.3 = (s32[256,128]{1,0:T(8,128)}, s32[256,128]{1,0:T(8,128)S(1)}, u32[]{:S(2)}) copy-start(s32[256,128]{1,0:T(8,128)S(1)} %broadcast_in_dim.2.owner) | copy-start | bytes 393220
  17.4 1.2 %copy-start.1 = (f32[128,1024]{1,0:T(8,128)S(1)}, f32[128,1024]{1,0:T(8,128)}, u32[]{:S(2)}) copy-start(f32[128,1024]{1,0:T(8,128)} %get-tuple-element.21.own) | copy-start | bytes 1572868
  18.6 44.7 %copy-start.2 = (f32[128,1024]{1,0:T(8,128)S(1)}, f32[128,1024]{1,0:T(8,128)}, u32[]{:S(2)}) copy-start(f32[128,1024]{1,0:T(8,128)} %get-tuple-element.21.own) | copy-start | bytes 1572868
  19.5 21.1 %all-to-all-start = ((f32[8,16,1024]{2,1,0:T(8,128)}), f32[8,16,1024]{2,1,0:T(8,128)S(1)}, u32[]{:S(2)}, u32[]{:S(2)}) async-start(f32[8,16,1024]{2,1,0:T(8,128)} %bitcast), calls=%async_computation | async-start | bytes 1048576 | tf_op jit(solution)/shard_map/all_to_all | solution.py:314
  24.1 5.5 %collective-permute-start.2 = (f32[32,256]{1,0:T(8,128)S(1)}, f32[32,256]{1,0:T(8,128)S(1)}, u32[]{:S(2)}, u32[]{:S(2)}) collective-permute-start(f32[32,256]{1,0:T(8,128)S(1)} %get-tuple-element.24.mine), channel_id=1, source_target_pairs={{0,2},{1,3},{2,0},{3,1},{4,6},{5,7},{6,4},{7,5},{8,10},{9,11},{10,... | collective-permute-start | bytes 98312 | tf_op jit(solution)/shard_map/ppermute | solution.py:317
  29.7 11.0 %copy-start.10 = (f32[64,256]{1,0:T(8,128)}, f32[64,256]{1,0:T(8,128)S(1)}, u32[]{:S(2)}) copy-start(f32[64,256]{1,0:T(8,128)S(1)} %join.1.mine) | copy-start | bytes 196612
  29.7 9.6 %collective-permute-start.3 = (f32[64,256]{1,0:T(8,128)S(1)}, f32[64,256]{1,0:T(8,128)S(1)}, u32[]{:S(2)}, u32[]{:S(2)}) collective-permute-start(f32[64,256]{1,0:T(8,128)S(1)} %join.1.mine), channel_id=1, source_target_pairs={{0,4},{1,5},{2,6},{3,7},{4,0},{5,1},{6,2},{7,3},{8,12},{9,13},{10,... | collective-permute-start | bytes 196616 | tf_op jit(solution)/shard_map/ppermute | solution.py:317
  39.2 1.4 %copy-start.17 = (f32[64,256]{1,0:T(8,128)}, f32[64,256]{1,0:T(8,128)S(1)}, u32[]{:S(2)}) copy-start(f32[64,256]{1,0:T(8,128)S(1)} %collective-permute-done.3.theirs) | copy-start | bytes 196612
  40.6 0.8 %copy-start.16 = (f32[8,16,1024]{2,1,0:T(8,128)}, f32[8,16,1024]{2,1,0:T(8,128)S(1)}, u32[]{:S(2)}) copy-start(f32[8,16,1024]{2,1,0:T(8,128)S(1)} %all-to-all-done) | copy-start | bytes 1572868
  41.4 30.9 %copy-start.13 = (s32[2,128]{1,0:T(2,128)S(1)}, s32[2,128]{1,0:T(2,128)}, u32[]{:S(2)}) copy-start(s32[2,128]{1,0:T(2,128)} %get-tuple-element.18.slots) | copy-start | bytes 3076
  41.4 30.9 %copy-start.14 = (s32[2,128]{1,0:T(2,128)S(1)}, s32[2,128]{1,0:T(2,128)}, u32[]{:S(2)}) copy-start(s32[2,128]{1,0:T(2,128)} %get-tuple-element.19.rows) | copy-start | bytes 3076
  41.4 30.9 %copy-start.15 = (s32[2]{0:T(128)S(1)}, s32[2]{0:T(128)}, u32[]{:S(2)}) copy-start(s32[2]{0:T(128)} %get-tuple-element.20.counts) | copy-start | bytes 28
  43.3 29.0 %copy-start = (f32[512,1024]{1,0:T(8,128)S(1)}, f32[512,1024]{1,0:T(8,128)}, u32[]{:S(2)}) copy-start(f32[512,1024]{1,0:T(8,128)} %win.3) | copy-start | bytes 6291460
  43.3 20.0 %all-to-all-start.1 = ((f32[8,16,1024]{2,1,0:T(8,128)}), f32[8,16,1024]{2,1,0:T(8,128)S(1)}, u32[]{:S(2)}, u32[]{:S(2)}) async-start(f32[8,16,1024]{2,1,0:T(8,128)} %bitcast.7), calls=%async_computation.1 | async-start | bytes 1048576 | tf_op jit(solution)/shard_map/all_to_all | solution.py:314
  49.1 9.3 %collective-permute-start.6 = (f32[128,256]{1,0:T(8,128)}, f32[128,256]{1,0:T(8,128)S(1)}, u32[]{:S(2)}, u32[]{:S(2)}) collective-permute-start(f32[128,256]{1,0:T(8,128)} %get-tuple-element.25.refs_0_), channel_id=1, source_target_pairs={{0,24},{1,25},{2,26},{3,27},{4,28},{5,29},{6,30},{7,31},{8,0},{9,1... | collective-permute-start | bytes 393224 | tf_op jit(solution)/shard_map/ppermute | solution.py:322
  53.4 7.7 %collective-permute-start.5 = (f32[128,256]{1,0:T(8,128)}, f32[128,256]{1,0:T(8,128)S(1)}, u32[]{:S(2)}, u32[]{:S(2)}) collective-permute-start(f32[128,256]{1,0:T(8,128)} %get-tuple-element.25.refs_0_), channel_id=1, source_target_pairs={{0,16},{1,17},{2,18},{3,19},{4,20},{5,21},{6,22},{7,23},{8,24},{9,... | collective-permute-start | bytes 393224 | tf_op jit(solution)/shard_map/ppermute | solution.py:322
  55.9 7.4 %collective-permute-start.4 = (f32[128,256]{1,0:T(8,128)}, f32[128,256]{1,0:T(8,128)S(1)}, u32[]{:S(2)}, u32[]{:S(2)}) collective-permute-start(f32[128,256]{1,0:T(8,128)} %get-tuple-element.25.refs_0_), channel_id=1, source_target_pairs={{0,8},{1,9},{2,10},{3,11},{4,12},{5,13},{6,14},{7,15},{8,16},{9,17... | collective-permute-start | bytes 393224 | tf_op jit(solution)/shard_map/ppermute | solution.py:322
  63.3 0.9 %copy-start.4 = (s32[256,128]{1,0:T(8,128)S(1)}, s32[256,128]{1,0:T(8,128)}, u32[]{:S(2)}) copy-start(s32[256,128]{1,0:T(8,128)} %copy-done.3) | copy-start | bytes 393220
  64.2 7.9 %copy-start.9 = (f32[256,256]{1,0:T(8,128)S(1)}, f32[256,256]{1,0:T(8,128)}, u32[]{:S(2)}) copy-start(f32[256,256]{1,0:T(8,128)} %linv.1) | copy-start | bytes 786436
  64.2 7.9 %copy-start.11 = (f32[128,256]{1,0:T(8,128)S(1)}, f32[128,256]{1,0:T(8,128)}, u32[]{:S(2)}) copy-start(f32[128,256]{1,0:T(8,128)} %get-tuple-element.25.refs_0_) | copy-start | bytes 393220
  64.2 8.1 %copy-start.5 = (s32[256,128]{1,0:T(8,128)S(1)}, s32[256,128]{1,0:T(8,128)}, u32[]{:S(2)}) copy-start(s32[256,128]{1,0:T(8,128)} %copy-done.3) | copy-start | bytes 393220
  64.2 8.1 %copy-start.7 = (f32[128,1024]{1,0:T(8,128)S(1)}, f32[128,1024]{1,0:T(8,128)}, u32[]{:S(2)}) copy-start(f32[128,1024]{1,0:T(8,128)} %copy-done.6) | copy-start | bytes 1572868
  64.3 9.3 %collective-permute-start.7 = (f32[128,1024]{1,0:T(8,128)S(1)}, f32[128,1024]{1,0:T(8,128)S(1)}, u32[]{:S(2)}, u32[]{:S(2)}) collective-permute-start(f32[128,1024]{1,0:T(8,128)S(1)} %pair.1), channel_id=1, source_target_pairs={{0,32},{32,0},{64,96},{96,64},{128,160},{160,128},{192,224},{224,1... | collective-permute-start | bytes 1572872 | tf_op jit(solution)/shard_map/ppermute | solution.py:311
  72.3 1.4 %copy-start.8 = (f32[128,1024]{1,0:T(8,128)S(1)}, f32[128,1024]{1,0:T(8,128)}, u32[]{:S(2)}) copy-start(f32[128,1024]{1,0:T(8,128)} %get-tuple-element.22.give) | copy-start | bytes 1572868
